TPU v7x, 32 devices: a whole 2x2x4 slice. The times are simulated.
32 devices in a mesh: rep: 2 (over x), fsdp: 16 (over z, y, core).
Axes of the slice: x: 2, y: 2, z: 4, core: 2. Of those that a mesh axis runs over, the one named last changes fastest.
Arguments:
- pixels: bfloat16 [2, 96, 196, 768], P(None, ('rep', 'fsdp')), may hold values from -9 to 9
- merge_map: int32 [2, 96, 196], P(None, ('rep', 'fsdp')), may hold values from 0 to 195, as said below
- merge_weight: float32 [2, 96, 196], P(None, ('rep', 'fsdp')), may hold values from 0.5 to 2
- counts: int32 [2, 96], P(None, ('rep', 'fsdp')), may hold values from 60 to 196, as said below
- captions: bfloat16 [2, 96, 768], replicated, may hold values from -12 to 12
- pairing: int32 [2, 96], replicated, may hold values from 0 to 95, each once within a row
- embedder: float32 [768, 768], P('fsdp'), may hold values from -0.21875 to 0.21875
- positions: float32 [196, 768], P(None, 'fsdp'), may hold values from -3 to 3
- widener: float32 [768, 5376], P('fsdp'), may hold values from -0.21650635 to 0.21650635
- narrower: float32 [3840, 768], P('fsdp'), may hold values from -0.21875 to 0.21875
- projector: float32 [768, 768], P('fsdp'), may hold values from -0.21875 to 0.21875
- scales: float32 [4, 768], P(None, 'fsdp'), may hold values from 0.33 to 2.34
- biases: float32 [4608], P('fsdp'), may hold values from -1.8 to 1.8
- moment_embedder: float32 [768, 768], P('fsdp'), may hold values from -2.4e-05 to 2.4e-05
- moment_positions: float32 [196, 768], P(None, 'fsdp'), may hold values from -2.4e-05 to 2.4e-05
- moment_widener: float32 [768, 5376], P('fsdp'), may hold values from -2.4e-05 to 2.4e-05
- moment_narrower: float32 [3840, 768], P('fsdp'), may hold values from -2.4e-05 to 2.4e-05
- moment_projector: float32 [768, 768], P('fsdp'), may hold values from -2.4e-05 to 2.4e-05
- moment_scales: float32 [4, 768], P(None, 'fsdp'), may hold values from -2.4e-05 to 2.4e-05
- moment_biases: float32 [4608], P('fsdp'), may hold values from -2.4e-05 to 2.4e-05
- square_embedder: float32 [768, 768], P('fsdp'), may hold values from 3e-13 to 3e-12
- square_positions: float32 [196, 768], P(None, 'fsdp'), may hold values from 3e-13 to 3e-12
- square_widener: float32 [768, 5376], P('fsdp'), may hold values from 3e-13 to 3e-12
- square_narrower: float32 [3840, 768], P('fsdp'), may hold values from 3e-13 to 3e-12
- square_projector: float32 [768, 768], P('fsdp'), may hold values from 3e-13 to 3e-12
- square_scales: float32 [4, 768], P(None, 'fsdp'), may hold values from 3e-13 to 3e-12
- square_biases: float32 [4608], P('fsdp'), may hold values from 3e-13 to 3e-12
Outputs:
- objective: float32 [], replicated
- weight_total: float32 [], replicated
- total_norm: float32 [], replicated
- change_embedder: float32 [768, 768], P('fsdp')
- change_positions: float32 [196, 768], P(None, 'fsdp')
- change_widener: float32 [768, 5376], P('fsdp')
- change_narrower: float32 [3840, 768], P('fsdp')
- change_projector: float32 [768, 768], P('fsdp')
- change_scales: float32 [4, 768], P(None, 'fsdp')
- change_biases: float32 [4608], P('fsdp')
- clipped_embedder: float32 [768, 768], P('fsdp')
- clipped_positions: float32 [196, 768], P(None, 'fsdp')
- clipped_widener: float32 [768, 5376], P('fsdp')
- clipped_narrower: float32 [3840, 768], P('fsdp')
- clipped_projector: float32 [768, 768], P('fsdp')
- clipped_scales: float32 [4, 768], P(None, 'fsdp')
- clipped_biases: float32 [4608], P('fsdp')
Inputs may be any that keep to these rules, and one draw needn't show every extreme that they name: `counts`: in every micro-batch one image keeps 196 tokens and one keeps 60. `merge_map`: each patch names a slot below its image's count; every such slot is named by one patch or more. `pairing`: each micro-batch's row names every text once.
All inputs are finite; a program needn't handle non-finite values.
Results may differ from a plain program's by a relative error of at most 0.02.
The roundings to bfloat16 on the way count: a program that leaves them out, or rounds other values in their place, can miss the bound.
Values may be sent and summed in bfloat16 or wider, within the bound.
No kernel may reach another device: no remote copies, remote signals or barrier semaphores. Data moves between devices by JAX's collectives and lax.ppermute only.
A program may use at most 256 MiB of HBM per device.

v0:
```python
import jax
import jax.numpy as jnp
from jax import lax
from jax.sharding import PartitionSpec as P

HEADS = 12


highest = lax.Precision.HIGHEST
norm_eps = 1e-06
clip_bound = 0.1
beta_first = 0.9
beta_second = 0.999
learn_rate = 0.03
weight_decay = 0.1
adam_eps = 1e-08
step_number = 10
logit_temper = 10.0


def product(left, right):
    return jnp.dot(left, right, preferred_element_type=jnp.float32)


def product_across(left, right):
    return lax.dot_general(
        left, right, (((0,), (0,)), ((), ())), preferred_element_type=jnp.float32
    )


def product_along(left, right):
    return lax.dot_general(
        left, right, (((1,), (1,)), ((), ())), preferred_element_type=jnp.float32
    )


def layer_norm(values, gain_row):
    center = values - jnp.mean(values, axis=-1, keepdims=True)
    spread = jnp.mean(center * center, axis=-1, keepdims=True)
    return center * lax.rsqrt(spread + norm_eps) * gain_row


def head_norm(values, gain_row):
    return layer_norm(values, gain_row.reshape(values.shape[-2], values.shape[-1]))


def gelu_exact(values):
    return 0.5 * values * (1.0 + lax.erf(values * 0.7071067811865476))


def merge_matrix(slot_map, slot_weight, live_count):
    slot_total = slot_map.shape[-1]
    slot_ids = jnp.arange(slot_total, dtype=jnp.int32)
    member = (slot_map[:, None, :] == slot_ids[None, :, None]).astype(jnp.float32) * slot_weight[
        :, None, :
    ]
    vacant = (slot_ids[None, :] >= live_count[:, None]).astype(jnp.float32)
    return member / (jnp.sum(member, axis=-1) + vacant)[:, :, None]


def pool_final(stream, gain_row, live_mask, count_float):
    final_rows = layer_norm(stream, gain_row)
    return jnp.sum(final_rows * live_mask[:, :, None], axis=1) / count_float[:, None]


def adam_step(weight, gradient, moment, square, factor):
    clipped = gradient * factor
    moment_new = beta_first * moment + (1.0 - beta_first) * clipped
    square_new = beta_second * square + (1.0 - beta_second) * clipped * clipped
    mean_hat = moment_new / (1.0 - beta_first**step_number)
    square_hat = square_new / (1.0 - beta_second**step_number)
    change = -learn_rate * (mean_hat / (jnp.sqrt(square_hat) + adam_eps) + weight_decay * weight)
    return (change, clipped)


def per_device(
    pixels,
    merge_map,
    merge_weight,
    counts,
    captions,
    pairing,
    embedder,
    positions,
    widener,
    narrower,
    projector,
    scales,
    biases,
    moment_embedder,
    moment_positions,
    moment_widener,
    moment_narrower,
    moment_projector,
    moment_scales,
    moment_biases,
    square_embedder,
    square_positions,
    square_widener,
    square_narrower,
    square_projector,
    square_scales,
    square_biases,
):
    gathered_weights = (
        lax.all_gather(embedder.astype(jnp.bfloat16), "fsdp", axis=0, tiled=True),
        lax.all_gather(positions.astype(jnp.bfloat16), "fsdp", axis=1, tiled=True),
        lax.all_gather(widener.astype(jnp.bfloat16), "fsdp", axis=0, tiled=True),
        lax.all_gather(narrower.astype(jnp.bfloat16), "fsdp", axis=0, tiled=True),
        lax.all_gather(projector.astype(jnp.bfloat16), "fsdp", axis=0, tiled=True),
        lax.all_gather(scales.astype(jnp.bfloat16), "fsdp", axis=1, tiled=True),
        lax.all_gather(biases.astype(jnp.bfloat16), "fsdp", axis=0, tiled=True),
    )
    embed_full, place_full, wide_full, narrow_full, project_full, scale_full, bias_full = (
        gathered_weights
    )
    place_float = place_full.astype(jnp.float32)
    scale_float = scale_full.astype(jnp.float32)
    bias_float = bias_full.astype(jnp.float32)
    micro_count, images_dev, slot_total, patch_size = pixels.shape
    model_width = embed_full.shape[1]
    hidden_width = narrow_full.shape[0] - model_width
    head_count = HEADS
    head_size = model_width // head_count
    images_all = pairing.shape[1]
    embed_width = captions.shape[2]
    logit_factor = logit_temper * embed_width ** (-0.5)
    attend_factor = head_size ** (-0.5)
    fsdp_count = lax.axis_size("fsdp")
    first_row = (lax.axis_index("rep") * fsdp_count + lax.axis_index("fsdp")) * images_dev
    row_count = images_dev * slot_total
    grad_embed = jnp.zeros(embed_full.shape, jnp.float32)
    grad_place = jnp.zeros(place_full.shape, jnp.float32)
    grad_wide = jnp.zeros(wide_full.shape, jnp.float32)
    grad_narrow = jnp.zeros(narrow_full.shape, jnp.float32)
    grad_project = jnp.zeros(project_full.shape, jnp.float32)
    grad_scale = jnp.zeros(scale_full.shape, jnp.float32)
    grad_bias = jnp.zeros(bias_full.shape, jnp.float32)
    objective = jnp.zeros((), jnp.float32)
    weight_total_all = jnp.zeros((), jnp.float32)
    image_ids = jnp.arange(images_all, dtype=jnp.int32)
    for step_index in range(micro_count):
        pixel_rows = pixels[step_index].reshape(row_count, patch_size)
        live_count = counts[step_index]
        count_float = live_count.astype(jnp.float32)
        live_mask = (jnp.arange(slot_total, dtype=jnp.int32)[None, :] < live_count[:, None]).astype(
            jnp.float32
        )
        key_live = live_mask[:, None, None, :] > 0
        merger = merge_matrix(merge_map[step_index], merge_weight[step_index], live_count)
        patches = product(pixel_rows, embed_full).reshape(images_dev, slot_total, model_width)
        patches = patches + bias_float[hidden_width + model_width :] + place_float
        merged = jnp.einsum("isp,ipd->isd", merger, patches, precision=highest)
        normed, normed_back = jax.vjp(layer_norm, merged, scale_float[0])
        normed_low = normed.astype(jnp.bfloat16).reshape(row_count, model_width)
        widened = product(normed_low, wide_full)
        query_pre = widened[:, :model_width].reshape(images_dev, slot_total, head_count, head_size)
        key_pre = widened[:, model_width : 2 * model_width].reshape(
            images_dev, slot_total, head_count, head_size
        )
        queries, query_back = jax.vjp(head_norm, query_pre, scale_float[2])
        key_rows, key_back = jax.vjp(head_norm, key_pre, scale_float[3])
        query_low = queries.astype(jnp.bfloat16)
        key_low = key_rows.astype(jnp.bfloat16)
        value_low = (
            widened[:, 2 * model_width : 3 * model_width]
            .reshape(images_dev, slot_total, head_count, head_size)
            .astype(jnp.bfloat16)
        )
        scores = (
            jnp.einsum("ishd,ithd->ihst", query_low, key_low, preferred_element_type=jnp.float32)
            * attend_factor
        )
        scores = jnp.where(key_live, scores, -1e30)
        score_top = jnp.max(scores, axis=-1, keepdims=True)
        log_total = score_top + jnp.log(
            jnp.sum(jnp.exp(scores - score_top), axis=-1, keepdims=True)
        )
        softmax = jnp.exp(scores - log_total)
        attended = jnp.einsum(
            "ihst,ithd->ishd",
            softmax.astype(jnp.bfloat16),
            value_low,
            preferred_element_type=jnp.float32,
        )
        attended = attended.reshape(row_count, model_width).astype(jnp.bfloat16)
        hidden, gelu_back = jax.vjp(
            gelu_exact, widened[:, 3 * model_width :] + bias_float[:hidden_width]
        )
        joined = jnp.concatenate([attended, hidden.astype(jnp.bfloat16)], axis=1)
        stream = (
            merged
            + product(joined, narrow_full).reshape(images_dev, slot_total, model_width)
            + bias_float[hidden_width : hidden_width + model_width]
        )
        pooled, pool_back = jax.vjp(
            lambda values, gain_row: pool_final(values, gain_row, live_mask, count_float),
            stream,
            scale_float[1],
        )
        pooled_low = pooled.astype(jnp.bfloat16)
        embeds = product(pooled_low, project_full).astype(jnp.bfloat16)
        everyone, count_all = (
            lax.all_gather(embeds, ("rep", "fsdp"), axis=0, tiled=True),
            lax.all_gather(count_float.astype(jnp.bfloat16), ("rep", "fsdp"), axis=0, tiled=True),
        )
        caption_rows = captions[step_index]
        logits = product_along(everyone, caption_rows) * logit_factor
        row_top = jnp.max(logits, axis=1, keepdims=True)
        row_logsum = row_top[:, 0] + jnp.log(jnp.sum(jnp.exp(logits - row_top), axis=1))
        column_top = jnp.max(logits, axis=0, keepdims=True)
        column_logsum = column_top[0] + jnp.log(jnp.sum(jnp.exp(logits - column_top), axis=0))
        target = (pairing[step_index][:, None] == image_ids[None, :]).astype(jnp.float32)
        picked = jnp.sum(logits * target, axis=1)
        column_pick = jnp.sum(target * column_logsum[None, :], axis=1)
        weight_all = count_all.astype(jnp.float32)
        weight_total = jnp.sum(weight_all)
        weight_total_all = weight_total_all + weight_total
        part_loss = 0.5 * (
            -jnp.sum(weight_all * (picked - row_logsum)) / weight_total
            - jnp.mean(picked - column_pick)
        )
        objective = objective + part_loss / micro_count
        own_logits = lax.dynamic_slice_in_dim(logits, first_row, images_dev, 0)
        own_target = lax.dynamic_slice_in_dim(target, first_row, images_dev, 0)
        own_logsum = lax.dynamic_slice_in_dim(row_logsum, first_row, images_dev, 0)
        row_soft = jnp.exp(own_logits - own_logsum[:, None])
        column_soft = jnp.exp(own_logits - column_logsum[None, :])
        grad_logits = (
            0.5
            / micro_count
            * (
                (count_float / weight_total)[:, None] * (row_soft - own_target)
                + (column_soft - own_target) / images_all
            )
        )
        grad_product = (grad_logits * logit_factor).astype(jnp.bfloat16)
        grad_embeds = product(grad_product, caption_rows).astype(jnp.bfloat16)
        grad_project = grad_project + product_across(pooled_low, grad_embeds)
        grad_pooled = product_along(grad_embeds, project_full)
        grad_stream, grad_final_scale = pool_back(grad_pooled)
        grad_branch = grad_stream.reshape(row_count, model_width).astype(jnp.bfloat16)
        grad_narrow = grad_narrow + product_across(joined, grad_branch)
        grad_joined = product_along(grad_branch, narrow_full)
        grad_attended = (
            grad_joined[:, :model_width]
            .astype(jnp.bfloat16)
            .reshape(images_dev, slot_total, head_count, head_size)
        )
        (grad_act,) = gelu_back(grad_joined[:, model_width:])
        again = (
            jnp.einsum("ishd,ithd->ihst", query_low, key_low, preferred_element_type=jnp.float32)
            * attend_factor
        )
        again = jnp.where(key_live, again, -1e30)
        softmax_again = jnp.exp(again - log_total)
        grad_probs = jnp.einsum(
            "ishd,ithd->ihst", grad_attended, value_low, preferred_element_type=jnp.float32
        )
        row_dot = jnp.sum(softmax_again * grad_probs, axis=-1, keepdims=True)
        grad_scores = (softmax_again * (grad_probs - row_dot) * attend_factor).astype(jnp.bfloat16)
        grad_values = jnp.einsum(
            "ihst,ishd->ithd",
            softmax_again.astype(jnp.bfloat16),
            grad_attended,
            preferred_element_type=jnp.float32,
        )
        grad_queries = jnp.einsum(
            "ihst,ithd->ishd", grad_scores, key_low, preferred_element_type=jnp.float32
        )
        grad_keys = jnp.einsum(
            "ihst,ishd->ithd", grad_scores, query_low, preferred_element_type=jnp.float32
        )
        grad_query_pre, grad_query_scale = query_back(grad_queries)
        grad_key_pre, grad_key_scale = key_back(grad_keys)
        grad_widened = jnp.concatenate(
            [
                grad_query_pre.reshape(row_count, model_width),
                grad_key_pre.reshape(row_count, model_width),
                grad_values.reshape(row_count, model_width),
                grad_act,
            ],
            axis=1,
        ).astype(jnp.bfloat16)
        grad_wide = grad_wide + product_across(normed_low, grad_widened)
        grad_normed = product_along(grad_widened, wide_full).reshape(
            images_dev, slot_total, model_width
        )
        grad_merged_norm, grad_first_scale = normed_back(grad_normed)
        grad_merged = grad_stream + grad_merged_norm
        grad_patches = jnp.einsum("isp,isd->ipd", merger, grad_merged, precision=highest)
        grad_place = grad_place + jnp.sum(grad_patches, axis=0)
        grad_embed = grad_embed + product_across(
            pixel_rows, grad_patches.reshape(row_count, model_width).astype(jnp.bfloat16)
        )
        grad_scale = grad_scale + jnp.stack(
            [grad_first_scale, grad_final_scale, grad_query_scale, grad_key_scale]
        )
        grad_bias = grad_bias + jnp.concatenate(
            [
                jnp.sum(grad_act, axis=0),
                jnp.sum(grad_stream, axis=(0, 1)),
                jnp.sum(grad_patches, axis=(0, 1)),
            ]
        )
    pieces = (
        lax.psum_scatter(
            grad_embed.astype(jnp.bfloat16), "fsdp", scatter_dimension=0, tiled=True
        ).astype(jnp.float32),
        lax.psum_scatter(
            grad_place.astype(jnp.bfloat16), "fsdp", scatter_dimension=1, tiled=True
        ).astype(jnp.float32),
        lax.psum_scatter(
            grad_wide.astype(jnp.bfloat16), "fsdp", scatter_dimension=0, tiled=True
        ).astype(jnp.float32),
        lax.psum_scatter(
            grad_narrow.astype(jnp.bfloat16), "fsdp", scatter_dimension=0, tiled=True
        ).astype(jnp.float32),
        lax.psum_scatter(
            grad_project.astype(jnp.bfloat16), "fsdp", scatter_dimension=0, tiled=True
        ).astype(jnp.float32),
        lax.psum_scatter(
            grad_scale.astype(jnp.bfloat16), "fsdp", scatter_dimension=1, tiled=True
        ).astype(jnp.float32),
        lax.psum_scatter(
            grad_bias.astype(jnp.bfloat16), "fsdp", scatter_dimension=0, tiled=True
        ).astype(jnp.float32),
    )
    shards = (
        lax.psum(pieces[0].astype(jnp.bfloat16), "rep").astype(jnp.float32),
        lax.psum(pieces[1].astype(jnp.bfloat16), "rep").astype(jnp.float32),
        lax.psum(pieces[2].astype(jnp.bfloat16), "rep").astype(jnp.float32),
        lax.psum(pieces[3].astype(jnp.bfloat16), "rep").astype(jnp.float32),
        lax.psum(pieces[4].astype(jnp.bfloat16), "rep").astype(jnp.float32),
        lax.psum(pieces[5].astype(jnp.bfloat16), "rep").astype(jnp.float32),
        lax.psum(pieces[6].astype(jnp.bfloat16), "rep").astype(jnp.float32),
    )
    local_square = jnp.zeros((), jnp.float32)
    for shard in shards:
        local_square = local_square + jnp.sum(shard * shard)
    total_norm = jnp.sqrt(lax.psum(local_square, "fsdp"))
    factor = clip_bound / jnp.maximum(total_norm, clip_bound)
    weights = (embedder, positions, widener, narrower, projector, scales, biases)
    moments = (
        moment_embedder,
        moment_positions,
        moment_widener,
        moment_narrower,
        moment_projector,
        moment_scales,
        moment_biases,
    )
    squares = (
        square_embedder,
        square_positions,
        square_widener,
        square_narrower,
        square_projector,
        square_scales,
        square_biases,
    )
    results = [
        adam_step(weights[index], shards[index], moments[index], squares[index], factor)
        for index in range(7)
    ]
    return (
        objective,
        weight_total_all,
        total_norm,
        results[0][0],
        results[1][0],
        results[2][0],
        results[3][0],
        results[4][0],
        results[5][0],
        results[6][0],
        results[0][1],
        results[1][1],
        results[2][1],
        results[3][1],
        results[4][1],
        results[5][1],
        results[6][1],
    )


def solution(mesh):
    return jax.shard_map(
        per_device,
        mesh=mesh,
        in_specs=(
            P(None, ("rep", "fsdp"), None, None),
            P(None, ("rep", "fsdp"), None),
            P(None, ("rep", "fsdp"), None),
            P(None, ("rep", "fsdp")),
            P(),
            P(),
            P("fsdp", None),
            P(None, "fsdp"),
            P("fsdp", None),
            P("fsdp", None),
            P("fsdp", None),
            P(None, "fsdp"),
            P("fsdp"),
            P("fsdp", None),
            P(None, "fsdp"),
            P("fsdp", None),
            P("fsdp", None),
            P("fsdp", None),
            P(None, "fsdp"),
            P("fsdp"),
            P("fsdp", None),
            P(None, "fsdp"),
            P("fsdp", None),
            P("fsdp", None),
            P("fsdp", None),
            P(None, "fsdp"),
            P("fsdp"),
        ),
        out_specs=(
            P(),
            P(),
            P(),
            P("fsdp", None),
            P(None, "fsdp"),
            P("fsdp", None),
            P("fsdp", None),
            P("fsdp", None),
            P(None, "fsdp"),
            P("fsdp"),
            P("fsdp", None),
            P(None, "fsdp"),
            P("fsdp", None),
            P("fsdp", None),
            P("fsdp", None),
            P(None, "fsdp"),
            P("fsdp"),
        ),
        check_vma=False,
    )
```

profile of v0, /device:TPU:0, one launch (start us, length us, event | category | flops | bytes accessed | tf_op | source)
XLA Modules:
  0.0 1149.0 jit_solution(17841642280529042038)
XLA Ops:
  14.3 63.6 %all-reduce.1 = bf16[4608]{0:T(1024)(128)(2,1)S(1)} all-reduce(bf16[4608]{0:T(1024)(128)(2,1)S(1)} %dynamic-update-slice.1), channel_id=1, replica_groups=mesh['rep'=2,'fsdp'=16] {'fsdp'}, use_global_device_ids=true, to_apply=%add.1 | all-reduce | flops 4608 | bytes 18432
  80.6 17.3 %all-gather = bf16[16,48,4]{1,2,0:T(4,128)(2,1)S(1)} all-gather(bf16[1,48,4]{1,2,0:T(4,128)(2,1)S(1)} %convert_bitcast_fusion), channel_id=1, replica_groups=mesh['rep'=2,'fsdp'=16] {'fsdp'}, dimensions={0}, use_global_device_ids=true | all-gather | bytes 6528 | tf_op jit(solution)/shard_map/all_gather | solution.py:111
  98.1 21.5 %all_gather.36 = bf16[196,768]{0,1:T(8,128)(2,1)S(1)} all-gather(bf16[196,48]{0,1:T(8,128)(2,1)S(1)} %convert_element_type.288), channel_id=1, replica_groups=mesh['rep'=2,'fsdp'=16] {'fsdp'}, dimensions={1}, use_global_device_ids=true | all-gather | bytes 319872 | tf_op jit(solution)/shard_map/all_gather | solution.py:107
  127.4 38.2 %all-reduce.4 = (bf16[96]{0:T(256)(128)(2,1)}, bf16[96]{0:T(256)(128)(2,1)}) all-reduce(bf16[96]{0:T(256)(128)(2,1)S(1)} %dynamic-update-slice, bf16[96]{0:T(256)(128)(2,1)S(1)} %dynamic-update-slice.2), channel_id=1, replica_groups=mesh['rep'=2,'fsdp'=16] {'rep','fsdp'}, use_global_device_ids=true, to_apply=%add | all-reduce | flops 192 | bytes 768
  177.5 7.6 fusion.308
  187.3 10.7 fusion.307
  269.3 11.1 multiply_convert_fusion.3
  295.3 7.6 fusion.56
  319.8 41.8 %all-gather.1 = bf16[32,3,768]{2,1,0:T(4,128)(2,1)S(1)} all-gather(bf16[1,3,768]{2,1,0:T(4,128)(2,1)S(1)} %fusion.94), channel_id=1, replica_groups=mesh['rep'=2,'fsdp'=16] {'rep','fsdp'}, dimensions={0}, use_global_device_ids=true | all-gather | bytes 152064 | tf_op jit(solution)/shard_map/all_gather | solution.py:204
  365.1 37.6 %all-gather.2 = bf16[32,3,768]{2,1,0:T(4,128)(2,1)S(1)} all-gather(bf16[1,3,768]{2,1,0:T(4,128)(2,1)S(1)} %fusion.95), channel_id=1, replica_groups=mesh['rep'=2,'fsdp'=16] {'rep','fsdp'}, dimensions={0}, use_global_device_ids=true | all-gather | bytes 152064 | tf_op jit(solution)/shard_map/all_gather | solution.py:204
  424.4 6.4 fusion.312
  431.8 9.2 fusion.309
  441.1 11.4 fusion.286
  470.6 17.3 %multiply_reduce_fusion.5 = (f32[3,196,12]{1,2,0:T(8,128)S(1)}, f32[3,12,64,196]{3,2,1,0:T(8,128)}) fusion(f32[3,196,12,64]{1,3,2,0:T(8,128)} %copy-done.15, f32[12,64]{1,0:T(8,128)S(1)} %mul.900, f32[3,12,196,196]{2,3,1,0:T(8,128)} %fusion.310, f32[3,12,196,196]{2,3,1,0:T(8,128)} %copy-done.11, f32[3,12,196]{2,1,0:T(8,128)S(1)} %copy-done.122, ...), kind=kOutput, calls=%fused_computation.96 | convolution fusion | flops 194943360 | bytes 16574220 | tf_op jit(solution)/shard_map/ihst,ithd->ishd/dot_general | solution.py:268
  487.9 17.4 %multiply_reduce_fusion.4 = (f32[3,196,12]{1,2,0:T(8,128)S(1)}, f32[3,12,64,196]{3,2,1,0:T(8,128)}) fusion(f32[3,196,12,64]{1,3,2,0:T(8,128)} %get-tuple-element.168, f32[12,64]{1,0:T(8,128)S(1)} %mul.906, f32[3,12,196,196]{2,3,1,0:T(8,128)} %fusion.310, f32[3,12,196,196]{2,3,1,0:T(8,128)} %copy-done.11, f32[3,12,196]{2,1,0:T(8,128)S(1)} %copy-done.122, ...), kind=kOutput, calls=%fused_computation.94 | convolution fusion | flops 194943360 | bytes 16574220 | tf_op jit(solution)/shard_map/ihst,ishd->ithd/dot_general | solution.py:271
  538.6 17.2 %fusion.65 = (f32[12,64]{1,0:T(8,128)}, f32[3,196,12]{1,2,0:T(8,128)S(1)}, f32[3,196,12]{1,2,0:T(8,128)S(1)}, f32[3,12,64,196]{3,2,1,0:T(8,128)}) fusion(f32[3,12,64,196]{3,2,1,0:T(8,128)} %get-tuple-element.232, f32[3,196,12,64]{1,3,2,0:T(8,128)} %get-tuple-element.168, f32[3,196,12]{1,2,0:T(8,128)S(1)} %fusion.186, ...), kind=kOutput, calls=%fused_computation.79 | convolution fusion | flops 198999792 | bytes 20274636 | tf_op jit(solution)/shard_map/ihst,ishd->ithd/dot_general | solution.py:271
  555.8 17.2 %fusion.66 = (f32[12,64]{1,0:T(8,128)}, f32[3,196,12]{1,2,0:T(8,128)S(1)}, f32[3,196,12]{1,2,0:T(8,128)S(1)}, f32[3,12,64,196]{3,2,1,0:T(8,128)}) fusion(f32[3,12,64,196]{3,2,1,0:T(8,128)} %get-tuple-element.235, f32[3,196,12,64]{1,3,2,0:T(8,128)} %copy-done.15, f32[3,196,12]{1,2,0:T(8,128)S(1)} %fusion.185, ...), kind=kOutput, calls=%fused_computation.82 | convolution fusion | flops 198999792 | bytes 20274636 | tf_op jit(solution)/shard_map/ihst,ithd->ishd/dot_general | solution.py:268
  591.3 6.9 add_convert_fusion.5
  607.0 10.6 fusion.96
  635.4 10.5 fusion.98
  662.6 6.1 fusion.283
  674.5 11.6 %fusion.57 = f32[3840,768]{1,0:T(8,128)} fusion(bf16[588,768]{1,0:T(8,128)(2,1)} %convert_element_type.327, bf16[588,3072]{1,0:T(8,128)(2,1)} %get-tuple-element.189, bf16[588,768]{1,0:T(8,128)(2,1)S(1)} %copy-done.51), kind=kOutput, calls=%fused_computation.57 | convolution fusion | flops 3477196800 | bytes 17215488 | tf_op jit(solution)/shard_map/dot_general | solution.py:26
  686.1 9.7 add_convert_fusion.1
  696.2 15.7 %fusion.97 = f32[768,5376]{1,0:T(8,128)} fusion(bf16[588,768]{1,0:T(8,128)(2,1)} %reshape.570, bf16[588,3072]{1,0:T(8,128)(2,1)} %get-tuple-element.188, bf16[588,768]{1,0:T(8,128)(2,1)} %reshape.613, bf16[588,768]{1,0:T(8,128)(2,1)} %reshape.612, bf16[588,768]{1,0:T(8,128)(2,1)} %reshape.611), kind=kOutput, calls=%fused_computation.173 | convolution fusion | flops 4880719872 | bytes 23740416 | tf_op jit(solution)/shard_map/dot_general | solution.py:26
  711.8 13.3 %add_convert_fusion = bf16[768,5376]{1,0:T(8,128)(2,1)} fusion(f32[768,5376]{1,0:T(8,128)} %fusion.97, bf16[588,768]{1,0:T(8,128)(2,1)} %copy-done.36, bf16[588,3072]{1,0:T(8,128)(2,1)} %get-tuple-element.160, bf16[588,768]{1,0:T(8,128)(2,1)S(1)} %copy-done.33, bf16[588,768]{1,0:T(8,128)(2,1)S(1)} %copy-done.34, bf16[588,768]{1,0:T(8,128)(2,1)S(1)} %copy-done.35), kind=kOutput, calls=%fused_computation.2 | convolution fusion | flops 4888977408 | bytes 31997952 | tf_op jit(solution)/shard_map/dot_general | solution.py:26
  729.5 85.7 %reduce-scatter.17.cloned.1.call-done = bf16[240,768]{1,0:T(8,128)(2,1)} async-done(((bf16[3840,768]{1,0:T(8,128)(2,1)}), bf16[240,768]{1,0:T(8,128)(2,1)}) %reduce-scatter.17.cloned.1.call-update) | async-done | bytes 368656 | tf_op jit(solution)/shard_map/reduce_scatter | solution.py:316
  815.2 107.6 %reduce-scatter.15.cloned.1.call-done = bf16[48,5376]{1,0:T(8,128)(2,1)} async-done(((bf16[768,5376]{1,0:T(8,128)(2,1)}), bf16[48,5376]{1,0:T(8,128)(2,1)}) %reduce-scatter.15.cloned.1.call-update) | async-done | bytes 516112 | tf_op jit(solution)/shard_map/reduce_scatter | solution.py:313
  929.4 60.3 %all-reduce.3 = bf16[4608]{0:T(1024)(128)(2,1)S(1)} all-reduce(bf16[4608]{0:T(1024)(128)(2,1)S(1)} %fusion.189), channel_id=8, replica_groups=mesh['rep'=2,'fsdp'=16] {'fsdp'}, use_global_device_ids=true, to_apply=%region_94.95.clone | all-reduce | flops 4608 | bytes 18432
  990.5 49.2 %reduce-scatter.21.cloned.1.call-done = bf16[48,196]{1,0:T(8,128)(2,1)} async-done(((bf16[768,196]{1,0:T(8,128)(2,1)}), bf16[48,196]{1,0:T(8,128)(2,1)}) %reduce-scatter.21.cloned.1.call-update) | async-done | bytes 18832
  1039.7 9.1 all-reduce.5
  1050.7 30.8 %all-reduce.9.cloned.1.call-done = (bf16[48,768]{1,0:T(8,128)(2,1)}, bf16[48,5376]{1,0:T(8,128)(2,1)}, bf16[240,768]{1,0:T(8,128)(2,1)}, bf16[48,768]{1,0:T(8,128)(2,1)}) async-done(((bf16[48,768]{1,0:T(8,128)(2,1)}, bf16[48,5376]{1,0:T(8,128)(2,1)}, bf16[240,768]{1,0:T(8,128)(2,1)}, bf16[48,768]{1,0:T(8,128)(2,1)}), (bf16[48,768]{1,0:T(8,128)(2,1)}, bf16[48,5376]{1,0:T(8,128)(2,1)}, ...) | async-done | bytes 1032208 | tf_op jit(solution)/shard_map/psum | solution.py:330
  1092.8 33.7 %psum.63 = f32[]{:T(128)} all-reduce(f32[]{:T(128)S(6)} %add.449), channel_id=1, replica_groups=mesh['rep'=2,'fsdp'=16] {'fsdp'}, use_global_device_ids=true, to_apply=%region_97.98 | all-reduce | flops 1 | bytes 8 | tf_op jit(solution)/shard_map/psum | solution.py:341
  (641 shorter events, 303.4 us)
Async XLA Ops:
  7.3 159.0 %all-gather.8.cloned.1.call-start = ((), (), s32[]{:S(2)}) async-start(), calls=%async_computation.6 | async-start | bytes 1253376 | tf_op jit(solution)/shard_map/all_gather | solution.py:106
  9.0 168.5 %all-gather.10.cloned.1.call-start = ((), (), s32[]{:S(2)}) async-start(), calls=%async_computation.7 | async-start | bytes 8773632 | tf_op jit(solution)/shard_map/all_gather | solution.py:108
  11.1 108.7 %copy-start.22 = (bf16[2,3,196,768]{3,0,2,1:T(2,128)(2,1)S(1)}, bf16[2,3,196,768]{3,0,2,1:T(2,128)(2,1)}, u32[]{:S(2)}) copy-start(bf16[2,3,196,768]{3,0,2,1:T(2,128)(2,1)} %param.27) | copy-start | bytes 5419012
  11.1 284.2 %all-gather.12.cloned.1.call-start = ((), (), s32[]{:S(2)}) async-start(), calls=%async_computation.8 | async-start | bytes 6266880 | tf_op jit(solution)/shard_map/all_gather | solution.py:109
  12.0 306.2 %all-gather.14.cloned.1.call-start = ((), (), s32[]{:S(2)}) async-start(), calls=%async_computation.9 | async-start | bytes 1253376 | tf_op jit(solution)/shard_map/all_gather | solution.py:110
  12.7 715.6 %reduce-scatter.23.cloned.1.call-start = ((), (), s32[]{:S(2)}) async-start(), calls=%async_computation.14 | async-start | bytes 1253376 | tf_op jit(solution)/shard_map/reduce_scatter | solution.py:319
  78.6 190.7 %copy-start.92 = (f32[3072]{0:T(1024)}, f32[3072]{0:T(1024)S(1)}, u32[]{:S(2)}) copy-start(f32[3072]{0:T(1024)S(1)} %slice.143) | copy-start | bytes 36868
  80.2 236.9 %copy-start.105 = (f32[3,196]{1,0:T(4,128)}, f32[3,196]{1,0:T(4,128)S(1)}, u32[]{:S(2)}) copy-start(f32[3,196]{1,0:T(4,128)S(1)} %get-tuple-element.243) | copy-start | bytes 7060
  80.2 236.9 %copy-start.108 = (f32[3,196]{1,0:T(4,128)}, f32[3,196]{1,0:T(4,128)S(1)}, u32[]{:S(2)}) copy-start(f32[3,196]{1,0:T(4,128)S(1)} %get-tuple-element.219) | copy-start | bytes 7060
  98.0 219.1 %copy-start.102 = (f32[768]{0:T(1024)}, f32[768]{0:T(1024)S(1)}, u32[]{:S(2)}) copy-start(f32[768]{0:T(1024)S(1)} %get-tuple-element.115) | copy-start | bytes 9220
  523.3 206.3 %reduce-scatter.19.cloned.1.call-start = ((), (), s32[]{:S(2)}) async-start(), calls=%async_computation.12 | async-start | bytes 1253376 | tf_op jit(solution)/shard_map/reduce_scatter | solution.py:307
  674.0 141.2 %reduce-scatter.17.cloned.1.call-start = ((), (), s32[]{:S(2)}) async-start(), calls=%async_computation.11 | async-start | bytes 6266880 | tf_op jit(solution)/shard_map/reduce_scatter | solution.py:316
  695.9 226.9 %reduce-scatter.15.cloned.1.call-start = ((), (), s32[]{:S(2)}) async-start(), calls=%async_computation.10 | async-start | bytes 8773632 | tf_op jit(solution)/shard_map/reduce_scatter | solution.py:313
  725.2 203.4 %copy-start.117 = (f32[3072]{0:T(1024)S(1)}, f32[3072]{0:T(1024)}, u32[]{:S(2)}) copy-start(f32[3072]{0:T(1024)} %get-tuple-element.159) | copy-start | bytes 36868
  725.2 203.4 %copy-start.118 = (f32[3072]{0:T(1024)S(1)}, f32[3072]{0:T(1024)}, u32[]{:S(2)}) copy-start(f32[3072]{0:T(1024)} %get-tuple-element.187) | copy-start | bytes 36868
  725.2 203.4 %copy-start.143 = (f32[768]{0:T(1024)S(1)}, f32[768]{0:T(1024)}, u32[]{:S(2)}) copy-start(f32[768]{0:T(1024)} %get-tuple-element.97) | copy-start | bytes 9220
  725.2 203.4 %copy-start.144 = (f32[768]{0:T(1024)S(1)}, f32[768]{0:T(1024)}, u32[]{:S(2)}) copy-start(f32[768]{0:T(1024)} %get-tuple-element.123) | copy-start | bytes 9220
  725.2 264.5 %reduce-scatter.25.cloned.1.call-start = ((), (), s32[]{:S(2)}) async-start(), calls=%async_computation.15 | async-start | bytes 208896
  727.1 312.6 %reduce-scatter.21.cloned.1.call-start = ((), (), s32[]{:S(2)}) async-start(), calls=%async_computation.13 | async-start | bytes 417792
  727.1 400.1 %copy-start.172 = (f32[288]{0:T(512)S(1)}, f32[288]{0:T(512)}, u32[]{:S(2)}) copy-start(f32[288]{0:T(512)} %param.39) | copy-start | bytes 3460
  727.1 401.4 %copy-start.174 = (f32[4,48]{1,0:T(4,128)S(1)}, f32[4,48]{1,0:T(4,128)}, u32[]{:S(2)}) copy-start(f32[4,48]{1,0:T(4,128)} %param.38) | copy-start | bytes 2308
  727.1 402.8 %copy-start.80 = (f32[196,48]{0,1:T(8,128)S(1)}, f32[196,48]{0,1:T(8,128)}, u32[]{:S(2)}) copy-start(f32[196,48]{0,1:T(8,128)} %param.34) | copy-start | bytes 112900
  727.2 404.2 %copy-start.63 = (f32[48,768]{1,0:T(8,128)S(1)}, f32[48,768]{1,0:T(8,128)}, u32[]{:S(2)}) copy-start(f32[48,768]{1,0:T(8,128)} %param.37) | copy-start | bytes 442372
  727.2 404.2 %copy-start.82 = (f32[48,768]{1,0:T(8,128)S(1)}, f32[48,768]{1,0:T(8,128)}, u32[]{:S(2)}) copy-start(f32[48,768]{1,0:T(8,128)} %param.51) | copy-start | bytes 442372
  727.2 404.2 %copy-start.83 = (f32[48,768]{1,0:T(8,128)S(1)}, f32[48,768]{1,0:T(8,128)}, u32[]{:S(2)}) copy-start(f32[48,768]{1,0:T(8,128)} %param.44) | copy-start | bytes 442372
  727.3 405.8 %copy-start.64 = (f32[48,768]{1,0:T(8,128)S(1)}, f32[48,768]{1,0:T(8,128)}, u32[]{:S(2)}) copy-start(f32[48,768]{1,0:T(8,128)} %param.33) | copy-start | bytes 442372
  727.3 405.8 %copy-start.84 = (f32[48,768]{1,0:T(8,128)S(1)}, f32[48,768]{1,0:T(8,128)}, u32[]{:S(2)}) copy-start(f32[48,768]{1,0:T(8,128)} %param.47) | copy-start | bytes 442372
  727.3 405.8 %copy-start.85 = (f32[48,768]{1,0:T(8,128)S(1)}, f32[48,768]{1,0:T(8,128)}, u32[]{:S(2)}) copy-start(f32[48,768]{1,0:T(8,128)} %param.40) | copy-start | bytes 442372
  728.3 406.8 %copy-start.40 = (f32[240,768]{1,0:T(8,128)S(1)}, f32[240,768]{1,0:T(8,128)}, u32[]{:S(2)}) copy-start(f32[240,768]{1,0:T(8,128)} %param.36) | copy-start | bytes 2211844
  728.3 406.8 %copy-start.58 = (f32[240,768]{1,0:T(8,128)S(1)}, f32[240,768]{1,0:T(8,128)}, u32[]{:S(2)}) copy-start(f32[240,768]{1,0:T(8,128)} %param.50) | copy-start | bytes 2211844
  728.3 406.8 %copy-start.59 = (f32[240,768]{1,0:T(8,128)S(1)}, f32[240,768]{1,0:T(8,128)}, u32[]{:S(2)}) copy-start(f32[240,768]{1,0:T(8,128)} %param.43) | copy-start | bytes 2211844
  728.3 353.2 %all-reduce.9.cloned.1.call-start = ((), (), s32[]{:S(2)}) async-start(), calls=%async_computation.16 | async-start | bytes 2064384 | tf_op jit(solution)/shard_map/psum | solution.py:330
  (176 other events, 2484.3 us)
Sparse Core Ops, SparseCore 0:
  11.0 41.1 all-gather.7
  55.1 76.4 all-gather.9
  134.5 59.2 all-gather.11
  196.5 36.8 all-gather.13
  523.4 55.5 reduce-scatter.22
  674.1 55.3 reduce-scatter.18
  733.5 81.6 reduce-scatter.16
  819.8 102.9 reduce-scatter.14
  927.3 53.3 reduce-scatter.24
  985.1 54.5 reduce-scatter.20
  1042.2 39.2 all-reduce.8
where the time goes:
time: 1160 us; the launch traced here: 1150 us
  blocking collectives  323 us (28%)
  waiting for transfers between devices  275 us (24%)
  matrix products  251 us (22%)
  local copies, waits for them, and re-layouts  160 us (14%)
  other arithmetic  108 us (9%)
  between operations  31.8 us (3%)
    unnamed x3, blocking collectives  162 us
    reduce_scatter x1, waiting for transfers between devices, per_device(): lax.psum_scatter(grad_wide.astype(jnp.bfloat16), 'fsdp', scatter_dimensio...  108 us
    reduce_scatter x1, waiting for transfers between devices, per_device(): lax.psum_scatter(grad_narrow.astype(jnp.bfloat16), 'fsdp', scatter_dimens...  85.7 us
    all_gather x2, blocking collectives, per_device(): lax.all_gather(embeds, ('rep', 'fsdp'), axis=0, tiled=True)  79.4 us
    dot_general x8, matrix products, product_across(): lax.dot_general(left, right, (((0,), (0,)), ((), ())), preferred_element_...  57.7 us
    unnamed x13, waiting for transfers between devices  49.4 us
    dot_general x10, matrix products, product(): return jnp.dot(left, right, preferred_element_type=jnp.float32)  39.4 us
    dot_general x8, matrix products, product_along(): lax.dot_general(left, right, (((1,), (1,)), ((), ())), preferred_element_...  39.2 us
  transfers between devices with their start and end apart: 11, of which 5 were waited for; matrix products, arithmetic and copies ran while one was open for 31% of the time, Pallas kernels for 0%

commit v1 on v0

--- a/solution.py
+++ b/solution.py
@@ -71,6 +71,134 @@
     square_hat = square_new / (1.0 - beta_second**step_number)
     change = -learn_rate * (mean_hat / (jnp.sqrt(square_hat) + adam_eps) + weight_decay * weight)
     return (change, clipped)
+
+
+def bit_swap(size, bit):
+    return [(index, index ^ bit) for index in range(size)]
+
+
+def ordered_pair(own, other, axis, bit):
+    low_side = (lax.axis_index(axis) & bit) == 0
+    return jnp.where(low_side, own, other), jnp.where(low_side, other, own)
+
+
+def exchange_steps():
+    steps = []
+    for axis in ("fsdp", "rep"):
+        size = lax.axis_size(axis)
+        bit = 1
+        while bit < size:
+            steps.append((axis, size, bit))
+            bit *= 2
+    return steps
+
+
+def column_totals(top, total, sums):
+    micro_count = top.shape[0]
+    for axis, size, bit in exchange_steps():
+        packed = jnp.concatenate([top, total, sums], axis=0)
+        other = lax.ppermute(packed, axis, bit_swap(size, bit))
+        first, second = ordered_pair(packed, other, axis, bit)
+        top_a, top_b = first[:micro_count], second[:micro_count]
+        top = jnp.maximum(top_a, top_b)
+        total = first[micro_count : 2 * micro_count] * jnp.exp(top_a - top) + second[
+            micro_count : 2 * micro_count
+        ] * jnp.exp(top_b - top)
+        sums = first[2 * micro_count :] + second[2 * micro_count :]
+    return top, total, sums
+
+
+def sum_over(value, axis):
+    size = lax.axis_size(axis)
+    bit = 1
+    while bit < size:
+        value = value + lax.ppermute(value, axis, bit_swap(size, bit))
+        bit *= 2
+    return value
+
+
+def pack_weights(embedder, positions, widener, narrower, projector, scales, biases):
+    model_width = embedder.shape[1]
+    blocks = widener.shape[1] // model_width
+    rows = [embedder]
+    rows += [widener[:, k * model_width : (k + 1) * model_width] for k in range(blocks)]
+    rows += [narrower, projector]
+    small = jnp.concatenate([positions.reshape(-1), scales.reshape(-1), biases.reshape(-1)])
+    small_rows = -(-small.shape[0] // (16 * model_width)) * 16
+    small = jnp.pad(small, (0, small_rows * model_width - small.shape[0]))
+    rows.append(small.reshape(small_rows, model_width))
+    return jnp.concatenate(rows, axis=0)
+
+
+def unpack_weights(full, shapes):
+    owners, _, width = full.shape
+    (e_rows, _), (slots, p_cols), (w_rows, w_cols), (n_rows, _), (j_rows, _), (s_rows, s_cols), (
+        b_len,
+    ) = shapes
+    at = 0
+    embed = full[:, at : at + e_rows].reshape(owners * e_rows, width)
+    at += e_rows
+    wide = []
+    for _ in range(w_cols // width):
+        wide.append(full[:, at : at + w_rows].reshape(owners * w_rows, width))
+        at += w_rows
+    narrow = full[:, at : at + n_rows].reshape(owners * n_rows, width)
+    at += n_rows
+    project = full[:, at : at + j_rows].reshape(owners * j_rows, width)
+    at += j_rows
+    small = full[:, at:].reshape(owners, -1)
+    place = small[:, : slots * p_cols].reshape(owners, slots, p_cols)
+    place = jnp.swapaxes(place, 0, 1).reshape(slots, owners * p_cols)
+    at = slots * p_cols
+    scale = small[:, at : at + s_rows * s_cols].reshape(owners, s_rows, s_cols)
+    scale = jnp.swapaxes(scale, 0, 1).reshape(s_rows, owners * s_cols)
+    at += s_rows * s_cols
+    bias = small[:, at : at + b_len].reshape(owners * b_len)
+    return embed, place, wide, narrow, project, scale, bias
+
+
+def pack_grads(owners, embed, place, wide, narrow, project, scale, bias):
+    width = embed.shape[1]
+    by_owner = lambda grad: grad.astype(jnp.bfloat16).reshape(owners, -1, width)
+    rows = [by_owner(embed)]
+    rows += [by_owner(block) for block in wide]
+    rows += [by_owner(narrow), by_owner(project)]
+    flat = lambda grad: jnp.swapaxes(
+        grad.astype(jnp.bfloat16).reshape(grad.shape[0], owners, -1), 0, 1
+    ).reshape(owners, -1)
+    small = jnp.concatenate(
+        [flat(place), flat(scale), bias.astype(jnp.bfloat16).reshape(owners, -1)], axis=1
+    )
+    small_rows = -(-small.shape[1] // (16 * width)) * 16
+    small = jnp.pad(small, ((0, 0), (0, small_rows * width - small.shape[1])))
+    rows.append(small.reshape(owners, small_rows, width))
+    return jnp.concatenate(rows, axis=1)
+
+
+def unpack_grads(shard, shapes):
+    (e_rows, width), (slots, p_cols), (w_rows, w_cols), (n_rows, _), (j_rows, _), (
+        s_rows,
+        s_cols,
+    ), (b_len,) = shapes
+    at = 0
+    embed = shard[at : at + e_rows]
+    at += e_rows
+    wide = []
+    for _ in range(w_cols // width):
+        wide.append(shard[at : at + w_rows])
+        at += w_rows
+    wide = jnp.concatenate(wide, axis=1)
+    narrow = shard[at : at + n_rows]
+    at += n_rows
+    project = shard[at : at + j_rows]
+    at += j_rows
+    small = shard[at:].reshape(-1)
+    place = small[: slots * p_cols].reshape(slots, p_cols)
+    at = slots * p_cols
+    scale = small[at : at + s_rows * s_cols].reshape(s_rows, s_cols)
+    at += s_rows * s_cols
+    bias = small[at : at + b_len]
+    return embed, place, wide, narrow, project, scale, bias
 
 
 def per_device(
@@ -102,18 +230,15 @@
     square_scales,
     square_biases,
 ):
-    gathered_weights = (
-        lax.all_gather(embedder.astype(jnp.bfloat16), "fsdp", axis=0, tiled=True),
-        lax.all_gather(positions.astype(jnp.bfloat16), "fsdp", axis=1, tiled=True),
-        lax.all_gather(widener.astype(jnp.bfloat16), "fsdp", axis=0, tiled=True),
-        lax.all_gather(narrower.astype(jnp.bfloat16), "fsdp", axis=0, tiled=True),
-        lax.all_gather(projector.astype(jnp.bfloat16), "fsdp", axis=0, tiled=True),
-        lax.all_gather(scales.astype(jnp.bfloat16), "fsdp", axis=1, tiled=True),
-        lax.all_gather(biases.astype(jnp.bfloat16), "fsdp", axis=0, tiled=True),
-    )
-    embed_full, place_full, wide_full, narrow_full, project_full, scale_full, bias_full = (
-        gathered_weights
-    )
+    weights = (embedder, positions, widener, narrower, projector, scales, biases)
+    shapes = tuple(weight.shape for weight in weights)
+    owners = lax.axis_size("fsdp")
+    packed = pack_weights(*(weight.astype(jnp.bfloat16) for weight in weights))
+    full = lax.all_gather(packed, "fsdp", axis=0)
+    embed_full, place_full, wide_blocks, narrow_full, project_full, scale_full, bias_full = (
+        unpack_weights(full, shapes)
+    )
+    wide_full = jnp.concatenate(wide_blocks, axis=1)
     place_float = place_full.astype(jnp.float32)
     scale_float = scale_full.astype(jnp.float32)
     bias_float = bias_full.astype(jnp.float32)
@@ -126,8 +251,6 @@
     embed_width = captions.shape[2]
     logit_factor = logit_temper * embed_width ** (-0.5)
     attend_factor = head_size ** (-0.5)
-    fsdp_count = lax.axis_size("fsdp")
-    first_row = (lax.axis_index("rep") * fsdp_count + lax.axis_index("fsdp")) * images_dev
     row_count = images_dev * slot_total
     grad_embed = jnp.zeros(embed_full.shape, jnp.float32)
     grad_place = jnp.zeros(place_full.shape, jnp.float32)
@@ -136,9 +259,8 @@
     grad_project = jnp.zeros(project_full.shape, jnp.float32)
     grad_scale = jnp.zeros(scale_full.shape, jnp.float32)
     grad_bias = jnp.zeros(bias_full.shape, jnp.float32)
-    objective = jnp.zeros((), jnp.float32)
-    weight_total_all = jnp.zeros((), jnp.float32)
     image_ids = jnp.arange(images_all, dtype=jnp.int32)
+    kept = []
     for step_index in range(micro_count):
         pixel_rows = pixels[step_index].reshape(row_count, patch_size)
         live_count = counts[step_index]
@@ -200,40 +322,54 @@
         )
         pooled_low = pooled.astype(jnp.bfloat16)
         embeds = product(pooled_low, project_full).astype(jnp.bfloat16)
-        everyone, count_all = (
-            lax.all_gather(embeds, ("rep", "fsdp"), axis=0, tiled=True),
-            lax.all_gather(count_float.astype(jnp.bfloat16), ("rep", "fsdp"), axis=0, tiled=True),
-        )
+        kept.append((pixel_rows, live_mask, count_float, key_live, merger, merged, normed_back, normed_low, query_low, key_low, value_low, query_back, key_back, log_total, joined, gelu_back, pool_back, pooled_low, embeds))
+    all_embeds = jnp.concatenate([item[-1] for item in kept], axis=0)
+    all_logits = [
+        product_along(kept[index][-1], captions[index]) * logit_factor
+        for index in range(micro_count)
+    ]
+    first_row = (lax.axis_index("rep") * owners + lax.axis_index("fsdp")) * images_dev
+    logits = jnp.stack(all_logits)
+    own_pairs = lax.dynamic_slice_in_dim(pairing, first_row, images_dev, 1)
+    target = (own_pairs[:, :, None] == image_ids[None, None, :]).astype(jnp.float32)
+    row_top = jnp.max(logits, axis=2, keepdims=True)
+    row_logsum = row_top[:, :, 0] + jnp.log(jnp.sum(jnp.exp(logits - row_top), axis=2))
+    own_top = jnp.max(logits, axis=1)
+    own_total = jnp.sum(jnp.exp(logits - own_top[:, None, :]), axis=1)
+    picked = jnp.sum(logits * target, axis=2)
+    counts_float = counts.astype(jnp.float32)
+    scalars = jnp.concatenate(
+        [
+            jnp.sum(counts_float * (picked - row_logsum), axis=1),
+            jnp.sum(picked, axis=1),
+            jnp.sum(counts_float, axis=1),
+        ]
+    )
+    sums = jnp.pad(scalars[None, :], ((0, 0), (0, images_all - scalars.shape[0])))
+    column_top, column_total, sums = column_totals(own_top, own_total, sums)
+    column_logsum = column_top + jnp.log(column_total)
+    row_terms = sums[0, :micro_count]
+    picked_sums = sums[0, micro_count : 2 * micro_count]
+    weight_totals = sums[0, 2 * micro_count : 3 * micro_count]
+    weight_total_all = jnp.sum(weight_totals)
+    part_losses = 0.5 * (
+        -row_terms / weight_totals - (picked_sums - jnp.sum(column_logsum, axis=1)) / images_all
+    )
+    objective = jnp.sum(part_losses) / micro_count
+    row_soft = jnp.exp(logits - row_logsum[:, :, None])
+    column_soft = jnp.exp(logits - column_logsum[:, None, :])
+    all_grad_logits = (
+        0.5
+        / micro_count
+        * (
+            (counts_float / weight_totals[:, None])[:, :, None] * (row_soft - target)
+            + (column_soft - target) / images_all
+        )
+    )
+    for step_index in range(micro_count):
+        (pixel_rows, live_mask, count_float, key_live, merger, merged, normed_back, normed_low, query_low, key_low, value_low, query_back, key_back, log_total, joined, gelu_back, pool_back, pooled_low, embeds) = kept[step_index]
+        grad_logits = all_grad_logits[step_index]
         caption_rows = captions[step_index]
-        logits = product_along(everyone, caption_rows) * logit_factor
-        row_top = jnp.max(logits, axis=1, keepdims=True)
-        row_logsum = row_top[:, 0] + jnp.log(jnp.sum(jnp.exp(logits - row_top), axis=1))
-        column_top = jnp.max(logits, axis=0, keepdims=True)
-        column_logsum = column_top[0] + jnp.log(jnp.sum(jnp.exp(logits - column_top), axis=0))
-        target = (pairing[step_index][:, None] == image_ids[None, :]).astype(jnp.float32)
-        picked = jnp.sum(logits * target, axis=1)
-        column_pick = jnp.sum(target * column_logsum[None, :], axis=1)
-        weight_all = count_all.astype(jnp.float32)
-        weight_total = jnp.sum(weight_all)
-        weight_total_all = weight_total_all + weight_total
-        part_loss = 0.5 * (
-            -jnp.sum(weight_all * (picked - row_logsum)) / weight_total
-            - jnp.mean(picked - column_pick)
-        )
-        objective = objective + part_loss / micro_count
-        own_logits = lax.dynamic_slice_in_dim(logits, first_row, images_dev, 0)
-        own_target = lax.dynamic_slice_in_dim(target, first_row, images_dev, 0)
-        own_logsum = lax.dynamic_slice_in_dim(row_logsum, first_row, images_dev, 0)
-        row_soft = jnp.exp(own_logits - own_logsum[:, None])
-        column_soft = jnp.exp(own_logits - column_logsum[None, :])
-        grad_logits = (
-            0.5
-            / micro_count
-            * (
-                (count_float / weight_total)[:, None] * (row_soft - own_target)
-                + (column_soft - own_target) / images_all
-            )
-        )
         grad_product = (grad_logits * logit_factor).astype(jnp.bfloat16)
         grad_embeds = product(grad_product, caption_rows).astype(jnp.bfloat16)
         grad_project = grad_project + product_across(pooled_low, grad_embeds)
@@ -303,44 +439,18 @@
                 jnp.sum(grad_patches, axis=(0, 1)),
             ]
         )
-    pieces = (
-        lax.psum_scatter(
-            grad_embed.astype(jnp.bfloat16), "fsdp", scatter_dimension=0, tiled=True
-        ).astype(jnp.float32),
-        lax.psum_scatter(
-            grad_place.astype(jnp.bfloat16), "fsdp", scatter_dimension=1, tiled=True
-        ).astype(jnp.float32),
-        lax.psum_scatter(
-            grad_wide.astype(jnp.bfloat16), "fsdp", scatter_dimension=0, tiled=True
-        ).astype(jnp.float32),
-        lax.psum_scatter(
-            grad_narrow.astype(jnp.bfloat16), "fsdp", scatter_dimension=0, tiled=True
-        ).astype(jnp.float32),
-        lax.psum_scatter(
-            grad_project.astype(jnp.bfloat16), "fsdp", scatter_dimension=0, tiled=True
-        ).astype(jnp.float32),
-        lax.psum_scatter(
-            grad_scale.astype(jnp.bfloat16), "fsdp", scatter_dimension=1, tiled=True
-        ).astype(jnp.float32),
-        lax.psum_scatter(
-            grad_bias.astype(jnp.bfloat16), "fsdp", scatter_dimension=0, tiled=True
-        ).astype(jnp.float32),
-    )
-    shards = (
-        lax.psum(pieces[0].astype(jnp.bfloat16), "rep").astype(jnp.float32),
-        lax.psum(pieces[1].astype(jnp.bfloat16), "rep").astype(jnp.float32),
-        lax.psum(pieces[2].astype(jnp.bfloat16), "rep").astype(jnp.float32),
-        lax.psum(pieces[3].astype(jnp.bfloat16), "rep").astype(jnp.float32),
-        lax.psum(pieces[4].astype(jnp.bfloat16), "rep").astype(jnp.float32),
-        lax.psum(pieces[5].astype(jnp.bfloat16), "rep").astype(jnp.float32),
-        lax.psum(pieces[6].astype(jnp.bfloat16), "rep").astype(jnp.float32),
-    )
-    local_square = jnp.zeros((), jnp.float32)
-    for shard in shards:
-        local_square = local_square + jnp.sum(shard * shard)
-    total_norm = jnp.sqrt(lax.psum(local_square, "fsdp"))
+    wide_parts = [
+        grad_wide[:, k * model_width : (k + 1) * model_width]
+        for k in range(grad_wide.shape[1] // model_width)
+    ]
+    packed_grads = pack_grads(
+        owners, grad_embed, grad_place, wide_parts, grad_narrow, grad_project, grad_scale, grad_bias
+    )
+    shard = lax.psum_scatter(packed_grads, "fsdp", scatter_dimension=0)
+    shard = lax.psum(shard, "rep").astype(jnp.float32)
+    total_norm = jnp.sqrt(sum_over(jnp.sum(shard * shard), "fsdp"))
+    shards = unpack_grads(shard, shapes)
     factor = clip_bound / jnp.maximum(total_norm, clip_bound)
-    weights = (embedder, positions, widener, narrower, projector, scales, biases)
     moments = (
         moment_embedder,
         moment_positions,

time: 1160 us -> 953 us (0.82)
  blocking collectives: 323 us -> 0 us
  local copies, waits for them, and re-layouts: 160 us -> 225 us
  waiting for transfers between devices: 275 us -> 312 us
  starting transfers between devices: 1.03 us -> 16.8 us
    unnamed x3 -> x0, blocking collectives: 162 us -> none
    all_gather x4 -> x0, blocking collectives: 118 us -> none  [the longest x2 79.4 us: per_device(): lax.all_gather(embeds, ('rep', 'fsdp'), axis=0, tiled=True)]
    all_gather x4 -> x1, waiting for transfers between devices: 0.05 us -> 77.7 us  [per_device(): full = lax.all_gather(packed, 'fsdp', axis=0)]
    unnamed x13 -> x3, waiting for transfers between devices: 49.4 us -> 0.05 us
    psum x2 -> x0, blocking collectives: 42.8 us -> none  [the longest x1 33.7 us: per_device(): total_norm = jnp.sqrt(lax.psum(local_square, 'fsdp'))]
    unnamed x412 -> x492, local copies, waits for them, and re-layouts: 19.9 us -> 42 us
    slice x1 -> x8, local copies, waits for them, and re-layouts: 0.59 us -> 19.7 us  [the longest x1 7.69 us: unpack_weights(): wide.append(full[:, at:at + w_rows].reshape(owners * w_rows, width))]
    ppermute x0 -> x9, starting transfers between devices: none -> 16.6 us  [the longest x4 9.45 us: sum_over(): value = value + lax.ppermute(value, axis, bit_swap(size, bit))]
  transfers between devices with their start and end apart: 11 -> 12, of which waited for: 5 -> 12; matrix products, arithmetic and copies ran while one was open for 31% -> 2% of each run, Pallas kernels for 0% -> 0%
where the time goes in v1:
time: 953 us; the launch traced here: 944 us
  waiting for transfers between devices  312 us (33%)
  matrix products  250 us (26%)
  local copies, waits for them, and re-layouts  225 us (24%)
  other arithmetic  117 us (12%)
  between operations  23.4 us (2%)
  starting transfers between devices  16.8 us (2%)
    reduce_scatter x1, waiting for transfers between devices, per_device(): shard = lax.psum_scatter(packed_grads, 'fsdp', scatter_dimension=0)  181 us
    all_gather x1, waiting for transfers between devices, per_device(): full = lax.all_gather(packed, 'fsdp', axis=0)  77.7 us
    dot_general x8, matrix products, product_across(): lax.dot_general(left, right, (((0,), (0,)), ((), ())), preferred_element_...  57.2 us
    unnamed x492, local copies, waits for them, and re-layouts  42 us
    dot_general x8, matrix products, product_along(): lax.dot_general(left, right, (((1,), (1,)), ((), ())), preferred_element_...  40.3 us
    psum x1, waiting for transfers between devices, per_device(): shard = lax.psum(shard, 'rep').astype(jnp.float32)  40.3 us
    dot_general x8, matrix products, product(): return jnp.dot(left, right, preferred_element_type=jnp.float32)  34.4 us
    dot_general x2, matrix products, per_device(): jnp.einsum('ihst,ithd->ishd', grad_scores, key_low, preferred_element_typ...  34.1 us
  transfers between devices with their start and end apart: 12, of which 12 were waited for; matrix products, arithmetic and copies ran while one was open for 2% of the time, Pallas kernels for 0%

profile of v1, /device:TPU:0, one launch (start us, length us, event | category | flops | bytes accessed | tf_op | source)
XLA Modules:
  0.0 944.1 jit_solution(9730533646610090198)
XLA Ops:
  19.5 8.7 slice_reduce_fusion.1
  34.3 77.7 %all-gather.3.cloned.1.call-done = bf16[11008,768]{1,0:T(8,128)(2,1)} async-done(((bf16[688,768]{1,0:T(8,128)(2,1)}), bf16[11008,768]{1,0:T(8,128)(2,1)}) %all-gather.3.cloned.1.call-update) | async-done | bytes 16908304 | tf_op jit(solution)/shard_map/all_gather | solution.py:237
  114.5 5.6 slice.481
  120.2 7.7 fusion.267
  158.0 5.1 fusion.287
  170.9 7.5 fusion.286
  208.2 5.1 reshape.712
  265.1 9.3 multiply_convert_fusion.2
  278.7 4.8 dot_general.152
  283.5 8.6 fusion.277
  313.3 5.0 dot_general.142
  318.4 8.4 fusion.276
  363.9 11.9 %fusion.261 = f32[3840,768]{1,0:T(8,128)} fusion(bf16[588,768]{1,0:T(8,128)(2,1)} %convert_element_type.331, bf16[588,3072]{1,0:T(8,128)(2,1)} %get-tuple-element.199, bf16[588,768]{1,0:T(8,128)(2,1)} %copy-done.49), kind=kOutput, calls=%fused_computation.490 | convolution fusion | flops 3477196800 | bytes 17215488 | tf_op jit(solution)/shard_map/dot_general | solution.py:26
  375.9 6.5 fusion.288
  382.4 10.9 %fusion.291 = f32[588,3840]{1,0:T(8,128)} fusion(bf16[588,768]{1,0:T(8,128)(2,1)} %convert_element_type.339, bf16[3840,768]{1,0:T(8,128)(2,1)} %bitcast.222), kind=kOutput, calls=%fused_computation.512 | convolution fusion | flops 3468165120 | bytes 15833088 | tf_op jit(solution)/shard_map/dot_general | solution.py:32
  395.0 11.4 %fusion.264 = (f32[3072]{0:T(1024)}, bf16[588,3072]{1,0:T(8,128)(2,1)}, f32[3072]{0:T(1024)}, bf16[588,3072]{1,0:T(8,128)(2,1)}) fusion(f32[588,3840]{1,0:T(8,128)} %fusion.291, f32[3072]{0:T(1024)S(1)} %copy-done.123, f32[588,5376]{1,0:T(8,128)S(1)} %bitcast.213, f32[588,3840]{1,0:T(8,128)} %fusion.288, f32[588,5376]{1,0:T(8,128)S(1)} %bitcast.215), kind=kLoop, calls=%fused_computation.493 | loop fusion | flops 54183936 | bytes 36163584 | tf_op jit(solution)/shard_map/reduce_sum | solution.py:437
  414.6 6.4 fusion.84
  429.6 6.4 fusion.85
  440.2 17.6 %multiply_reduce_fusion.3 = (f32[3,196,12]{1,2,0:T(8,128)}, f32[3,12,64,196]{3,2,1,0:T(8,128)}) fusion(f32[3,196,12,64]{1,3,2,0:T(8,128)S(1)} %copy-done.21, f32[12,64]{1,0:T(8,128)S(1)} %copy-done.98, f32[3,12,196,196]{2,3,1,0:T(8,128)} %fusion.292, f32[3,12,196,196]{2,3,1,0:T(8,128)} %copy-done.14, f32[3,12,196]{2,1,0:T(8,128)S(1)} %copy-done.153, ...), kind=kOutput, calls=%fused_computation.89 | convolution fusion | flops 194943360 | bytes 16574220 | tf_op jit(solution)/shard_map/ihst,ithd->ishd/dot_general | solution.py:404
  457.8 16.5 %multiply_reduce_fusion.2 = (f32[3,196,12]{1,2,0:T(8,128)}, f32[3,12,64,196]{3,2,1,0:T(8,128)}) fusion(f32[3,196,12,64]{1,3,2,0:T(8,128)} %copy-done.22, f32[12,64]{1,0:T(8,128)} %mul.893, f32[3,12,196,196]{2,3,1,0:T(8,128)} %fusion.292, f32[3,12,196,196]{2,3,1,0:T(8,128)} %copy-done.14, f32[3,12,196]{2,1,0:T(8,128)} %copy-done.152, ...), kind=kOutput, calls=%fused_computation.87 | convolution fusion | flops 194943360 | bytes 16574220 | tf_op jit(solution)/shard_map/ihst,ishd->ithd/dot_general | solution.py:407
  482.2 16.6 %fusion.60 = (f32[12,64]{1,0:T(8,128)}, f32[3,196,12]{1,2,0:T(8,128)S(1)}, f32[3,196,12]{1,2,0:T(8,128)S(1)}, f32[3,12,64,196]{3,2,1,0:T(8,128)}) fusion(f32[3,12,64,196]{3,2,1,0:T(8,128)} %get-tuple-element.243, f32[3,196,12,64]{1,3,2,0:T(8,128)} %copy-done.22, f32[3,196,12]{1,2,0:T(8,128)S(1)} %copy-done.84, ...), kind=kOutput, calls=%fused_computation.70 | convolution fusion | flops 198999792 | bytes 20274636 | tf_op jit(solution)/shard_map/ihst,ishd->ithd/dot_general | solution.py:407
  498.9 16.5 %fusion.61 = (f32[12,64]{1,0:T(8,128)}, f32[3,196,12]{1,2,0:T(8,128)S(1)}, f32[3,196,12]{1,2,0:T(8,128)S(1)}, f32[3,12,64,196]{3,2,1,0:T(8,128)}) fusion(f32[3,12,64,196]{3,2,1,0:T(8,128)} %get-tuple-element.246, f32[3,196,12,64]{1,3,2,0:T(8,128)} %copy-done.20, f32[3,196,12]{1,2,0:T(8,128)S(1)} %copy-done.80, ...), kind=kOutput, calls=%fused_computation.73 | convolution fusion | flops 198999792 | bytes 20274636 | tf_op jit(solution)/shard_map/ihst,ithd->ishd/dot_general | solution.py:404
  533.7 6.1 add_convert_fusion.5
  546.0 10.6 %fusion.94 = f32[588,768]{1,0:T(8,128)} fusion(bf16[768,5376]{1,0:T(8,128)(2,1)} %copy-done.115, bf16[588,3072]{1,0:T(8,128)(2,1)} %get-tuple-element.197, bf16[588,768]{1,0:T(8,128)(2,1)S(1)} %copy-done.61, bf16[588,768]{1,0:T(8,128)(2,1)} %reshape.747, bf16[588,768]{1,0:T(8,128)(2,1)} %reshape.746), kind=kOutput, calls=%fused_computation.171 | convolution fusion | flops 4880719872 | bytes 16386048 | tf_op jit(solution)/shard_map/dot_general | solution.py:32
  556.7 10.5 %fusion.93 = f32[768,5376]{1,0:T(8,128)} fusion(bf16[588,768]{1,0:T(8,128)(2,1)S(1)} %copy-done.66, bf16[588,3072]{1,0:T(8,128)(2,1)S(1)} %copy-done.53, bf16[588,768]{1,0:T(8,128)(2,1)S(1)} %copy-done.61, bf16[588,768]{1,0:T(8,128)(2,1)S(1)} %copy-done.62, bf16[588,768]{1,0:T(8,128)(2,1)S(1)} %copy-done.63), kind=kOutput, calls=%fused_computation.170 | convolution fusion | flops 4880719872 | bytes 23740416 | tf_op jit(solution)/shard_map/dot_general | solution.py:26
  569.2 11.6 %add_convert_fusion.1 = bf16[3840,768]{1,0:T(8,128)(2,1)} fusion(f32[3840,768]{1,0:T(8,128)} %fusion.261, bf16[588,768]{1,0:T(8,128)(2,1)S(1)} %copy-done.67, bf16[588,3072]{1,0:T(8,128)(2,1)} %copy-done.25, bf16[588,768]{1,0:T(8,128)(2,1)S(1)} %copy-done.48), kind=kOutput, calls=%fused_computation.3 | convolution fusion | flops 3483095040 | bytes 23113728 | tf_op jit(solution)/shard_map/dot_general | solution.py:26
  598.7 10.5 %fusion.92 = f32[588,768]{1,0:T(8,128)} fusion(bf16[768,5376]{1,0:T(8,128)(2,1)} %copy-done.115, bf16[588,3072]{1,0:T(8,128)(2,1)} %get-tuple-element.145, bf16[588,768]{1,0:T(8,128)(2,1)S(1)} %reshape.751, bf16[588,768]{1,0:T(8,128)(2,1)} %reshape.750, bf16[588,768]{1,0:T(8,128)(2,1)} %reshape.749), kind=kOutput, calls=%fused_computation.169 | convolution fusion | flops 4880719872 | bytes 16386048 | tf_op jit(solution)/shard_map/dot_general | solution.py:32
  621.6 7.2 fusion.262
  630.5 7.1 fusion.263
  648.8 14.1 %add_convert_fusion = bf16[768,5376]{1,0:T(8,128)(2,1)} fusion(f32[768,5376]{1,0:T(8,128)} %fusion.93, bf16[588,768]{1,0:T(8,128)(2,1)} %copy-done.52, bf16[588,3072]{1,0:T(8,128)(2,1)} %get-tuple-element.145, bf16[588,768]{1,0:T(8,128)(2,1)S(1)} %reshape.751, bf16[588,768]{1,0:T(8,128)(2,1)S(1)} %copy-done.50, bf16[588,768]{1,0:T(8,128)(2,1)S(1)} %copy-done.51), kind=kOutput, calls=%fused_computation.2 | convolution fusion | flops 4888977408 | bytes 31997952 | tf_op jit(solution)/shard_map/dot_general | solution.py:26
  682.7 181.3 %reduce-scatter.2.cloned.1.call-done = bf16[1,688,768]{2,1,0:T(8,128)(2,1)} async-done(((bf16[16,688,768]{2,1,0:T(8,128)(2,1)}), bf16[1,688,768]{2,1,0:T(8,128)(2,1)}) %reduce-scatter.2.cloned.1.call-update) | async-done | bytes 1056784 | tf_op jit(solution)/shard_map/reduce_scatter | solution.py:449
  865.3 40.3 %all-reduce.5.cloned.1.call-done = bf16[688,768]{1,0:T(8,128)(2,1)} async-done(((bf16[688,768]{1,0:T(8,128)(2,1)}), bf16[688,768]{1,0:T(8,128)(2,1)}) %all-reduce.5.cloned.1.call-update) | async-done | bytes 1056784 | tf_op jit(solution)/shard_map/psum | solution.py:450
  (750 shorter events, 347.2 us)
Async XLA Ops:
  7.2 24.6 %copy-start = (s32[2,96]{1,0:T(2,128)S(1)}, s32[2,96]{1,0:T(2,128)}, u32[]{:S(2)}) copy-start(s32[2,96]{1,0:T(2,128)} %param.32) | copy-start | bytes 2308
  7.2 104.8 %all-gather.3.cloned.1.call-start = ((), (), s32[]{:S(2)}) async-start(), calls=%async_computation.3 | async-start | bytes 17965056 | tf_op jit(solution)/shard_map/all_gather | solution.py:237
  19.5 844.5 %reduce-scatter.2.cloned.1.call-start = ((), (), s32[]{:S(2)}) async-start(), calls=%async_computation.1 | async-start | bytes 17965056 | tf_op jit(solution)/shard_map/reduce_scatter | solution.py:449
  32.4 103.8 %copy-start.187 = (s32[3,196]{1,0:T(4,128)}, s32[3,196]{1,0:T(4,128)S(1)}, u32[]{:S(2)}) copy-start(s32[3,196]{1,0:T(4,128)S(1)} %get-tuple-element.252) | copy-start | bytes 7060
  32.4 112.9 %copy-start.183 = (s32[3,196]{1,0:T(4,128)}, s32[3,196]{1,0:T(4,128)S(1)}, u32[]{:S(2)}) copy-start(s32[3,196]{1,0:T(4,128)S(1)} %get-tuple-element.253) | copy-start | bytes 7060
  32.5 103.8 %copy-start.189 = (f32[3,196]{1,0:T(4,128)}, f32[3,196]{1,0:T(4,128)S(1)}, u32[]{:S(2)}) copy-start(f32[3,196]{1,0:T(4,128)S(1)} %get-tuple-element.250) | copy-start | bytes 7060
  32.5 112.9 %copy-start.185 = (f32[3,196]{1,0:T(4,128)}, f32[3,196]{1,0:T(4,128)S(1)}, u32[]{:S(2)}) copy-start(f32[3,196]{1,0:T(4,128)S(1)} %get-tuple-element.251) | copy-start | bytes 7060
  33.6 102.7 %copy-start.211 = (f32[3,196]{1,0:T(4,128)}, f32[3,196]{1,0:T(4,128)S(1)}, u32[]{:S(2)}) copy-start(f32[3,196]{1,0:T(4,128)S(1)} %convert_add_fusion) | copy-start | bytes 7060
  33.6 111.8 %copy-start.209 = (f32[3,196]{1,0:T(4,128)}, f32[3,196]{1,0:T(4,128)S(1)}, u32[]{:S(2)}) copy-start(f32[3,196]{1,0:T(4,128)S(1)} %convert_add_fusion.1) | copy-start | bytes 7060
  34.3 189.6 %copy-start.196 = (pred[3,196]{1,0:T(4,128)(4,1)}, pred[3,196]{1,0:T(4,128)(4,1)S(1)}, u32[]{:S(2)}) copy-start(pred[3,196]{1,0:T(4,128)(4,1)S(1)} %get-tuple-element.255) | copy-start | bytes 1768
  128.1 21.4 %copy-start.128 = (f32[768]{0:T(1024)}, f32[768]{0:T(1024)S(1)}, u32[]{:S(2)}) copy-start(f32[768]{0:T(1024)S(1)} %mul.881) | copy-start | bytes 9220
  186.8 107.4 %copy-start.97 = (f32[12,64]{1,0:T(8,128)}, f32[12,64]{1,0:T(8,128)S(1)}, u32[]{:S(2)}) copy-start(f32[12,64]{1,0:T(8,128)S(1)} %mul.887) | copy-start | bytes 9220
  264.3 29.9 %copy-start.8 = (f32[3,196,12,64]{1,3,2,0:T(8,128)}, f32[3,196,12,64]{1,3,2,0:T(8,128)S(1)}, u32[]{:S(2)}) copy-start(f32[3,196,12,64]{1,3,2,0:T(8,128)S(1)} %get-tuple-element.166) | copy-start | bytes 5419012
  326.8 29.2 %copy-start.2 = (f32[3,196,768]{2,1,0:T(8,128)}, f32[3,196,768]{2,1,0:T(8,128)S(1)}, u32[]{:S(2)}) copy-start(f32[3,196,768]{2,1,0:T(8,128)S(1)} %get-tuple-element.239) | copy-start | bytes 5419012
  326.8 29.2 %copy-start.120 = (f32[3,196]{1,0:T(4,128)}, f32[3,196]{1,0:T(4,128)S(1)}, u32[]{:S(2)}) copy-start(f32[3,196]{1,0:T(4,128)S(1)} %broadcast_multiply_fusion.4) | copy-start | bytes 7060
  327.3 27.2 %copy-start.141 = (f32[3,196]{1,0:T(4,128)}, f32[3,196]{1,0:T(4,128)S(1)}, u32[]{:S(2)}) copy-start(f32[3,196]{1,0:T(4,128)S(1)} %fusion.189) | copy-start | bytes 7060
  330.0 22.9 %copy-start.124 = (f32[3,768]{1,0:T(4,128)}, f32[3,768]{1,0:T(4,128)S(1)}, u32[]{:S(2)}) copy-start(f32[3,768]{1,0:T(4,128)S(1)} %get-tuple-element.127) | copy-start | bytes 27652
  331.5 1.2 collective-permute-start
  332.8 3.7 collective-permute-start.1
  336.5 3.7 collective-permute-start.2
  340.2 4.6 collective-permute-start.3
  344.9 3.7 collective-permute-start.4
  682.6 181.4 %copy-start.208 = (f32[1,96]{1,0:T(1,128)S(1)}, f32[1,96]{1,0:T(1,128)}, u32[]{:S(2)}) copy-start(f32[1,96]{1,0:T(1,128)} %copy-done.207) | copy-start | bytes 1156
  682.6 181.4 %copy-start.215 = (f32[2]{0:T(128)S(1)}, f32[2]{0:T(128)}, u32[]{:S(2)}) copy-start(f32[2]{0:T(128)} %get-tuple-element.148) | copy-start | bytes 28
  682.6 223.0 %all-reduce.5.cloned.1.call-start = ((), (), s32[]{:S(2)}) async-start(), calls=%async_computation.2 | async-start | bytes 2113536 | tf_op jit(solution)/shard_map/psum | solution.py:450
  908.9 1.4 collective-permute-start.5
  909.3 22.0 %copy-start.110 = (f32[196,48]{0,1:T(8,128)S(1)}, f32[196,48]{0,1:T(8,128)}, u32[]{:S(2)}) copy-start(f32[196,48]{0,1:T(8,128)} %param.34) | copy-start | bytes 112900
  909.3 22.0 %copy-start.150 = (f32[196,48]{0,1:T(8,128)S(1)}, f32[196,48]{0,1:T(8,128)}, u32[]{:S(2)}) copy-start(f32[196,48]{0,1:T(8,128)} %param.48) | copy-start | bytes 112900
  909.3 22.0 %copy-start.151 = (f32[196,48]{0,1:T(8,128)S(1)}, f32[196,48]{0,1:T(8,128)}, u32[]{:S(2)}) copy-start(f32[196,48]{0,1:T(8,128)} %param.41) | copy-start | bytes 112900
  911.5 3.6 collective-permute-start.6
  915.8 3.6 collective-permute-start.7
  920.0 4.5 collective-permute-start.8
  (209 other events, 1222.3 us)
Sparse Core Ops, SparseCore 0:
  19.6 92.3 all-gather.2
  682.8 181.1 reduce-scatter.1
  866.4 39.1 all-reduce.4

commit v2 on v1

--- a/solution.py
+++ b/solution.py
@@ -1,12 +1,15 @@
+import functools
+
 import jax
 import jax.numpy as jnp
 from jax import lax
+from jax.experimental import pallas as pl
+from jax.experimental.pallas import tpu as pltpu
 from jax.sharding import PartitionSpec as P
 
 HEADS = 12
 
 
-highest = lax.Precision.HIGHEST
 norm_eps = 1e-06
 clip_bound = 0.1
 beta_first = 0.9
@@ -32,35 +35,6 @@
     return lax.dot_general(
         left, right, (((1,), (1,)), ((), ())), preferred_element_type=jnp.float32
     )
-
-
-def layer_norm(values, gain_row):
-    center = values - jnp.mean(values, axis=-1, keepdims=True)
-    spread = jnp.mean(center * center, axis=-1, keepdims=True)
-    return center * lax.rsqrt(spread + norm_eps) * gain_row
-
-
-def head_norm(values, gain_row):
-    return layer_norm(values, gain_row.reshape(values.shape[-2], values.shape[-1]))
-
-
-def gelu_exact(values):
-    return 0.5 * values * (1.0 + lax.erf(values * 0.7071067811865476))
-
-
-def merge_matrix(slot_map, slot_weight, live_count):
-    slot_total = slot_map.shape[-1]
-    slot_ids = jnp.arange(slot_total, dtype=jnp.int32)
-    member = (slot_map[:, None, :] == slot_ids[None, :, None]).astype(jnp.float32) * slot_weight[
-        :, None, :
-    ]
-    vacant = (slot_ids[None, :] >= live_count[:, None]).astype(jnp.float32)
-    return member / (jnp.sum(member, axis=-1) + vacant)[:, :, None]
-
-
-def pool_final(stream, gain_row, live_mask, count_float):
-    final_rows = layer_norm(stream, gain_row)
-    return jnp.sum(final_rows * live_mask[:, :, None], axis=1) / count_float[:, None]
 
 
 def adam_step(weight, gradient, moment, square, factor):
@@ -199,6 +173,326 @@
     at += s_rows * s_cols
     bias = small[at : at + b_len]
     return embed, place, wide, narrow, project, scale, bias
+
+
+def padded_rows(rows):
+    return -(-rows // 16) * 16
+
+
+def split_two(values):
+    high = values.astype(jnp.bfloat16)
+    return high, (values - high.astype(jnp.float32)).astype(jnp.bfloat16)
+
+
+def normal_rows(values):
+    center = values - jnp.mean(values, axis=-1, keepdims=True)
+    rstd = lax.rsqrt(jnp.mean(center * center, axis=-1, keepdims=True) + norm_eps)
+    return center * rstd, rstd
+
+
+def head_mixer(head_size):
+    row = lax.broadcasted_iota(jnp.int32, (256, 256), 0) // head_size
+    column = lax.broadcasted_iota(jnp.int32, (256, 256), 1) // head_size
+    return jnp.where(row == column, 1.0 / head_size, 0.0).astype(jnp.bfloat16)
+
+
+def head_mean(values, mixer):
+    parts = []
+    for at in range(0, values.shape[1], 256):
+        high, low = split_two(values[:, at : at + 256])
+        parts.append(product(high, mixer) + product(low, mixer))
+    return jnp.concatenate(parts, axis=1)
+
+
+def embed_kernel(
+    counts_ref, pixel_ref, map_ref, row_ref, column_ref, embed_ref, place_ref, gain_ref,
+    merged_ref, normed_ref,
+):
+    live_count = counts_ref[pl.program_id(0)]
+    slots = merged_ref.shape[1]
+    patches = product(pixel_ref[0], embed_ref[...]) + place_ref[...]
+    high, low = split_two(patches * column_ref[0])
+    slot = lax.broadcasted_iota(jnp.int32, (slots, slots), 0)
+    member = slot == map_ref[0]
+    hot = jnp.where(member, 1.0, 0.0).astype(jnp.bfloat16)
+    total = jnp.sum(jnp.where(member, row_ref[0], 0.0), axis=1, keepdims=True)
+    vacant = lax.broadcasted_iota(jnp.int32, (slots, 1), 0) >= live_count
+    total = total + jnp.where(vacant, 1.0, 0.0)
+    merged = (product(hot, high) + product(hot, low)) / total
+    merged_ref[0] = merged
+    unit, _ = normal_rows(merged)
+    normed_ref[0] = (unit * gain_ref[...]).astype(jnp.bfloat16)
+
+
+def gelu_pair(values):
+    size = jnp.abs(values)
+    turn = 1.0 / (1.0 + (0.3275911 * 0.7071067811865476) * size)
+    bell = jnp.exp(-0.5 * values * values)
+    poly = turn * (
+        0.5 * 0.254829592
+        + turn
+        * (
+            0.5 * -0.284496736
+            + turn
+            * (0.5 * 1.421413741 + turn * (0.5 * -1.453152027 + turn * (0.5 * 1.061405429)))
+        )
+    )
+    tail = poly * bell
+    share = jnp.where(values >= 0, 1.0 - tail, tail)
+    return values * share, share + values * (bell * 0.3989422804014327)
+
+
+def widen_kernel(
+    normed_ref, wide_ref, gain_ref, bias_ref, qkv_ref, rstd_ref, hidden_ref, slope_ref, *, chunk,
+    head_size,
+):
+    step = pl.program_id(0)
+    chunks = normed_ref.shape[0] // chunk
+
+    def rows_of(index):
+        return pl.ds(pl.multiple_of(index * chunk, chunk), chunk)
+
+    @pl.when(step < 2)
+    def _():
+        mixer = head_mixer(head_size)
+        gain = gain_ref[0]
+
+        @pl.loop(0, chunks)
+        def _(index):
+            rows = rows_of(index)
+            values = product(normed_ref[rows, :], wide_ref[0])
+            center = values - head_mean(values, mixer)
+            rstd = lax.rsqrt(head_mean(center * center, mixer) + norm_eps)
+            rstd_ref[0, rows, :] = rstd
+            qkv_ref[0, rows, :] = (center * rstd * gain).astype(jnp.bfloat16)
+
+    @pl.when(step == 2)
+    def _():
+        @pl.loop(0, chunks)
+        def _(index):
+            rows = rows_of(index)
+            qkv_ref[0, rows, :] = product(normed_ref[rows, :], wide_ref[0]).astype(jnp.bfloat16)
+
+    @pl.when(step > 2)
+    def _():
+        @pl.loop(0, chunks)
+        def _(index):
+            rows = rows_of(index)
+            values = product(normed_ref[rows, :], wide_ref[0]) + bias_ref[0]
+            hidden, slope = gelu_pair(values)
+            hidden_ref[0, rows, :] = hidden.astype(jnp.bfloat16)
+            slope_ref[0, rows, :] = slope.astype(jnp.bfloat16)
+
+
+def attend_kernel(
+    counts_ref, qkv_ref, hidden_ref, merged_ref, narrow_hbm, bias_ref, gain_ref,
+    attended_ref, stream_ref, pooled_ref, narrow_ref, sem, *, head_size,
+):
+    image = pl.program_id(0)
+    live_count = counts_ref[image]
+    slots, width = merged_ref.shape[1:]
+    copy = pltpu.make_async_copy(narrow_hbm, narrow_ref, sem)
+
+    @pl.when(image == 0)
+    def _():
+        copy.start()
+
+    factor = head_size ** (-0.5) * 1.4426950408889634
+    key_live = jnp.where(
+        lax.broadcasted_iota(jnp.int32, (1, slots), 1) < live_count, 1.0, 0.0
+    )
+    first_half = lax.broadcasted_iota(jnp.int32, (slots, 2 * head_size), 1) < head_size
+    zero = jnp.zeros((slots, 2 * head_size), jnp.bfloat16)
+    for at in range(0, width, 2 * head_size):
+        columns = slice(at, at + 2 * head_size)
+        queries, keys, values = (qkv_ref[part, :, columns] for part in range(3))
+        outs = []
+        for half in range(2):
+            own = jnp.where(first_half, queries, zero) if half == 0 else jnp.where(first_half, zero, queries)
+            weights = jnp.exp2(product_along(own, keys) * factor) * key_live
+            share = weights * (1.0 / jnp.sum(weights, axis=1, keepdims=True))
+            outs.append(product(share.astype(jnp.bfloat16), values))
+        attended_ref[0, :, columns] = jnp.where(first_half, outs[0], outs[1]).astype(jnp.bfloat16)
+
+    @pl.when(image == 0)
+    def _():
+        copy.wait()
+
+    stream = merged_ref[0] + bias_ref[...] + product(attended_ref[0], narrow_ref[:width, :])
+    for part in range(hidden_ref.shape[0]):
+        stream = stream + product(
+            hidden_ref[part], narrow_ref[(part + 1) * width : (part + 2) * width, :]
+        )
+    stream_ref[0] = stream
+    unit, _ = normal_rows(stream)
+    live = lax.broadcasted_iota(jnp.int32, (slots, 1), 0) < live_count
+    total = jnp.sum(jnp.where(live, unit, 0.0), axis=0, keepdims=True)
+    pooled_ref[0] = total * gain_ref[...] / live_count.astype(jnp.float32)
+
+
+def branch_kernel(
+    counts_ref, stream_ref, grad_pooled_ref, gain_ref, slope_ref, narrow_hbm,
+    grad_stream_ref, grad_branch_ref, grad_attended_ref, grad_act_ref, sums_ref, narrow_ref, sem,
+):
+    image = pl.program_id(0)
+    live_count = counts_ref[image]
+    slots, width = stream_ref.shape[1:]
+    copy = pltpu.make_async_copy(narrow_hbm, narrow_ref, sem)
+
+    @pl.when(image == 0)
+    def _():
+        copy.start()
+        sums_ref[...] = jnp.zeros_like(sums_ref)
+
+    unit, rstd = normal_rows(stream_ref[0])
+    live = lax.broadcasted_iota(jnp.int32, (slots, 1), 0) < live_count
+    above = grad_pooled_ref[0] / live_count.astype(jnp.float32)
+    slanted = above * gain_ref[...]
+    mean_first = jnp.mean(slanted, axis=-1, keepdims=True)
+    mean_second = jnp.mean(slanted * unit, axis=-1, keepdims=True)
+    grad_stream = jnp.where(live, rstd * (slanted - mean_first - unit * mean_second), 0.0)
+    grad_stream_ref[0] = grad_stream
+    grad_branch = grad_stream.astype(jnp.bfloat16)
+    grad_branch_ref[0] = grad_branch
+    parts = slope_ref.shape[0]
+    sums_ref[parts : parts + 1, :] += jnp.sum(grad_stream, axis=0, keepdims=True)
+    sums_ref[parts + 1 : parts + 2, :] += above * jnp.sum(
+        jnp.where(live, unit, 0.0), axis=0, keepdims=True
+    )
+
+    @pl.when(image == 0)
+    def _():
+        copy.wait()
+
+    grad_attended_ref[0] = product_along(grad_branch, narrow_ref[:width, :]).astype(jnp.bfloat16)
+    for part in range(parts):
+        grad_act = product_along(
+            grad_branch, narrow_ref[(part + 1) * width : (part + 2) * width, :]
+        ) * slope_ref[part].astype(jnp.float32)
+        grad_act_ref[part] = grad_act.astype(jnp.bfloat16)
+        sums_ref[part : part + 1, :] += jnp.sum(grad_act, axis=0, keepdims=True)
+
+
+def attend_back_kernel(
+    counts_ref, qkv_ref, rstd_ref, grad_attended_ref, gain_ref, grad_qkv_ref, sums_ref,
+    grad_ref, *, head_size,
+):
+    image = pl.program_id(0)
+    live_count = counts_ref[image]
+    slots, width = grad_attended_ref.shape[1:]
+
+    @pl.when(image == 0)
+    def _():
+        sums_ref[...] = jnp.zeros_like(sums_ref)
+
+    factor = head_size ** (-0.5)
+    key_live = lax.broadcasted_iota(jnp.int32, (slots, 1), 0) < live_count
+    first_half = lax.broadcasted_iota(jnp.int32, (slots, 2 * head_size), 1) < head_size
+    zero = jnp.zeros((slots, 2 * head_size), jnp.bfloat16)
+    for at in range(0, width, 2 * head_size):
+        columns = slice(at, at + 2 * head_size)
+        queries, keys, values = (qkv_ref[part, :, columns] for part in range(3))
+        above = grad_attended_ref[0, :, columns]
+        grad_queries, grad_keys, grad_values = [], [], []
+        for half in range(2):
+            pick = lambda both: jnp.where(first_half, both, zero) if half == 0 else jnp.where(first_half, zero, both)
+            own_queries, own_above = pick(queries), pick(above)
+            weights = jnp.exp2(product_along(keys, own_queries) * (factor * 1.4426950408889634))
+            weights = jnp.where(key_live, weights, 0.0)
+            share = weights * (1.0 / jnp.sum(weights, axis=0, keepdims=True))
+            grad_share = product_along(values, own_above)
+            dot_row = jnp.sum(share * grad_share, axis=0, keepdims=True)
+            grad_raw = (share * (grad_share - dot_row) * factor).astype(jnp.bfloat16)
+            grad_values.append(product(share.astype(jnp.bfloat16), own_above))
+            grad_keys.append(product(grad_raw, own_queries))
+            grad_queries.append(product_across(grad_raw, keys))
+        grad_qkv_ref[2, :, columns] = (grad_values[0] + grad_values[1]).astype(jnp.bfloat16)
+        grad_ref[1, :, columns] = grad_keys[0] + grad_keys[1]
+        grad_ref[0, :, columns] = jnp.where(first_half, grad_queries[0], grad_queries[1])
+    mixer = head_mixer(head_size)
+    for part in range(2):
+        gain = gain_ref[part]
+        above = grad_ref[part]
+        unit = qkv_ref[part].astype(jnp.float32) / gain
+        sums_ref[part : part + 1, :] += jnp.sum(above * unit, axis=0, keepdims=True)
+        slanted = above * gain
+        back = slanted - head_mean(slanted, mixer) - unit * head_mean(slanted * unit, mixer)
+        grad_qkv_ref[part] = (rstd_ref[part] * back).astype(jnp.bfloat16)
+
+
+def merge_back_kernel(
+    counts_ref, grad_qkv_ref, grad_act_ref, wide_hbm, merged_ref, grad_stream_ref, gain_ref,
+    map_ref, row_ref, column_ref, grad_patch_ref, grad_place_ref, sums_ref, wide_ref, sem,
+):
+    image = pl.program_id(0)
+    live_count = counts_ref[image]
+    slots, width = merged_ref.shape[1:]
+    copy = pltpu.make_async_copy(wide_hbm, wide_ref, sem)
+
+    @pl.when(image == 0)
+    def _():
+        copy.start()
+        sums_ref[...] = jnp.zeros_like(sums_ref)
+        grad_place_ref[...] = jnp.zeros_like(grad_place_ref)
+        copy.wait()
+
+    grad_normed = jnp.zeros((slots, width), jnp.float32)
+    for part in range(3):
+        grad_normed = grad_normed + product_along(grad_qkv_ref[part], wide_ref[part])
+    for part in range(grad_act_ref.shape[0]):
+        grad_normed = grad_normed + product_along(grad_act_ref[part], wide_ref[3 + part])
+    unit, rstd = normal_rows(merged_ref[0])
+    sums_ref[0:1, :] += jnp.sum(grad_normed * unit, axis=0, keepdims=True)
+    slanted = grad_normed * gain_ref[...]
+    back = (
+        slanted
+        - jnp.mean(slanted, axis=-1, keepdims=True)
+        - unit * jnp.mean(slanted * unit, axis=-1, keepdims=True)
+    )
+    grad_merged = grad_stream_ref[0] + rstd * back
+    slot = lax.broadcasted_iota(jnp.int32, (slots, slots), 0)
+    member = slot == map_ref[0]
+    hot = jnp.where(member, 1.0, 0.0).astype(jnp.bfloat16)
+    total = jnp.sum(jnp.where(member, row_ref[0], 0.0), axis=1, keepdims=True)
+    vacant = lax.broadcasted_iota(jnp.int32, (slots, 1), 0) >= live_count
+    total = total + jnp.where(vacant, 1.0, 0.0)
+    high, low = split_two(grad_merged / total)
+    grad_patches = (product_across(hot, high) + product_across(hot, low)) * column_ref[0]
+    grad_patch_ref[0] = grad_patches.astype(jnp.bfloat16)
+    grad_place_ref[...] += grad_patches
+    sums_ref[1:2, :] += jnp.sum(grad_patches, axis=0, keepdims=True)
+
+
+def block(shape, index_map):
+    return pl.BlockSpec(shape, index_map)
+
+
+def per_image(rows, width):
+    return block((1, rows, width), lambda image, counts: (image, 0, 0))
+
+
+def whole(*shape):
+    return block(shape, lambda *_: (0,) * len(shape))
+
+
+anywhere = pl.BlockSpec(memory_space=pl.ANY)
+roomy = pltpu.CompilerParams(vmem_limit_bytes=60 * 1024 * 1024)
+
+
+def image_call(kernel, images, in_specs, out_specs, out_shape, scratch=(), name=None):
+    return pl.pallas_call(
+        kernel,
+        grid_spec=pltpu.PrefetchScalarGridSpec(
+            num_scalar_prefetch=1,
+            grid=(images,),
+            in_specs=in_specs,
+            out_specs=out_specs,
+            scratch_shapes=list(scratch),
+        ),
+        out_shape=out_shape,
+        compiler_params=roomy,
+        name=name,
+    )
 
 
 def per_device(
@@ -238,98 +532,116 @@
     embed_full, place_full, wide_blocks, narrow_full, project_full, scale_full, bias_full = (
         unpack_weights(full, shapes)
     )
-    wide_full = jnp.concatenate(wide_blocks, axis=1)
     place_float = place_full.astype(jnp.float32)
     scale_float = scale_full.astype(jnp.float32)
     bias_float = bias_full.astype(jnp.float32)
     micro_count, images_dev, slot_total, patch_size = pixels.shape
     model_width = embed_full.shape[1]
     hidden_width = narrow_full.shape[0] - model_width
-    head_count = HEADS
-    head_size = model_width // head_count
+    hidden_blocks = hidden_width // model_width
+    head_size = model_width // HEADS
     images_all = pairing.shape[1]
-    embed_width = captions.shape[2]
-    logit_factor = logit_temper * embed_width ** (-0.5)
-    attend_factor = head_size ** (-0.5)
-    row_count = images_dev * slot_total
-    grad_embed = jnp.zeros(embed_full.shape, jnp.float32)
-    grad_place = jnp.zeros(place_full.shape, jnp.float32)
-    grad_wide = jnp.zeros(wide_full.shape, jnp.float32)
-    grad_narrow = jnp.zeros(narrow_full.shape, jnp.float32)
-    grad_project = jnp.zeros(project_full.shape, jnp.float32)
-    grad_scale = jnp.zeros(scale_full.shape, jnp.float32)
-    grad_bias = jnp.zeros(bias_full.shape, jnp.float32)
+    logit_factor = logit_temper * captions.shape[2] ** (-0.5)
+    images = micro_count * images_dev
+    slots = padded_rows(slot_total)
+    spare = slots - slot_total
+    rows = images * slots
+    pixel_rows = jnp.pad(
+        pixels.reshape(images, slot_total, patch_size), ((0, 0), (0, spare), (0, 0))
+    )
+    slot_map = jnp.pad(
+        merge_map.reshape(images, 1, slot_total), ((0, 0), (0, 0), (0, spare)), constant_values=-1
+    )
+    row_weight = jnp.pad(merge_weight.reshape(images, 1, slot_total), ((0, 0), (0, 0), (0, spare)))
+    column_weight = row_weight.reshape(images, slots, 1)
+    live_counts = counts.reshape(images)
+    place_bias = jnp.pad(
+        place_float + bias_float[hidden_width + model_width :], ((0, spare), (0, 0))
+    )
+    out_bias = bias_float[hidden_width : hidden_width + model_width].reshape(1, model_width)
+    wide_stack = jnp.stack(wide_blocks)
+    f32, low = jnp.float32, jnp.bfloat16
+    shape = jax.ShapeDtypeStruct
+    merged, normed = image_call(
+        embed_kernel,
+        images,
+        [
+            per_image(slots, patch_size),
+            per_image(1, slots),
+            per_image(1, slots),
+            per_image(slots, 1),
+            whole(patch_size, model_width),
+            whole(slots, model_width),
+            whole(1, model_width),
+        ],
+        [per_image(slots, model_width)] * 2,
+        [shape((images, slots, model_width), f32), shape((images, slots, model_width), low)],
+        name="embed",
+    )(
+        live_counts, pixel_rows, slot_map, row_weight, column_weight, embed_full, place_bias,
+        scale_float[0:1],
+    )
+    normed_rows = normed.reshape(rows, model_width)
+    column_block = lambda index_map: block((1, rows, model_width), index_map)
+    qkv, rstd, hidden, slope = pl.pallas_call(
+        functools.partial(widen_kernel, chunk=slots, head_size=head_size),
+        grid=(3 + hidden_blocks,),
+        in_specs=[
+            whole(rows, model_width),
+            block((1, model_width, model_width), lambda k: (k, 0, 0)),
+            block((1, 1, model_width), lambda k: (jnp.minimum(k, 1), 0, 0)),
+            block((1, 1, model_width), lambda k: (jnp.maximum(k - 3, 0), 0, 0)),
+        ],
+        out_specs=[
+            column_block(lambda k: (jnp.minimum(k, 2), 0, 0)),
+            column_block(lambda k: (jnp.minimum(k, 1), 0, 0)),
+            column_block(lambda k: (jnp.maximum(k - 3, 0), 0, 0)),
+            column_block(lambda k: (jnp.maximum(k - 3, 0), 0, 0)),
+        ],
+        out_shape=[
+            shape((3, rows, model_width), low),
+            shape((2, rows, model_width), f32),
+            shape((hidden_blocks, rows, model_width), low),
+            shape((hidden_blocks, rows, model_width), low),
+        ],
+        compiler_params=roomy,
+        name="widen",
+    )(
+        normed_rows, wide_stack, scale_float[2:4].reshape(2, 1, model_width),
+        bias_float[:hidden_width].reshape(hidden_blocks, 1, model_width),
+    )
+    image_columns = lambda parts: block(
+        (parts, slots, model_width), lambda image, counts: (0, image, 0)
+    )
+    narrow_scratch = [
+        pltpu.VMEM((hidden_width + model_width, model_width), low), pltpu.SemaphoreType.DMA
+    ]
+    attended, stream, pooled = image_call(
+        functools.partial(attend_kernel, head_size=head_size),
+        images,
+        [
+            image_columns(3),
+            image_columns(hidden_blocks),
+            per_image(slots, model_width),
+            anywhere,
+            whole(1, model_width),
+            whole(1, model_width),
+        ],
+        [per_image(slots, model_width), per_image(slots, model_width), per_image(1, model_width)],
+        [
+            shape((images, slots, model_width), low),
+            shape((images, slots, model_width), f32),
+            shape((images, 1, model_width), f32),
+        ],
+        narrow_scratch,
+        name="attend",
+    )(live_counts, qkv, hidden, merged, narrow_full, out_bias, scale_float[1:2])
+    pooled_low = pooled.reshape(images, model_width).astype(low)
+    embeds = product(pooled_low, project_full).astype(low)
+    embeds = embeds.reshape(micro_count, images_dev, -1)
+    logits = jnp.einsum("mie,mje->mij", embeds, captions, preferred_element_type=f32) * logit_factor
     image_ids = jnp.arange(images_all, dtype=jnp.int32)
-    kept = []
-    for step_index in range(micro_count):
-        pixel_rows = pixels[step_index].reshape(row_count, patch_size)
-        live_count = counts[step_index]
-        count_float = live_count.astype(jnp.float32)
-        live_mask = (jnp.arange(slot_total, dtype=jnp.int32)[None, :] < live_count[:, None]).astype(
-            jnp.float32
-        )
-        key_live = live_mask[:, None, None, :] > 0
-        merger = merge_matrix(merge_map[step_index], merge_weight[step_index], live_count)
-        patches = product(pixel_rows, embed_full).reshape(images_dev, slot_total, model_width)
-        patches = patches + bias_float[hidden_width + model_width :] + place_float
-        merged = jnp.einsum("isp,ipd->isd", merger, patches, precision=highest)
-        normed, normed_back = jax.vjp(layer_norm, merged, scale_float[0])
-        normed_low = normed.astype(jnp.bfloat16).reshape(row_count, model_width)
-        widened = product(normed_low, wide_full)
-        query_pre = widened[:, :model_width].reshape(images_dev, slot_total, head_count, head_size)
-        key_pre = widened[:, model_width : 2 * model_width].reshape(
-            images_dev, slot_total, head_count, head_size
-        )
-        queries, query_back = jax.vjp(head_norm, query_pre, scale_float[2])
-        key_rows, key_back = jax.vjp(head_norm, key_pre, scale_float[3])
-        query_low = queries.astype(jnp.bfloat16)
-        key_low = key_rows.astype(jnp.bfloat16)
-        value_low = (
-            widened[:, 2 * model_width : 3 * model_width]
-            .reshape(images_dev, slot_total, head_count, head_size)
-            .astype(jnp.bfloat16)
-        )
-        scores = (
-            jnp.einsum("ishd,ithd->ihst", query_low, key_low, preferred_element_type=jnp.float32)
-            * attend_factor
-        )
-        scores = jnp.where(key_live, scores, -1e30)
-        score_top = jnp.max(scores, axis=-1, keepdims=True)
-        log_total = score_top + jnp.log(
-            jnp.sum(jnp.exp(scores - score_top), axis=-1, keepdims=True)
-        )
-        softmax = jnp.exp(scores - log_total)
-        attended = jnp.einsum(
-            "ihst,ithd->ishd",
-            softmax.astype(jnp.bfloat16),
-            value_low,
-            preferred_element_type=jnp.float32,
-        )
-        attended = attended.reshape(row_count, model_width).astype(jnp.bfloat16)
-        hidden, gelu_back = jax.vjp(
-            gelu_exact, widened[:, 3 * model_width :] + bias_float[:hidden_width]
-        )
-        joined = jnp.concatenate([attended, hidden.astype(jnp.bfloat16)], axis=1)
-        stream = (
-            merged
-            + product(joined, narrow_full).reshape(images_dev, slot_total, model_width)
-            + bias_float[hidden_width : hidden_width + model_width]
-        )
-        pooled, pool_back = jax.vjp(
-            lambda values, gain_row: pool_final(values, gain_row, live_mask, count_float),
-            stream,
-            scale_float[1],
-        )
-        pooled_low = pooled.astype(jnp.bfloat16)
-        embeds = product(pooled_low, project_full).astype(jnp.bfloat16)
-        kept.append((pixel_rows, live_mask, count_float, key_live, merger, merged, normed_back, normed_low, query_low, key_low, value_low, query_back, key_back, log_total, joined, gelu_back, pool_back, pooled_low, embeds))
-    all_embeds = jnp.concatenate([item[-1] for item in kept], axis=0)
-    all_logits = [
-        product_along(kept[index][-1], captions[index]) * logit_factor
-        for index in range(micro_count)
-    ]
     first_row = (lax.axis_index("rep") * owners + lax.axis_index("fsdp")) * images_dev
-    logits = jnp.stack(all_logits)
     own_pairs = lax.dynamic_slice_in_dim(pairing, first_row, images_dev, 1)
     target = (own_pairs[:, :, None] == image_ids[None, None, :]).astype(jnp.float32)
     row_top = jnp.max(logits, axis=2, keepdims=True)
@@ -366,83 +678,99 @@
             + (column_soft - target) / images_all
         )
     )
-    for step_index in range(micro_count):
-        (pixel_rows, live_mask, count_float, key_live, merger, merged, normed_back, normed_low, query_low, key_low, value_low, query_back, key_back, log_total, joined, gelu_back, pool_back, pooled_low, embeds) = kept[step_index]
-        grad_logits = all_grad_logits[step_index]
-        caption_rows = captions[step_index]
-        grad_product = (grad_logits * logit_factor).astype(jnp.bfloat16)
-        grad_embeds = product(grad_product, caption_rows).astype(jnp.bfloat16)
-        grad_project = grad_project + product_across(pooled_low, grad_embeds)
-        grad_pooled = product_along(grad_embeds, project_full)
-        grad_stream, grad_final_scale = pool_back(grad_pooled)
-        grad_branch = grad_stream.reshape(row_count, model_width).astype(jnp.bfloat16)
-        grad_narrow = grad_narrow + product_across(joined, grad_branch)
-        grad_joined = product_along(grad_branch, narrow_full)
-        grad_attended = (
-            grad_joined[:, :model_width]
-            .astype(jnp.bfloat16)
-            .reshape(images_dev, slot_total, head_count, head_size)
-        )
-        (grad_act,) = gelu_back(grad_joined[:, model_width:])
-        again = (
-            jnp.einsum("ishd,ithd->ihst", query_low, key_low, preferred_element_type=jnp.float32)
-            * attend_factor
-        )
-        again = jnp.where(key_live, again, -1e30)
-        softmax_again = jnp.exp(again - log_total)
-        grad_probs = jnp.einsum(
-            "ishd,ithd->ihst", grad_attended, value_low, preferred_element_type=jnp.float32
-        )
-        row_dot = jnp.sum(softmax_again * grad_probs, axis=-1, keepdims=True)
-        grad_scores = (softmax_again * (grad_probs - row_dot) * attend_factor).astype(jnp.bfloat16)
-        grad_values = jnp.einsum(
-            "ihst,ishd->ithd",
-            softmax_again.astype(jnp.bfloat16),
-            grad_attended,
-            preferred_element_type=jnp.float32,
-        )
-        grad_queries = jnp.einsum(
-            "ihst,ithd->ishd", grad_scores, key_low, preferred_element_type=jnp.float32
-        )
-        grad_keys = jnp.einsum(
-            "ihst,ishd->ithd", grad_scores, query_low, preferred_element_type=jnp.float32
-        )
-        grad_query_pre, grad_query_scale = query_back(grad_queries)
-        grad_key_pre, grad_key_scale = key_back(grad_keys)
-        grad_widened = jnp.concatenate(
-            [
-                grad_query_pre.reshape(row_count, model_width),
-                grad_key_pre.reshape(row_count, model_width),
-                grad_values.reshape(row_count, model_width),
-                grad_act,
-            ],
-            axis=1,
-        ).astype(jnp.bfloat16)
-        grad_wide = grad_wide + product_across(normed_low, grad_widened)
-        grad_normed = product_along(grad_widened, wide_full).reshape(
-            images_dev, slot_total, model_width
-        )
-        grad_merged_norm, grad_first_scale = normed_back(grad_normed)
-        grad_merged = grad_stream + grad_merged_norm
-        grad_patches = jnp.einsum("isp,isd->ipd", merger, grad_merged, precision=highest)
-        grad_place = grad_place + jnp.sum(grad_patches, axis=0)
-        grad_embed = grad_embed + product_across(
-            pixel_rows, grad_patches.reshape(row_count, model_width).astype(jnp.bfloat16)
-        )
-        grad_scale = grad_scale + jnp.stack(
-            [grad_first_scale, grad_final_scale, grad_query_scale, grad_key_scale]
-        )
-        grad_bias = grad_bias + jnp.concatenate(
-            [
-                jnp.sum(grad_act, axis=0),
-                jnp.sum(grad_stream, axis=(0, 1)),
-                jnp.sum(grad_patches, axis=(0, 1)),
-            ]
-        )
-    wide_parts = [
-        grad_wide[:, k * model_width : (k + 1) * model_width]
-        for k in range(grad_wide.shape[1] // model_width)
-    ]
+    grad_product = (all_grad_logits * logit_factor).astype(low)
+    grad_embeds = (
+        jnp.einsum("mij,mje->mie", grad_product, captions, preferred_element_type=f32)
+        .astype(low)
+        .reshape(images, -1)
+    )
+    grad_project = product_across(pooled_low, grad_embeds)
+    grad_pooled = product_along(grad_embeds, project_full)
+    grad_stream, grad_branch, grad_attended, grad_act, out_sums = image_call(
+        branch_kernel,
+        images,
+        [
+            per_image(slots, model_width),
+            per_image(1, model_width),
+            whole(1, model_width),
+            image_columns(hidden_blocks),
+            anywhere,
+        ],
+        [
+            per_image(slots, model_width),
+            per_image(slots, model_width),
+            per_image(slots, model_width),
+            image_columns(hidden_blocks),
+            whole(8, model_width),
+        ],
+        [
+            shape((images, slots, model_width), f32),
+            shape((images, slots, model_width), low),
+            shape((images, slots, model_width), low),
+            shape((hidden_blocks, rows, model_width), low),
+            shape((8, model_width), f32),
+        ],
+        narrow_scratch,
+        name="branch",
+    )(
+        live_counts, stream, grad_pooled.reshape(images, 1, model_width), scale_float[1:2], slope,
+        narrow_full,
+    )
+    across = lambda left, right: product_across(left, right).astype(low)
+    branch_rows = grad_branch.reshape(rows, model_width)
+    grad_narrow = jnp.concatenate(
+        [across(attended.reshape(rows, model_width), branch_rows)]
+        + [across(hidden[k], branch_rows) for k in range(hidden_blocks)],
+        axis=0,
+    )
+    wide_hidden = [across(normed_rows, grad_act[k]) for k in range(hidden_blocks)]
+    grad_qkv, head_sums = image_call(
+        functools.partial(attend_back_kernel, head_size=head_size),
+        images,
+        [
+            image_columns(3),
+            image_columns(2),
+            per_image(slots, model_width),
+            whole(2, 1, model_width),
+        ],
+        [image_columns(3), whole(8, model_width)],
+        [shape((3, rows, model_width), low), shape((8, model_width), f32)],
+        [pltpu.VMEM((2, slots, model_width), f32)],
+        name="attend_back",
+    )(live_counts, qkv, rstd, grad_attended, scale_float[2:4].reshape(2, 1, model_width))
+    wide_parts = [across(normed_rows, grad_qkv[k]) for k in range(3)] + wide_hidden
+    grad_patches, grad_place, merge_sums = image_call(
+        merge_back_kernel,
+        images,
+        [
+            image_columns(3),
+            image_columns(hidden_blocks),
+            anywhere,
+            per_image(slots, model_width),
+            per_image(slots, model_width),
+            whole(1, model_width),
+            per_image(1, slots),
+            per_image(1, slots),
+            per_image(slots, 1),
+        ],
+        [per_image(slots, model_width), whole(slots, model_width), whole(8, model_width)],
+        [
+            shape((images, slots, model_width), low),
+            shape((slots, model_width), f32),
+            shape((8, model_width), f32),
+        ],
+        [pltpu.VMEM((3 + hidden_blocks, model_width, model_width), low), pltpu.SemaphoreType.DMA],
+        name="merge_back",
+    )(
+        live_counts, grad_qkv, grad_act, wide_stack, merged, grad_stream, scale_float[0:1],
+        slot_map, row_weight, column_weight,
+    )
+    grad_embed = across(
+        pixel_rows.reshape(rows, patch_size), grad_patches.reshape(rows, model_width)
+    )
+    grad_place = grad_place[:slot_total]
+    grad_scale = jnp.stack([merge_sums[0], out_sums[hidden_blocks + 1], head_sums[0], head_sums[1]])
+    grad_bias = jnp.concatenate([out_sums[: hidden_blocks + 1].reshape(-1), merge_sums[1]])
     packed_grads = pack_grads(
         owners, grad_embed, grad_place, wide_parts, grad_narrow, grad_project, grad_scale, grad_bias
     )

time: 953 us -> 674 us (0.71)
  matrix products: 250 us -> 42.6 us
  Pallas kernels: 0 us -> 175 us
  local copies, waits for them, and re-layouts: 225 us -> 67.6 us
  other arithmetic: 117 us -> 20.9 us
    pallas_call x0 -> x6, Pallas kernels: none -> 175 us  [the longest x1 39 us: per_device(): pl.pallas_call(functools.partial(widen_kernel, chunk=slots, head_size=hea...]
    dot_general x16 -> x2, matrix products: 118 us -> 0.49 us  [the longest x1 0.28 us: per_device(): jnp.einsum('mie,mje->mij', embeds, captions, preferred_element_type=f32)]
    reshape x26 -> x11, local copies, waits for them, and re-layouts: 76.3 us -> 4.29 us  [the longest x2 1.7 us: per_device(): column_weight = row_weight.reshape(images, slots, 1)]
    reduce_sum x27 -> x1, other arithmetic: 59.3 us -> 0.17 us  [per_device(): own_total = jnp.sum(jnp.exp(logits - own_top[:, None, :]), axis=1)]
    dot_general x8 -> x1, matrix products: 40.3 us -> 0.42 us  [product_along(): lax.dot_general(left, right, (((1,), (1,)), ((), ())), preferred_element_...]
    convert_element_type x13 -> x0, local copies, waits for them, and re-layouts: 36.3 us -> none  [the longest x4 14.3 us: per_device(): attended = attended.reshape(row_count, model_width).astype(jnp.bfloat16)]
    dot_general x8 -> x1, matrix products: 34.4 us -> 0.27 us  [product(): return jnp.dot(left, right, preferred_element_type=jnp.float32)]
    slice x17 -> x11, local copies, waits for them, and re-layouts: 31.6 us -> 3.46 us  [the longest x2 1.28 us: per_device(): grad_place = grad_place[:slot_total]]
  transfers between devices with their start and end apart: 12 -> 12, of which waited for: 12 -> 11; matrix products, arithmetic and copies ran while one was open for 2% -> 2% of each run, Pallas kernels for 0% -> 0%
where the time goes in v2:
time: 674 us; the launch traced here: 665 us
  waiting for transfers between devices  320 us (47%)
  Pallas kernels  175 us (26%)
  local copies, waits for them, and re-layouts  67.6 us (10%)
  matrix products  42.6 us (6%)
  between operations  21.3 us (3%)
  other arithmetic  20.9 us (3%)
  starting transfers between devices  16.9 us (3%)
    reduce_scatter x1, waiting for transfers between devices, per_device(): shard = lax.psum_scatter(packed_grads, 'fsdp', scatter_dimension=0)  181 us
    all_gather x1, waiting for transfers between devices, per_device(): full = lax.all_gather(packed, 'fsdp', axis=0)  86.3 us
    dot_general x14, matrix products, product_across(): lax.dot_general(left, right, (((0,), (0,)), ((), ())), preferred_element_...  41.5 us
    psum x1, waiting for transfers between devices, per_device(): shard = lax.psum(shard, 'rep').astype(jnp.float32)  40.3 us
    pallas_call x1, Pallas kernels, per_device(): pl.pallas_call(functools.partial(widen_kernel, chunk=slots, head_size=hea...  39 us
    pallas_call x1, Pallas kernels, per_device(): image_call(branch_kernel, images, [per_image(slots, model_width), per_ima...  34.9 us
    pallas_call x1, Pallas kernels, per_device(): image_call(functools.partial(attend_back_kernel, head_size=head_size), im...  33.1 us
    pallas_call x1, Pallas kernels, per_device(): image_call(functools.partial(attend_kernel, head_size=head_size), images,...  30.1 us
  transfers between devices with their start and end apart: 12, of which 11 were waited for; matrix products, arithmetic and copies ran while one was open for 2% of the time, Pallas kernels for 0%

profile of v2, /device:TPU:0, one launch (start us, length us, event | category | flops | bytes accessed | tf_op | source)
XLA Modules:
  0.0 664.6 jit_solution(1988629217850437918)
XLA Ops:
  18.9 86.3 %all-gather.3.cloned.1.call-done = bf16[11008,768]{1,0:T(8,128)(2,1)} async-done(((bf16[688,768]{1,0:T(8,128)(2,1)}), bf16[11008,768]{1,0:T(8,128)(2,1)}) %all-gather.3.cloned.1.call-update) | async-done | bytes 16908304 | tf_op jit(solution)/shard_map/all_gather | solution.py:531
  107.5 5.5 slice.417
  113.0 7.7 %fusion.152 = (bf16[16,48,768]{2,1,0:T(8,128)(2,1)}, bf16[16,48,768]{2,1,0:T(8,128)(2,1)S(1)}, bf16[16,48,768]{2,1,0:T(8,128)(2,1)}, bf16[16,48,768]{2,1,0:T(8,1...) fusion(bf16[16,688,768]{2,1,0:T(8,128)(2,1)} %bitcast.173), kind=kLoop, calls=%fused_computation.242 | loop fusion | bytes 21233664 | tf_op jit(solution)/shard_map/slice | solution.py:117
  124.1 2.9 reshape.247
  127.0 2.9 copy.83
  132.1 2.5 bitcast_dynamic-update-slice_fusion.6
  142.3 9.9 %embed.1 = (f32[6,208,768]{2,1,0:T(8,128)}, bf16[6,208,768]{2,1,0:T(8,128)(2,1)}) custom-call(s32[6]{0:T(128)} %reshape.209.counts_ref, bf16[6,208,768]{2,1,0:T(8,128)(2,1)} %pad.28.pixel_ref, s32[6,1,208]{2,1,0:T(1,128)} %pad.29.map_ref, f32[6,1,208]{2,1,0:T(1,128)} %get-tuple-element.155.row_ref, f32[6,208,1]{2,1,0:T(8,128)} %copy.85.column_ref, ...), custom_call_target="tpu_custom_call" | custom-call | tf_op jit(solution)/shard_map/embed/pallas_call | solution.py:565
  152.2 39.0 %widen.1 = (bf16[3,1248,768]{2,1,0:T(8,128)(2,1)}, f32[2,1248,768]{2,1,0:T(8,128)}, bf16[4,1248,768]{2,1,0:T(8,128)(2,1)}, bf16[4,1248,768]{2,1,0:T(8,128)(2,1)}) custom-call(bf16[1248,768]{1,0:T(8,128)(2,1)} %bitcast.194, bf16[7,768,768]{2,1,0:T(8,128)(2,1)} %bitcast_dynamic-update-slice_fusion.wide_ref.wide_hbm, f32[2,1,768]{2,1,0:T(1,128)} %reshape.220.gain_ref, ...), custom_call_target="tpu_custom_call" | custom-call | tf_op jit(solution)/shard_map/widen/pallas_call | solution.py:586
  191.2 30.1 %attend.1 = (bf16[6,208,768]{2,1,0:T(8,128)(2,1)}, f32[6,208,768]{2,1,0:T(8,128)}, f32[6,1,768]{2,1,0:T(1,128)}) custom-call(s32[6]{0:T(128)} %reshape.209.counts_ref, bf16[3,1248,768]{2,1,0:T(8,128)(2,1)} %get-tuple-element.37.qkv_ref, bf16[4,1248,768]{2,1,0:T(8,128)(2,1)} %get-tuple-element.38.hidden_ref, f32[6,208,768]{2,1,0:T(8,128)} %get-tuple-element.39.merged_ref, ...), custom_call_target="tpu_custom_call" | custom-call | tf_op jit(solution)/shard_map/attend/pallas_call | solution.py:619
  231.8 2.5 collective-permute-start.3
  242.8 34.9 %branch.1 = (f32[6,208,768]{2,1,0:T(8,128)}, bf16[6,208,768]{2,1,0:T(8,128)(2,1)}, bf16[6,208,768]{2,1,0:T(8,128)(2,1)}, bf16[4,1248,768]{2,1,0:T(8,128)(2,1)}, f32[8,768]{1,0:T(8,128)}) custom-call(s32[6]{0:T(128)} %reshape.209.counts_ref, f32[6,208,768]{2,1,0:T(8,128)} %get-tuple-element.42.stream_ref, f32[6,1,768]{2,1,0:T(1,128)} %reshape.226.grad_pooled_ref, ...), custom_call_target="tpu_custom_call" | custom-call | tf_op jit(solution)/shard_map/branch/pallas_call | solution.py:689
  277.7 33.1 %attend_back.1 = (bf16[3,1248,768]{2,1,0:T(8,128)(2,1)}, f32[8,768]{1,0:T(8,128)}) custom-call(s32[6]{0:T(128)} %reshape.209.counts_ref, bf16[3,1248,768]{2,1,0:T(8,128)(2,1)} %get-tuple-element.37.qkv_ref, f32[2,1248,768]{2,1,0:T(8,128)} %get-tuple-element.41.rstd_ref, bf16[6,208,768]{2,1,0:T(8,128)(2,1)} %get-tuple-element.44.grad_attended_ref, ...), custom_call_target="tpu_custom_call" | custom-call | tf_op jit(solution)/shard_map/attend_back/pallas_call | solution.py:727
  310.8 5.1 fusion.39
  315.9 2.9 fusion.36
  318.8 2.8 fusion.33
  321.6 2.8 fusion.51
  324.4 2.9 fusion.48
  327.3 2.8 fusion.45
  330.2 2.8 fusion.42
  333.0 28.3 %merge_back.1 = (bf16[6,208,768]{2,1,0:T(8,128)(2,1)}, f32[208,768]{1,0:T(8,128)}, f32[8,768]{1,0:T(8,128)}) custom-call(s32[6]{0:T(128)} %reshape.209.counts_ref, bf16[3,1248,768]{2,1,0:T(8,128)(2,1)} %get-tuple-element.45.grad_qkv_ref, bf16[4,1248,768]{2,1,0:T(8,128)(2,1)} %get-tuple-element.46.grad_act_ref, ...), custom_call_target="tpu_custom_call" | custom-call | tf_op jit(solution)/shard_map/merge_back/pallas_call | solution.py:742
  362.0 4.3 bitcast_convert_fusion.1
  369.4 4.0 fusion.78
  373.5 3.5 fusion.57
  376.9 3.5 fusion.63
  393.8 2.9 constant_dynamic-update-slice_fusion.12
  398.6 181.3 %reduce-scatter.2.cloned.1.call-done = bf16[1,688,768]{2,1,0:T(8,128)(2,1)} async-done(((bf16[16,688,768]{2,1,0:T(8,128)(2,1)}), bf16[1,688,768]{2,1,0:T(8,128)(2,1)}) %reduce-scatter.2.cloned.1.call-update) | async-done | bytes 1056784 | tf_op jit(solution)/shard_map/reduce_scatter | solution.py:777
  581.3 40.3 %all-reduce.9.cloned.1.call-done = bf16[688,768]{1,0:T(8,128)(2,1)} async-done(((bf16[688,768]{1,0:T(8,128)(2,1)}), bf16[688,768]{1,0:T(8,128)(2,1)}) %all-reduce.9.cloned.1.call-update) | async-done | bytes 1056784 | tf_op jit(solution)/shard_map/psum | solution.py:778
  631.0 2.8 collective-permute-start.6
  635.4 2.8 collective-permute-start.7
  639.7 3.8 collective-permute-start.8
  645.9 3.2 fusion.92
  652.2 3.3 fusion.85
  (273 shorter events, 80.0 us)
Async XLA Ops:
  7.2 215.1 %copy-start = (bf16[2,96,768]{2,1,0:T(8,128)(2,1)S(1)}, bf16[2,96,768]{2,1,0:T(8,128)(2,1)}, u32[]{:S(2)}) copy-start(bf16[2,96,768]{2,1,0:T(8,128)(2,1)} %param.31) | copy-start | bytes 884740
  7.2 98.0 %all-gather.3.cloned.1.call-start = ((), (), s32[]{:S(2)}) async-start(), calls=%async_computation.3 | async-start | bytes 17965056 | tf_op jit(solution)/shard_map/all_gather | solution.py:531
  12.7 567.3 %reduce-scatter.2.cloned.1.call-start = ((), (), s32[]{:S(2)}) async-start(), calls=%async_computation.1 | async-start | bytes 17965056 | tf_op jit(solution)/shard_map/reduce_scatter | solution.py:777
  223.0 1.2 collective-permute-start
  224.3 3.7 collective-permute-start.1
  228.0 3.7 collective-permute-start.2
  231.8 4.6 collective-permute-start.3
  236.4 3.7 collective-permute-start.4
  310.8 5.1 copy-start.2
  310.8 5.1 copy-start.14
  315.9 5.7 slice-start
  362.0 4.6 copy-start.38
  373.5 6.9 %slice-start.2 = ((s8[7667712]{0:T(1024)(128)(4,1)}), s8[4194304]{0:T(1024)(128)(4,1)S(1)}, s32[]{:S(2)}) async-start(s8[7667712]{0:T(1024)(128)(4,1)} %bitcast.178), calls=%async_computation.6 | async-start | bytes 8388608
  398.6 223.0 %all-reduce.9.cloned.1.call-start = ((), (), s32[]{:S(2)}) async-start(), calls=%async_computation.2 | async-start | bytes 2113536 | tf_op jit(solution)/shard_map/psum | solution.py:778
  625.5 4.3 collective-permute-start.5
  625.6 19.5 %copy-start.39 = (f32[4,48]{1,0:T(4,128)S(1)}, f32[4,48]{1,0:T(4,128)}, u32[]{:S(2)}) copy-start(f32[4,48]{1,0:T(4,128)} %param.38) | copy-start | bytes 2308
  625.6 19.5 %copy-start.44 = (f32[4,48]{1,0:T(4,128)S(1)}, f32[4,48]{1,0:T(4,128)}, u32[]{:S(2)}) copy-start(f32[4,48]{1,0:T(4,128)} %param.52) | copy-start | bytes 2308
  625.6 19.5 %copy-start.45 = (f32[4,48]{1,0:T(4,128)S(1)}, f32[4,48]{1,0:T(4,128)}, u32[]{:S(2)}) copy-start(f32[4,48]{1,0:T(4,128)} %param.45) | copy-start | bytes 2308
  625.8 19.9 %copy-start.12 = (f32[240,768]{1,0:T(8,128)S(1)}, f32[240,768]{1,0:T(8,128)}, u32[]{:S(2)}) copy-start(f32[240,768]{1,0:T(8,128)} %param.36) | copy-start | bytes 2211844
  631.0 3.7 collective-permute-start.6
  635.4 3.7 collective-permute-start.7
  639.7 4.6 collective-permute-start.8
  645.7 4.8 copy-start.30
  645.7 4.8 copy-start.35
  645.8 4.7 copy-start.36
  645.8 5.4 copy-start.27
  645.8 5.4 copy-start.29
  645.8 5.4 copy-start.31
  645.8 5.4 copy-start.32
  645.8 5.4 copy-start.33
  645.8 5.4 copy-start.34
  645.8 6.4 copy-start.25
  (34 other events, 91.5 us)
Sparse Core Ops, SparseCore 0:
  12.8 92.3 all-gather.2
  398.7 181.1 reduce-scatter.1
  582.3 39.2 all-reduce.8

commit v3 on v2

--- a/solution.py
+++ b/solution.py
@@ -131,50 +131,6 @@
     return embed, place, wide, narrow, project, scale, bias
 
 
-def pack_grads(owners, embed, place, wide, narrow, project, scale, bias):
-    width = embed.shape[1]
-    by_owner = lambda grad: grad.astype(jnp.bfloat16).reshape(owners, -1, width)
-    rows = [by_owner(embed)]
-    rows += [by_owner(block) for block in wide]
-    rows += [by_owner(narrow), by_owner(project)]
-    flat = lambda grad: jnp.swapaxes(
-        grad.astype(jnp.bfloat16).reshape(grad.shape[0], owners, -1), 0, 1
-    ).reshape(owners, -1)
-    small = jnp.concatenate(
-        [flat(place), flat(scale), bias.astype(jnp.bfloat16).reshape(owners, -1)], axis=1
-    )
-    small_rows = -(-small.shape[1] // (16 * width)) * 16
-    small = jnp.pad(small, ((0, 0), (0, small_rows * width - small.shape[1])))
-    rows.append(small.reshape(owners, small_rows, width))
-    return jnp.concatenate(rows, axis=1)
-
-
-def unpack_grads(shard, shapes):
-    (e_rows, width), (slots, p_cols), (w_rows, w_cols), (n_rows, _), (j_rows, _), (
-        s_rows,
-        s_cols,
-    ), (b_len,) = shapes
-    at = 0
-    embed = shard[at : at + e_rows]
-    at += e_rows
-    wide = []
-    for _ in range(w_cols // width):
-        wide.append(shard[at : at + w_rows])
-        at += w_rows
-    wide = jnp.concatenate(wide, axis=1)
-    narrow = shard[at : at + n_rows]
-    at += n_rows
-    project = shard[at : at + j_rows]
-    at += j_rows
-    small = shard[at:].reshape(-1)
-    place = small[: slots * p_cols].reshape(slots, p_cols)
-    at = slots * p_cols
-    scale = small[at : at + s_rows * s_cols].reshape(s_rows, s_cols)
-    at += s_rows * s_cols
-    bias = small[at : at + b_len]
-    return embed, place, wide, narrow, project, scale, bias
-
-
 def padded_rows(rows):
     return -(-rows // 16) * 16
 
@@ -257,7 +213,7 @@
         mixer = head_mixer(head_size)
         gain = gain_ref[0]
 
-        @pl.loop(0, chunks)
+        @pl.loop(0, chunks, unroll=True)
         def _(index):
             rows = rows_of(index)
             values = product(normed_ref[rows, :], wide_ref[0])
@@ -268,14 +224,14 @@
 
     @pl.when(step == 2)
     def _():
-        @pl.loop(0, chunks)
+        @pl.loop(0, chunks, unroll=True)
         def _(index):
             rows = rows_of(index)
             qkv_ref[0, rows, :] = product(normed_ref[rows, :], wide_ref[0]).astype(jnp.bfloat16)
 
     @pl.when(step > 2)
     def _():
-        @pl.loop(0, chunks)
+        @pl.loop(0, chunks, unroll=True)
         def _(index):
             rows = rows_of(index)
             values = product(normed_ref[rows, :], wide_ref[0]) + bias_ref[0]
@@ -374,11 +330,11 @@
 
 
 def attend_back_kernel(
-    counts_ref, qkv_ref, rstd_ref, grad_attended_ref, gain_ref, grad_qkv_ref, sums_ref,
-    grad_ref, *, head_size,
+    counts_ref, qkv_ref, rstd_ref, grad_attended_ref, gain_ref, *refs, base, head_size
 ):
+    grad_qkv_ref, sums_ref, grad_ref = refs[-3:]
     image = pl.program_id(0)
-    live_count = counts_ref[image]
+    live_count = counts_ref[base + image]
     slots, width = grad_attended_ref.shape[1:]
 
     @pl.when(image == 0)
@@ -422,25 +378,30 @@
 
 def merge_back_kernel(
     counts_ref, grad_qkv_ref, grad_act_ref, wide_hbm, merged_ref, grad_stream_ref, gain_ref,
-    map_ref, row_ref, column_ref, grad_patch_ref, grad_place_ref, sums_ref, wide_ref, sem,
+    map_ref, row_ref, column_ref, *refs, base,
 ):
+    grad_patch_ref, grad_place_ref, sums_ref, wide_ref, sem = refs[-5:]
     image = pl.program_id(0)
-    live_count = counts_ref[image]
+    live_count = counts_ref[base + image]
     slots, width = merged_ref.shape[1:]
-    copy = pltpu.make_async_copy(wide_hbm, wide_ref, sem)
+    blocks = wide_ref.shape[0]
+    copies = [
+        pltpu.make_async_copy(wide_hbm.at[part], wide_ref.at[part], sem.at[part])
+        for part in range(blocks)
+    ]
 
     @pl.when(image == 0)
     def _():
-        copy.start()
+        for copy in copies:
+            copy.start()
         sums_ref[...] = jnp.zeros_like(sums_ref)
         grad_place_ref[...] = jnp.zeros_like(grad_place_ref)
-        copy.wait()
 
     grad_normed = jnp.zeros((slots, width), jnp.float32)
-    for part in range(3):
-        grad_normed = grad_normed + product_along(grad_qkv_ref[part], wide_ref[part])
-    for part in range(grad_act_ref.shape[0]):
-        grad_normed = grad_normed + product_along(grad_act_ref[part], wide_ref[3 + part])
+    for part in range(blocks):
+        pl.when(image == 0)(copies[part].wait)
+        grads = grad_qkv_ref[part] if part < 3 else grad_act_ref[part - 3]
+        grad_normed = grad_normed + product_along(grads, wide_ref[part])
     unit, rstd = normal_rows(merged_ref[0])
     sums_ref[0:1, :] += jnp.sum(grad_normed * unit, axis=0, keepdims=True)
     slanted = grad_normed * gain_ref[...]
@@ -479,6 +440,9 @@
 roomy = pltpu.CompilerParams(vmem_limit_bytes=60 * 1024 * 1024)
 
 
+long = pl.CostEstimate(flops=60_000_000_000, bytes_accessed=1000, transcendentals=0)
+
+
 def image_call(kernel, images, in_specs, out_specs, out_shape, scratch=(), name=None):
     return pl.pallas_call(
         kernel,
@@ -491,8 +455,250 @@
         ),
         out_shape=out_shape,
         compiler_params=roomy,
+        cost_estimate=long,
         name=name,
     )
+
+
+def picked(terms, axis, index):
+    return [lax.dynamic_index_in_dim(term, index, axis, keepdims=False) for term in terms]
+
+
+def added(terms):
+    total = terms[0].astype(jnp.float32)
+    for term in terms[1:]:
+        total = total + term.astype(jnp.float32)
+    return total
+
+
+def behind(terms, after):
+    if after is None:
+        return terms
+    return lax.optimization_barrier((terms, after))[0]
+
+
+def traded(terms, axis, index, count, mesh_axis, stride):
+    size = lax.axis_size(mesh_axis)
+    sends = [
+        added(picked(terms, axis, index ^ turn)).astype(jnp.bfloat16) for turn in range(1, count)
+    ]
+    after = yield sends
+    kept = picked(terms, axis, index)
+    for turn, send in enumerate(sends, 1):
+        kept.append(lax.ppermute(send, mesh_axis, bit_swap(size, turn * stride)))
+    return behind(kept, after)
+
+
+def core_terms(mine, other):
+    chips, rows, width = mine.shape
+    after = yield [other]
+    got = lax.ppermute(other, "fsdp", bit_swap(lax.axis_size("fsdp"), 1))
+    return [term.reshape(chips // 2, 2, rows, width) for term in behind([mine, got], after)]
+
+
+def rep_swap(own):
+    return lax.ppermute(own, "rep", bit_swap(2, 1))
+
+
+def places():
+    place = lax.axis_index("fsdp")
+    return place // 4, (place // 2) % 2
+
+
+def reduce_rows_first(mine, other):
+    high, middle = places()
+    reps = lax.axis_size("rep")
+    count = mine.shape[0] // 2
+    terms = yield from core_terms(mine, other)
+    terms = [
+        term.reshape(count, 2, reps, term.shape[2] // reps, term.shape[3]) for term in terms
+    ]
+    terms = yield from traded(terms, 2, lax.axis_index("rep"), reps, "rep", 1)
+    terms = yield from traded(terms, 1, middle, 2, "fsdp", 2)
+    terms = yield from traded(terms, 0, high, count, "fsdp", 4)
+    own = added(terms).astype(jnp.bfloat16)
+    yield [own]
+    if reps == 2:
+        first, second = ordered_pair(own, rep_swap(own), "rep", 1)
+        return jnp.concatenate([first, second], axis=0)
+    return lax.all_gather(own, "rep", axis=0, tiled=True)
+
+
+def reduce_rows_last(mine, other):
+    high, middle = places()
+    count = mine.shape[0] // 2
+    terms = yield from core_terms(mine, other)
+    terms = yield from traded(terms, 1, middle, 2, "fsdp", 2)
+    terms = yield from traded(terms, 0, high, count, "fsdp", 4)
+    own = added(terms).astype(jnp.bfloat16)
+    yield [own]
+    if lax.axis_size("rep") == 2:
+        return added([own, rep_swap(own)]).astype(jnp.bfloat16)
+    return lax.psum(own, "rep")
+
+
+class Flow:
+    def __init__(self, steps):
+        self.steps, self.result = steps, None
+
+    def go(self, after=None):
+        try:
+            return self.steps.send(after)
+        except StopIteration as end:
+            self.result = end.value
+            return []
+
+    def finish(self):
+        while self.result is None:
+            self.go()
+        return self.result
+
+
+def split_cores(result, core, mine_ref, other_ref):
+    chips, rows = mine_ref.shape[:2]
+    pairs = result.astype(jnp.bfloat16).reshape(chips, 2, rows, result.shape[1])
+    first, second = pairs[:, 0], pairs[:, 1]
+    mine_ref[...] = jnp.where(core == 0, first, second)
+    other_ref[...] = jnp.where(core == 0, second, first)
+
+
+def narrow_grad_kernel(
+    core_ref, attended_ref, hidden_ref, branch_ref, mine_hbm, other_hbm, total_ref, sem
+):
+    step = pl.program_id(0)
+    width = branch_ref.shape[1]
+    chips, rows = mine_hbm.shape[:2]
+
+    @pl.when(step == 0)
+    def _():
+        total_ref[:width, :] = product_across(attended_ref[...], branch_ref[...]).astype(
+            jnp.bfloat16
+        )
+
+    @pl.when(step > 0)
+    def _():
+        at = pl.multiple_of(step * width, width)
+        total_ref[pl.ds(at, width), :] = product_across(hidden_ref[0], branch_ref[...]).astype(
+            jnp.bfloat16
+        )
+
+    @pl.when(step == pl.num_programs(0) - 1)
+    def _():
+        core = core_ref[0]
+        copies = []
+        for chip in range(chips):
+            for side, out in enumerate((mine_hbm, other_hbm)):
+                owner = 2 * chip + (core ^ side)
+                source = total_ref.at[pl.ds(pl.multiple_of(owner * rows, rows), rows), :]
+                copies.append(
+                    pltpu.make_async_copy(source, out.at[chip], sem.at[2 * chip + side])
+                )
+        for copy in copies:
+            copy.start()
+        for copy in copies:
+            copy.wait()
+
+
+def wide_grad_kernel(core_ref, normed_ref, *refs):
+    *grad_refs, mine_ref, other_ref = refs
+    total = None
+    for part, grad_ref in enumerate(grad_refs):
+        rows = grad_ref.shape[1]
+        term = product_across(normed_ref[part * rows : (part + 1) * rows, :], grad_ref[0])
+        total = term if total is None else total + term
+    split_cores(total, core_ref[0], mine_ref, other_ref)
+
+
+def wide_project_grad_kernel(
+    core_ref, normed_ref, grad_ref, pooled_ref, embeds_ref, mine_ref, other_ref
+):
+    last = pl.program_id(0) == pl.num_programs(0) - 1
+
+    @pl.when(jnp.logical_not(last))
+    def _():
+        wide_grad_kernel(core_ref, normed_ref, grad_ref, mine_ref, other_ref)
+
+    @pl.when(last)
+    def _():
+        split_cores(
+            product_across(pooled_ref[...], embeds_ref[...]), core_ref[0], mine_ref, other_ref
+        )
+
+
+def embed_grad_kernel(core_ref, pixel_ref, *refs):
+    *grad_refs, extra_ref, mine_ref, other_ref = refs
+    parts = len(grad_refs) // 2
+    total, place = None, None
+    for part in range(parts):
+        rows = grad_refs[part].shape[0]
+        term = product_across(pixel_ref[part * rows : (part + 1) * rows, :], grad_refs[part][...])
+        total = term if total is None else total + term
+        own = grad_refs[parts + part][...]
+        place = own if place is None else place + own
+    width, wide_rows = total.shape[1], mine_ref.shape[1] - extra_ref.shape[1]
+    beside = mine_ref.shape[2] - width
+    spare = jnp.zeros((beside - place.shape[0], width), jnp.float32)
+    place = jnp.concatenate([place, spare], axis=0).T
+    core = core_ref[0]
+    top = jnp.concatenate([total, place], axis=1).astype(jnp.bfloat16)
+    chips = mine_ref.shape[0]
+    pairs = top.reshape(chips, 2, wide_rows, width + beside)
+    mine_ref[:, :wide_rows, :] = jnp.where(core == 0, pairs[:, 0], pairs[:, 1])
+    other_ref[:, :wide_rows, :] = jnp.where(core == 0, pairs[:, 1], pairs[:, 0])
+    extra = extra_ref[...].reshape(chips, 2, extra_ref.shape[1], width + beside)
+    mine_ref[:, wide_rows:, :] = jnp.where(core == 0, extra[:, 0], extra[:, 1])
+    other_ref[:, wide_rows:, :] = jnp.where(core == 0, extra[:, 1], extra[:, 0])
+
+
+def square_kernel(*refs):
+    *shard_refs, total_ref = refs
+    total = jnp.zeros((1, 1), jnp.float32)
+    for shard_ref in shard_refs:
+        values = shard_ref[...].astype(jnp.float32)
+        columns = jnp.sum(values * values, axis=0, keepdims=True)
+        total = total + jnp.sum(columns, axis=1, keepdims=True)
+    total_ref[...] = jnp.broadcast_to(total, total_ref.shape)
+
+
+def update_kernel(
+    total_ref, narrow_ref, hidden_ref, qkv_ref, embed_ref, *refs, wide_rows
+):
+    weights, moments, squares = refs[:7], refs[7:14], refs[14:21]
+    changes, clips = refs[21:28], refs[28:35]
+    factor = clip_bound / jnp.maximum(jnp.sqrt(total_ref[:1, :1]), clip_bound)
+    width = narrow_ref.shape[1]
+
+    def update(index, rows, columns, gradient):
+        at = (slice(*rows), slice(*columns))
+        change, clipped = adam_step(
+            weights[index][at],
+            gradient.astype(jnp.float32),
+            moments[index][at],
+            squares[index][at],
+            factor,
+        )
+        changes[index][at] = change
+        clips[index][at] = clipped
+
+    everything = (None,)
+    update(0, everything, everything, embed_ref[:wide_rows, :width])
+    blocks = weights[2].shape[1] // width
+    for k in range(blocks):
+        source, at = (qkv_ref, k) if k < 3 else (hidden_ref, k - 3)
+        update(
+            2,
+            everything,
+            (k * width, (k + 1) * width),
+            source[at * wide_rows : (at + 1) * wide_rows, :],
+        )
+    update(3, everything, everything, narrow_ref[...])
+    update(4, everything, everything, hidden_ref[(blocks - 3) * wide_rows :, :])
+    beside = embed_ref[:wide_rows, width:].astype(jnp.float32).T
+    update(1, everything, everything, beside[: weights[1].shape[0], :])
+    scale_rows, scale_columns = weights[5].shape
+    extra = embed_ref[wide_rows:, :].astype(jnp.float32)
+    update(5, everything, everything, extra[1 : 1 + scale_rows, :scale_columns])
+    update(6, everything, everything, extra[:1, : weights[6].shape[1]])
 
 
 def per_device(
@@ -684,7 +890,6 @@
         .astype(low)
         .reshape(images, -1)
     )
-    grad_project = product_across(pooled_low, grad_embeds)
     grad_pooled = product_along(grad_embeds, project_full)
     grad_stream, grad_branch, grad_attended, grad_act, out_sums = image_call(
         branch_kernel,
@@ -716,69 +921,211 @@
         live_counts, stream, grad_pooled.reshape(images, 1, model_width), scale_float[1:2], slope,
         narrow_full,
     )
-    across = lambda left, right: product_across(left, right).astype(low)
+    core = (lax.axis_index("fsdp") % 2).reshape(1)
+    chips = owners // 2
+    wide_rows = model_width // owners
+    narrow_rows = narrower.shape[0]
     branch_rows = grad_branch.reshape(rows, model_width)
-    grad_narrow = jnp.concatenate(
-        [across(attended.reshape(rows, model_width), branch_rows)]
-        + [across(hidden[k], branch_rows) for k in range(hidden_blocks)],
-        axis=0,
-    )
-    wide_hidden = [across(normed_rows, grad_act[k]) for k in range(hidden_blocks)]
-    grad_qkv, head_sums = image_call(
-        functools.partial(attend_back_kernel, head_size=head_size),
-        images,
-        [
-            image_columns(3),
-            image_columns(2),
-            per_image(slots, model_width),
-            whole(2, 1, model_width),
-        ],
-        [image_columns(3), whole(8, model_width)],
-        [shape((3, rows, model_width), low), shape((8, model_width), f32)],
-        [pltpu.VMEM((2, slots, model_width), f32)],
-        name="attend_back",
-    )(live_counts, qkv, rstd, grad_attended, scale_float[2:4].reshape(2, 1, model_width))
-    wide_parts = [across(normed_rows, grad_qkv[k]) for k in range(3)] + wide_hidden
-    grad_patches, grad_place, merge_sums = image_call(
-        merge_back_kernel,
-        images,
-        [
-            image_columns(3),
-            image_columns(hidden_blocks),
-            anywhere,
-            per_image(slots, model_width),
-            per_image(slots, model_width),
-            whole(1, model_width),
-            per_image(1, slots),
-            per_image(1, slots),
-            per_image(slots, 1),
-        ],
-        [per_image(slots, model_width), whole(slots, model_width), whole(8, model_width)],
-        [
-            shape((images, slots, model_width), low),
-            shape((slots, model_width), f32),
-            shape((8, model_width), f32),
-        ],
-        [pltpu.VMEM((3 + hidden_blocks, model_width, model_width), low), pltpu.SemaphoreType.DMA],
-        name="merge_back",
+    halves = lambda count, width: [shape((chips, count, width), low)] * 2
+    narrow_halves = pl.pallas_call(
+        narrow_grad_kernel,
+        grid_spec=pltpu.PrefetchScalarGridSpec(
+            num_scalar_prefetch=1,
+            grid=(1 + hidden_blocks,),
+            in_specs=[
+                whole(rows, model_width),
+                block((1, rows, model_width), lambda k, _: (jnp.maximum(k - 1, 0), 0, 0)),
+                whole(rows, model_width),
+            ],
+            out_specs=[anywhere] * 2,
+            scratch_shapes=[
+                pltpu.VMEM((hidden_width + model_width, model_width), low),
+                pltpu.SemaphoreType.DMA((2 * chips,)),
+            ],
+        ),
+        out_shape=halves(narrow_rows, model_width),
+        compiler_params=roomy,
+        cost_estimate=long,
+        name="narrow_grad",
+    )(core, attended.reshape(rows, model_width), hidden, branch_rows)
+    narrow_flow = Flow(reduce_rows_first(*narrow_halves))
+    narrow_flow.go()
+    owner_block = block((chips, wide_rows, model_width), lambda k, _: (0, k, 0))
+    few = padded_rows(images)
+    hidden_halves = pl.pallas_call(
+        wide_project_grad_kernel,
+        grid_spec=pltpu.PrefetchScalarGridSpec(
+            num_scalar_prefetch=1,
+            grid=(hidden_blocks + 1,),
+            in_specs=[
+                whole(rows, model_width),
+                block(
+                    (1, rows, model_width), lambda k, _: (jnp.minimum(k, hidden_blocks - 1), 0, 0)
+                ),
+                whole(few, model_width),
+                whole(few, model_width),
+            ],
+            out_specs=[owner_block] * 2,
+        ),
+        out_shape=halves((hidden_blocks + 1) * wide_rows, model_width),
+        compiler_params=roomy,
+        cost_estimate=long,
+        name="hidden_grad",
     )(
-        live_counts, grad_qkv, grad_act, wide_stack, merged, grad_stream, scale_float[0:1],
-        slot_map, row_weight, column_weight,
-    )
-    grad_embed = across(
-        pixel_rows.reshape(rows, patch_size), grad_patches.reshape(rows, model_width)
-    )
-    grad_place = grad_place[:slot_total]
+        core, normed_rows, grad_act, jnp.pad(pooled_low, ((0, few - images), (0, 0))),
+        jnp.pad(grad_embeds, ((0, few - images), (0, 0))),
+    )
+    hidden_flow = Flow(reduce_rows_last(*hidden_halves))
+    hidden_flow.go()
+    parts = images_dev
+    per_part = images // parts
+    part_rows = per_part * slots
+
+    def shifted(base, rows_count):
+        return block((1, rows_count, model_width), lambda image, counts: (base + image, 0, 0))
+
+    def shifted_columns(base, count):
+        return block((count, slots, model_width), lambda image, counts: (0, base + image, 0))
+
+    head_gains = scale_float[2:4].reshape(2, 1, model_width)
+    guards = narrow_flow.go()
+    grad_qkv, head_sums = [], 0.0
+    for part in range(parts):
+        base = part * per_part
+        grads, sums_part = image_call(
+            functools.partial(attend_back_kernel, base=base, head_size=head_size),
+            per_part,
+            [
+                shifted_columns(base, 3),
+                shifted_columns(base, 2),
+                shifted(base, slots),
+                whole(2, 1, model_width),
+            ]
+            + [anywhere] * len(guards),
+            [image_columns(3), whole(8, model_width)],
+            [shape((3, part_rows, model_width), low), shape((8, model_width), f32)],
+            [pltpu.VMEM((2, slots, model_width), f32)],
+            name="attend_back",
+        )(live_counts, qkv, rstd, grad_attended, head_gains, *guards)
+        grad_qkv.append(grads)
+        head_sums = head_sums + sums_part
+        guards = [grads]
+        if part == 0:
+            guards += hidden_flow.go(grads)
+    guards += narrow_flow.go(grads)
+    qkv_halves = pl.pallas_call(
+        lambda core_ref, normed_ref, *refs: wide_grad_kernel(
+            core_ref, normed_ref, *refs[:parts], *refs[-2:]
+        ),
+        grid_spec=pltpu.PrefetchScalarGridSpec(
+            num_scalar_prefetch=1,
+            grid=(3,),
+            in_specs=[whole(rows, model_width)]
+            + [block((1, part_rows, model_width), lambda k, _: (k, 0, 0))] * parts
+            + [anywhere] * len(guards),
+            out_specs=[owner_block] * 2,
+        ),
+        out_shape=halves(3 * wide_rows, model_width),
+        compiler_params=roomy,
+        cost_estimate=long,
+        name="qkv_grad",
+    )(core, normed_rows, *grad_qkv, *guards)
+    qkv_flow = Flow(reduce_rows_first(*qkv_halves))
+    guards = qkv_flow.go()
+    grad_patches, grad_places, merge_sums = [], [], 0.0
+    for part in range(parts):
+        base = part * per_part
+        grads, place_part, sums_part = image_call(
+            functools.partial(merge_back_kernel, base=base),
+            per_part,
+            [
+                image_columns(3),
+                shifted_columns(base, hidden_blocks),
+                anywhere,
+                shifted(base, slots),
+                shifted(base, slots),
+                whole(1, model_width),
+                block((1, 1, slots), lambda image, counts, base=base: (base + image, 0, 0)),
+                block((1, 1, slots), lambda image, counts, base=base: (base + image, 0, 0)),
+                block((1, slots, 1), lambda image, counts, base=base: (base + image, 0, 0)),
+            ]
+            + [anywhere] * len(guards),
+            [per_image(slots, model_width), whole(slots, model_width), whole(8, model_width)],
+            [
+                shape((per_part, slots, model_width), low),
+                shape((slots, model_width), f32),
+                shape((8, model_width), f32),
+            ],
+            [
+                pltpu.VMEM((3 + hidden_blocks, model_width, model_width), low),
+                pltpu.SemaphoreType.DMA((3 + hidden_blocks,)),
+            ],
+            name="merge_back",
+        )(
+            live_counts, grad_qkv[part], grad_act, wide_stack, merged, grad_stream,
+            scale_float[0:1], slot_map, row_weight, column_weight, *guards,
+        )
+        grad_patches.append(grads.reshape(part_rows, model_width))
+        grad_places.append(place_part)
+        merge_sums = merge_sums + sums_part
+        guards = [grads]
+        if part == 0:
+            guards += hidden_flow.go(grads) + qkv_flow.go(grads)
+        elif part == 1:
+            guards += narrow_flow.go(grads)
+    guards += hidden_flow.go(grads) + qkv_flow.go(grads)
+    scale_rows, scale_columns = scales.shape
+    bias_count = biases.shape[0]
     grad_scale = jnp.stack([merge_sums[0], out_sums[hidden_blocks + 1], head_sums[0], head_sums[1]])
     grad_bias = jnp.concatenate([out_sums[: hidden_blocks + 1].reshape(-1), merge_sums[1]])
-    packed_grads = pack_grads(
-        owners, grad_embed, grad_place, wide_parts, grad_narrow, grad_project, grad_scale, grad_bias
-    )
-    shard = lax.psum_scatter(packed_grads, "fsdp", scatter_dimension=0)
-    shard = lax.psum(shard, "rep").astype(jnp.float32)
-    total_norm = jnp.sqrt(sum_over(jnp.sum(shard * shard), "fsdp"))
-    shards = unpack_grads(shard, shapes)
-    factor = clip_bound / jnp.maximum(total_norm, clip_bound)
+    beside = -(-slots // 128) * 128
+    piece_width = model_width + beside
+    fill = lambda values: jnp.pad(
+        values, ((0, 0), (0, 0), (0, piece_width - values.shape[2]))
+    )
+    extra_rows = 16
+    extra = jnp.concatenate(
+        [
+            fill(grad_bias.reshape(owners, 1, bias_count)),
+            fill(jnp.swapaxes(grad_scale.reshape(scale_rows, owners, scale_columns), 0, 1)),
+            jnp.zeros((owners, extra_rows - 1 - scale_rows, piece_width), f32),
+        ],
+        axis=1,
+    ).astype(low)
+    embed_halves = pl.pallas_call(
+        lambda core_ref, pixel_ref, *refs: embed_grad_kernel(
+            core_ref, pixel_ref, *refs[: 2 * parts + 1], *refs[-2:]
+        ),
+        grid_spec=pltpu.PrefetchScalarGridSpec(
+            num_scalar_prefetch=1,
+            grid=(1,),
+            in_specs=[whole(rows, patch_size)]
+            + [whole(part_rows, model_width)] * parts
+            + [whole(slots, model_width)] * parts
+            + [whole(owners, extra_rows, piece_width)]
+            + [anywhere] * len(guards),
+            out_specs=[whole(chips, wide_rows + extra_rows, piece_width)] * 2,
+        ),
+        out_shape=halves(wide_rows + extra_rows, piece_width),
+        compiler_params=roomy,
+        cost_estimate=long,
+        name="embed_grad",
+    )(core, pixel_rows.reshape(rows, patch_size), *grad_patches, *grad_places, extra, *guards)
+    embed_flow = Flow(reduce_rows_last(*embed_halves))
+    flows = (narrow_flow, hidden_flow, qkv_flow, embed_flow)
+    while any(flow.result is None for flow in flows):
+        for flow in flows:
+            if flow.result is None:
+                flow.go()
+    shards = [flow.result for flow in flows]
+    squares_sum = pl.pallas_call(
+        square_kernel,
+        out_shape=shape((8, 128), f32),
+        compiler_params=roomy,
+        name="squares",
+    )(*shards)
+    squares_sum = sum_over(squares_sum, "fsdp")
+    total_norm = jnp.sqrt(squares_sum[0, 0])
     moments = (
         moment_embedder,
         moment_positions,
@@ -797,29 +1144,19 @@
         square_scales,
         square_biases,
     )
-    results = [
-        adam_step(weights[index], shards[index], moments[index], squares[index], factor)
-        for index in range(7)
+    as_rows = lambda arrays: [
+        array.reshape(1, -1) if array.ndim == 1 else array for array in arrays
     ]
-    return (
-        objective,
-        weight_total_all,
-        total_norm,
-        results[0][0],
-        results[1][0],
-        results[2][0],
-        results[3][0],
-        results[4][0],
-        results[5][0],
-        results[6][0],
-        results[0][1],
-        results[1][1],
-        results[2][1],
-        results[3][1],
-        results[4][1],
-        results[5][1],
-        results[6][1],
-    )
+    outs = pl.pallas_call(
+        functools.partial(update_kernel, wide_rows=wide_rows),
+        out_shape=[shape(array.shape, f32) for array in as_rows(weights) * 2],
+        compiler_params=roomy,
+        name="update",
+    )(squares_sum, *shards, *as_rows(weights), *as_rows(moments), *as_rows(squares))
+    outs = [
+        out.reshape(array.shape) for out, array in zip(outs, weights * 2, strict=True)
+    ]
+    return (objective, weight_total_all, total_norm, *outs)
 
 
 def solution(mesh):

time: 674 us -> 546 us (0.81)
  waiting for transfers between devices: 320 us -> 135 us
  Pallas kernels: 175 us -> 227 us
  matrix products: 42.6 us -> 1.17 us
  starting transfers between devices: 16.9 us -> 44.8 us
  other arithmetic: 20.9 us -> 41.3 us
    reduce_scatter x1 -> x0, waiting for transfers between devices: 181 us -> none  [per_device(): shard = lax.psum_scatter(packed_grads, 'fsdp', scatter_dimension=0)]
    pallas_call x2 -> x12, Pallas kernels: 61.3 us -> 134 us  [the longest x3 43.2 us: per_device(): image_call(functools.partial(merge_back_kernel, base=base), per_part, [im...]
    dot_general x14 -> x0, matrix products: 41.5 us -> none  [product_across(): lax.dot_general(left, right, (((0,), (0,)), ((), ())), preferred_element_...]
    psum x1 -> x0, waiting for transfers between devices: 40.3 us -> none  [per_device(): shard = lax.psum(shard, 'rep').astype(jnp.float32)]
    ppermute x0 -> x26, starting transfers between devices: none -> 34.4 us  [the longest x18 28.7 us: traded(): kept.append(lax.ppermute(send, mesh_axis, bit_swap(size, turn * stride)))]
    ppermute x0 -> x26, waiting for transfers between devices: none -> 31.2 us  [the longest x18 21.2 us: traded(): kept.append(lax.ppermute(send, mesh_axis, bit_swap(size, turn * stride)))]
    convert_element_type x2 -> x15, other arithmetic: 0.89 us -> 24.3 us  [the longest x9 17.3 us: traded(): added(picked(terms, axis, index ^ turn)).astype(jnp.bfloat16)]
    pallas_call x1, Pallas kernels: 34.9 us -> 20.9 us  [per_device(): image_call(branch_kernel, images, [per_image(slots, model_width), per_ima...]
  transfers between devices with their start and end apart: 12 -> 36, of which waited for: 11 -> 17; matrix products, arithmetic and copies ran while one was open for 2% -> 11% of each run, Pallas kernels for 0% -> 19%
where the time goes in v3:
time: 546 us; the launch traced here: 540 us
  Pallas kernels  227 us (42%)
  waiting for transfers between devices  135 us (25%)
  local copies, waits for them, and re-layouts  71.7 us (13%)
  starting transfers between devices  44.8 us (8%)
  other arithmetic  41.3 us (8%)
  between operations  18.8 us (3%)
    all_gather x1, waiting for transfers between devices, per_device(): full = lax.all_gather(packed, 'fsdp', axis=0)  87.8 us
    pallas_call x3, Pallas kernels, per_device(): image_call(functools.partial(merge_back_kernel, base=base), per_part, [im...  43.2 us
    pallas_call x3, Pallas kernels, per_device(): image_call(functools.partial(attend_back_kernel, base=base, head_size=hea...  40.1 us
    pallas_call x1, Pallas kernels, per_device(): pl.pallas_call(functools.partial(widen_kernel, chunk=slots, head_size=hea...  32.1 us
    pallas_call x1, Pallas kernels, per_device(): image_call(functools.partial(attend_kernel, head_size=head_size), images,...  30.3 us
    ppermute x18, starting transfers between devices, traded(): kept.append(lax.ppermute(send, mesh_axis, bit_swap(size, turn * stride)))  28.7 us
    ppermute x18, waiting for transfers between devices, traded(): kept.append(lax.ppermute(send, mesh_axis, bit_swap(size, turn * stride)))  21.2 us
    pallas_call x1, Pallas kernels, per_device(): image_call(branch_kernel, images, [per_image(slots, model_width), per_ima...  20.9 us
  transfers between devices with their start and end apart: 36, of which 17 were waited for; matrix products, arithmetic and copies ran while one was open for 11% of the time, Pallas kernels for 19%

profile of v3, /device:TPU:0, one launch (start us, length us, event | category | flops | bytes accessed | tf_op | source)
XLA Modules:
  0.0 539.9 jit_solution(12398287309087265479)
XLA Ops:
  17.2 87.8 %all-gather.3.cloned.1.call-done = bf16[11008,768]{1,0:T(8,128)(2,1)} async-done(((bf16[688,768]{1,0:T(8,128)(2,1)}), bf16[11008,768]{1,0:T(8,128)(2,1)}) %all-gather.3.cloned.1.call-update) | async-done | bytes 16908304 | tf_op jit(solution)/shard_map/all_gather | solution.py:737
  105.0 7.5 %fusion.59 = (bf16[16,48,768]{2,1,0:T(8,128)(2,1)S(1)}, bf16[16,48,768]{2,1,0:T(8,128)(2,1)}, bf16[16,48,768]{2,1,0:T(8,128)(2,1)}, bf16[16,48,768]{2,1,0:T(8,12...) fusion(bf16[16,688,768]{2,1,0:T(8,128)(2,1)} %bitcast.190), kind=kLoop, calls=%fused_computation.191 | loop fusion | bytes 21233664 | tf_op jit(solution)/shard_map/slice | solution.py:121
  114.8 5.5 %slice.313 = bf16[16,240,768]{2,1,0:T(8,128)(2,1)} slice(bf16[16,688,768]{2,1,0:T(8,128)(2,1)} %bitcast.192), slice={[0:16], [384:624], [0:768]} | slice | bytes 11796480 | tf_op jit(solution)/shard_map/slice | solution.py:119
  139.4 9.9 %embed.1 = (f32[6,208,768]{2,1,0:T(8,128)}, bf16[6,208,768]{2,1,0:T(8,128)(2,1)}) custom-call(s32[6]{0:T(128)} %reshape.364.counts_ref, bf16[6,208,768]{2,1,0:T(8,128)(2,1)} %pad.41.pixel_ref, s32[6,1,208]{2,1,0:T(1,128)} %pad.42.map_ref, f32[6,1,208]{2,1,0:T(1,128)} %get-tuple-element.268.row_ref, f32[6,208,1]{2,1,0:T(8,128)} %copy.67.column_ref, ...), custom_call_target="tpu_custom_call" | custom-call | flops 60000002048 | bytes 1000 | tf_op jit(solution)/shard_map/embed/pallas_call | solution.py:771
  149.3 32.1 %widen.1 = (bf16[3,1248,768]{2,1,0:T(8,128)(2,1)}, f32[2,1248,768]{2,1,0:T(8,128)}, bf16[4,1248,768]{2,1,0:T(8,128)(2,1)}, bf16[4,1248,768]{2,1,0:T(8,128)(2,1)}) custom-call(bf16[1248,768]{1,0:T(8,128)(2,1)} %bitcast.215, bf16[7,768,768]{2,1,0:T(8,128)(2,1)} %bitcast_dynamic-update-slice_fusion.wide_ref.wide_hbm, f32[2,1,768]{2,1,0:T(1,128)} %reshape.375.gain_ref, ...), custom_call_target="tpu_custom_call" | custom-call | tf_op jit(solution)/shard_map/widen/pallas_call | solution.py:792
  181.4 30.3 %attend.1 = (bf16[6,208,768]{2,1,0:T(8,128)(2,1)}, f32[6,208,768]{2,1,0:T(8,128)}, f32[6,1,768]{2,1,0:T(1,128)}) custom-call(s32[6]{0:T(128)} %reshape.364.counts_ref, bf16[3,1248,768]{2,1,0:T(8,128)(2,1)} %get-tuple-element.92.qkv_ref, bf16[4,1248,768]{2,1,0:T(8,128)(2,1)} %get-tuple-element.93.hidden_ref, f32[6,208,768]{2,1,0:T(8,128)} %get-tuple-element.94.merged_ref, ...), custom_call_target="tpu_custom_call" | custom-call | flops 60000002048 | bytes 1000 | tf_op jit(solution)/shard_map/attend/pallas_call | solution.py:825
  222.2 2.5 collective-permute-start.3
  233.9 20.9 %branch.1 = (f32[6,208,768]{2,1,0:T(8,128)}, bf16[6,208,768]{2,1,0:T(8,128)(2,1)}, bf16[6,208,768]{2,1,0:T(8,128)(2,1)}, bf16[4,1248,768]{2,1,0:T(8,128)(2,1)}, f32[8,768]{1,0:T(8,128)}) custom-call(s32[6]{0:T(128)} %reshape.364.counts_ref, f32[6,208,768]{2,1,0:T(8,128)} %get-tuple-element.97.stream_ref, f32[6,1,768]{2,1,0:T(1,128)} %reshape.383.grad_pooled_ref, ...), custom_call_target="tpu_custom_call" | custom-call | flops 60000002048 | bytes 1000 | tf_op jit(solution)/shard_map/branch/pallas_call | solution.py:894
  254.9 14.2 %narrow_grad.1 = (bf16[8,240,768]{2,1,0:T(8,128)(2,1)}, bf16[8,240,768]{2,1,0:T(8,128)(2,1)}) custom-call(s32[1]{0:T(128)} %bitcast.22.core_ref, bf16[1248,768]{1,0:T(8,128)(2,1)} %bitcast.234, bf16[4,1248,768]{2,1,0:T(8,128)(2,1)} %get-tuple-element.93.hidden_ref, bf16[1248,768]{1,0:T(8,128)(2,1)} %bitcast.235), custom_call_target="tpu_custom_call" | custom-call | flops 60000002048 | bytes 1000 | tf_op jit(solution)/shard_map/narrow_grad/pallas_call | solution.py:930
  269.1 11.5 %hidden_grad.1 = (bf16[8,240,768]{2,1,0:T(8,128)(2,1)}, bf16[8,240,768]{2,1,0:T(8,128)(2,1)}) custom-call(s32[1]{0:T(128)} %bitcast.22.core_ref, bf16[1248,768]{1,0:T(8,128)(2,1)} %bitcast.216, bf16[4,1248,768]{2,1,0:T(8,128)(2,1)} %get-tuple-element.105.grad_ref.grad_act_ref, bf16[16,768]{1,0:T(8,128)(2,1)} %pad.47.pooled_ref, bf16[16,768]{1,0:T(8,128)(2,1)} %pad.48.embeds_ref), custom_call_target="tpu_custom_call" | custom-call | flops 60000002048 | bytes 1000 | tf_op jit(solution)/shard_map/hidden_grad/pallas_call | solution.py:955
  285.6 3.1 constant_dynamic-slice_fusion
  290.3 2.6 copy.75.refs_0_
  294.3 13.4 %attend_back.3 = (bf16[3,416,768]{2,1,0:T(8,128)(2,1)}, f32[8,768]{1,0:T(8,128)}) custom-call(s32[6]{0:T(128)} %reshape.364.counts_ref, bf16[3,1248,768]{2,1,0:T(8,128)(2,1)} %get-tuple-element.92.qkv_ref, f32[2,1248,768]{2,1,0:T(8,128)} %get-tuple-element.102.rstd_ref, bf16[6,208,768]{2,1,0:T(8,128)(2,1)} %get-tuple-element.103.grad_attended_ref, ...), custom_call_target="tpu_custom_call" | custom-call | flops 60000002048 | bytes 1000 | tf_op jit(solution)/shard_map/attend_back/pallas_call | solution.py:995
  307.7 2.9 fusion.1.refs_1_
  310.6 13.2 %attend_back.4 = (bf16[3,416,768]{2,1,0:T(8,128)(2,1)}, f32[8,768]{1,0:T(8,128)}) custom-call(s32[6]{0:T(128)} %reshape.364.counts_ref, bf16[3,1248,768]{2,1,0:T(8,128)(2,1)} %get-tuple-element.92.qkv_ref, f32[2,1248,768]{2,1,0:T(8,128)} %get-tuple-element.102.rstd_ref, bf16[6,208,768]{2,1,0:T(8,128)(2,1)} %get-tuple-element.103.grad_attended_ref, ...), custom_call_target="tpu_custom_call" | custom-call | flops 60000002048 | bytes 1000 | tf_op jit(solution)/shard_map/attend_back/pallas_call | solution.py:995
  325.0 13.6 %attend_back.5 = (bf16[3,416,768]{2,1,0:T(8,128)(2,1)}, f32[8,768]{1,0:T(8,128)}) custom-call(s32[6]{0:T(128)} %reshape.364.counts_ref, bf16[3,1248,768]{2,1,0:T(8,128)(2,1)} %get-tuple-element.92.qkv_ref, f32[2,1248,768]{2,1,0:T(8,128)} %get-tuple-element.102.rstd_ref, bf16[6,208,768]{2,1,0:T(8,128)(2,1)} %get-tuple-element.103.grad_attended_ref, ...), custom_call_target="tpu_custom_call" | custom-call | flops 60000002048 | bytes 1000 | tf_op jit(solution)/shard_map/attend_back/pallas_call | solution.py:995
  346.3 9.8 %qkv_grad.1 = (bf16[8,144,768]{2,1,0:T(8,128)(2,1)}, bf16[8,144,768]{2,1,0:T(8,128)(2,1)}) custom-call(s32[1]{0:T(128)} %bitcast.22.core_ref, bf16[1248,768]{1,0:T(8,128)(2,1)} %bitcast.217, bf16[3,416,768]{2,1,0:T(8,128)(2,1)} %get-tuple-element.104.refs_0_.grad_qkv_ref, bf16[3,416,768]{2,1,0:T(8,128)(2,1)} %get-tuple-element.110.refs_0_.refs_1_.grad_qkv_ref, ...), custom_call_target="tpu_custom_call" | custom-call | flops 60000002048 | bytes 1000 | tf_op jit(solution)/shard_map/qkv_grad/pallas_call | solution.py:1016
  356.8 14.3 %merge_back.3 = (bf16[2,208,768]{2,1,0:T(8,128)(2,1)}, f32[208,768]{1,0:T(8,128)}, f32[8,768]{1,0:T(8,128)}) custom-call(s32[6]{0:T(128)} %reshape.364.counts_ref, bf16[3,416,768]{2,1,0:T(8,128)(2,1)} %get-tuple-element.104.refs_0_.grad_qkv_ref, bf16[4,1248,768]{2,1,0:T(8,128)(2,1)} %get-tuple-element.105.grad_ref.grad_act_ref, ...), custom_call_target="tpu_custom_call" | custom-call | flops 60000002048 | bytes 1000 | tf_op jit(solution)/shard_map/merge_back/pallas_call | solution.py:1038
  371.1 2.5 fusion.13
  385.4 14.5 %merge_back.4 = (bf16[2,208,768]{2,1,0:T(8,128)(2,1)}, f32[208,768]{1,0:T(8,128)}, f32[8,768]{1,0:T(8,128)}) custom-call(s32[6]{0:T(128)} %reshape.364.counts_ref, bf16[3,416,768]{2,1,0:T(8,128)(2,1)} %get-tuple-element.110.refs_0_.refs_1_.grad_qkv_ref, bf16[4,1248,768]{2,1,0:T(8,128)(2,1)} %get-tuple-element.105.grad_ref.grad_act_ref, ...), custom_call_target="tpu_custom_call" | custom-call | flops 60000002048 | bytes 1000 | tf_op jit(solution)/shard_map/merge_back/pallas_call | solution.py:1038
  402.7 14.4 %merge_back.5 = (bf16[2,208,768]{2,1,0:T(8,128)(2,1)}, f32[208,768]{1,0:T(8,128)}, f32[8,768]{1,0:T(8,128)}) custom-call(s32[6]{0:T(128)} %reshape.364.counts_ref, bf16[3,416,768]{2,1,0:T(8,128)(2,1)} %get-tuple-element.111.refs_2_.refs_3_.grad_qkv_ref, bf16[4,1248,768]{2,1,0:T(8,128)(2,1)} %get-tuple-element.105.grad_ref.grad_act_ref, ...), custom_call_target="tpu_custom_call" | custom-call | flops 60000002048 | bytes 1000 | tf_op jit(solution)/shard_map/merge_back/pallas_call | solution.py:1038
  425.1 6.3 %embed_grad.1 = (bf16[8,64,1024]{2,1,0:T(8,128)(2,1)}, bf16[8,64,1024]{2,1,0:T(8,128)(2,1)}) custom-call(s32[1]{0:T(128)} %bitcast.22.core_ref, bf16[1248,768]{1,0:T(8,128)(2,1)} %bitcast.214, bf16[416,768]{1,0:T(8,128)(2,1)} %bitcast.236, bf16[416,768]{1,0:T(8,128)(2,1)} %bitcast.237, bf16[416,768]{1,0:T(8,128)(2,1)} %bitcast.238, ...), custom_call_target="tpu_custom_call" | custom-call | flops 60000002048 | bytes 1000 | tf_op jit(solution)/shard_map/embed_grad/pallas_call | solution.py:1095
  432.0 3.3 collective-permute-start.12
  435.8 6.2 %collective-permute-done.11 = bf16[120,768]{1,0:T(8,128)(2,1)S(1)} collective-permute-done((bf16[120,768]{1,0:T(8,128)(2,1)S(1)}, bf16[120,768]{1,0:T(8,128)(2,1)S(1)}, u32[]{:S(2)}, u32[]{:S(2)}) %collective-permute-start.11) | collective-permute-done | bytes 184352 | tf_op jit(solution)/shard_map/ppermute | solution.py:488
  442.0 6.7 %collective-permute-done.12 = bf16[120,768]{1,0:T(8,128)(2,1)S(1)} collective-permute-done((bf16[120,768]{1,0:T(8,128)(2,1)S(1)}, bf16[120,768]{1,0:T(8,128)(2,1)S(1)}, u32[]{:S(2)}, u32[]{:S(2)}) %collective-permute-start.12) | collective-permute-done | bytes 184352 | tf_op jit(solution)/shard_map/ppermute | solution.py:488
  458.3 5.2 collective-permute-done.18
  466.5 4.1 collective-permute-start.21
  475.3 4.7 collective-permute-start.27
  485.0 6.3 %collective-permute-done.28 = bf16[64,1024]{1,0:T(8,128)(2,1)S(1)} collective-permute-done((bf16[64,1024]{1,0:T(8,128)(2,1)S(1)}, bf16[64,1024]{1,0:T(8,128)(2,1)S(1)}, u32[]{:S(2)}, u32[]{:S(2)}) %collective-permute-start.28) | collective-permute-done | bytes 131104 | tf_op jit(solution)/shard_map/ppermute | solution.py:488
  494.6 2.8 collective-permute-done.30
  502.2 3.6 collective-permute-done.32
  517.0 7.2 %update.1 = (f32[48,768]{1,0:T(8,128)}, f32[196,48]{1,0:T(8,128)}, f32[48,5376]{1,0:T(8,128)}, f32[240,768]{1,0:T(8,128)}, f32[48,768]{1,0:T(8,128)}, /*index=5*...) custom-call(f32[8,128]{1,0:T(8,128)} %copy-done.37, ...), custom_call_target="tpu_custom_call" | custom-call | tf_op jit(solution)/shard_map/update/pallas_call | solution.py:1150
  (323 shorter events, 138.3 us)
Async XLA Ops:
  7.3 97.7 %all-gather.3.cloned.1.call-start = ((), (), s32[]{:S(2)}) async-start(), calls=%async_computation | async-start | bytes 17965056 | tf_op jit(solution)/shard_map/all_gather | solution.py:737
  214.8 3.7 collective-permute-start.1
  218.5 3.7 collective-permute-start.2
  222.2 4.6 collective-permute-start.3
  269.0 16.6 %collective-permute-start.5 = (bf16[8,240,768]{2,1,0:T(8,128)(2,1)}, bf16[8,240,768]{2,1,0:T(8,128)(2,1)}, u32[]{:S(2)}, u32[]{:S(2)}) collective-permute-start(bf16[8,240,768]{2,1,0:T(8,128)(2,1)} %get-tuple-element.101), channel_id=1, source_target_pairs={{0,1},{1,0},{2,3},{3,2},{4,5},{5,4},{6,7},{7,6},{8,9},{9,8},{10,11... | collective-permute-start | bytes 8847368 | tf_op jit(solution)/shard_map/ppermute | solution.py:495
  280.6 27.1 %collective-permute-start.7 = (bf16[8,240,768]{2,1,0:T(8,128)(2,1)}, bf16[8,240,768]{2,1,0:T(8,128)(2,1)}, u32[]{:S(2)}, u32[]{:S(2)}) collective-permute-start(bf16[8,240,768]{2,1,0:T(8,128)(2,1)} %get-tuple-element.107), channel_id=1, source_target_pairs={{0,1},{1,0},{2,3},{3,2},{4,5},{5,4},{6,7},{7,6},{8,9},{9,8},{10,11... | collective-permute-start | bytes 8847368 | tf_op jit(solution)/shard_map/ppermute | solution.py:495
  292.8 51.2 %collective-permute-start.6 = (bf16[4,2,120,768]{3,2,0,1:T(8,128)(2,1)}, bf16[4,2,120,768]{3,2,0,1:T(8,128)(2,1)}, u32[]{:S(2)}, u32[]{:S(2)}) collective-permute-start(bf16[4,2,120,768]{3,2,0,1:T(8,128)(2,1)} %fusion), channel_id=1, source_target_pairs={{0,16},{16,0},{1,17},{17,1},{2,18},{18,2},{3,19},{19,3},{4,20},{20... | collective-permute-start | bytes 4423688 | tf_op jit(solution)/shard_map/ppermute | solution.py:488
  323.8 47.3 %collective-permute-start.9 = (bf16[4,240,768]{2,1,0:T(8,128)(2,1)}, bf16[4,240,768]{2,1,0:T(8,128)(2,1)}, u32[]{:S(2)}, u32[]{:S(2)}) collective-permute-start(bf16[4,240,768]{2,1,0:T(8,128)(2,1)} %fusion.1.refs_1_), channel_id=1, source_target_pairs={{0,2},{1,3},{2,0},{3,1},{4,6},{5,7},{6,4},{7,5},{8,10},{9,11},{10,... | collective-permute-start | bytes 4423688 | tf_op jit(solution)/shard_map/ppermute | solution.py:488
  356.1 44.4 %collective-permute-start.8 = (bf16[4,120,768]{2,1,0:T(8,128)(2,1)}, bf16[4,120,768]{2,1,0:T(8,128)(2,1)}, u32[]{:S(2)}, u32[]{:S(2)}) collective-permute-start(bf16[4,120,768]{2,1,0:T(8,128)(2,1)} %fusion.6.refs_4_), channel_id=1, source_target_pairs={{0,2},{1,3},{2,0},{3,1},{4,6},{5,7},{6,4},{7,5},{8,10},{9,11},{10,... | collective-permute-start | bytes 2211848 | tf_op jit(solution)/shard_map/ppermute | solution.py:488
  356.8 25.9 %collective-permute-start.10 = (bf16[8,144,768]{2,1,0:T(8,128)(2,1)}, bf16[8,144,768]{2,1,0:T(8,128)(2,1)}, u32[]{:S(2)}, u32[]{:S(2)}) collective-permute-start(bf16[8,144,768]{2,1,0:T(8,128)(2,1)} %get-tuple-element.116.refs_0_), channel_id=1, source_target_pairs={{0,1},{1,0},{2,3},{3,2},{4,5},{5,4},{6,7},{7,6},{8,9},{9,8},{10,11... | collective-permute-start | bytes 5308424 | tf_op jit(solution)/shard_map/ppermute | solution.py:495
  373.6 44.6 %collective-permute-start.15 = (bf16[240,768]{1,0:T(8,128)(2,1)}, bf16[240,768]{1,0:T(8,128)(2,1)}, u32[]{:S(2)}, u32[]{:S(2)}) collective-permute-start(bf16[240,768]{1,0:T(8,128)(2,1)} %get-tuple-element.233.refs_1_), channel_id=1, source_target_pairs={{0,4},{1,5},{2,6},{3,7},{4,0},{5,1},{6,2},{7,3},{8,12},{9,13},{10,... | collective-permute-start | bytes 1105928 | tf_op jit(solution)/shard_map/ppermute | solution.py:488
  375.1 43.1 %collective-permute-start.16 = (bf16[240,768]{1,0:T(8,128)(2,1)}, bf16[240,768]{1,0:T(8,128)(2,1)}, u32[]{:S(2)}, u32[]{:S(2)}) collective-permute-start(bf16[240,768]{1,0:T(8,128)(2,1)} %get-tuple-element.232.refs_2_), channel_id=1, source_target_pairs={{0,8},{1,9},{2,10},{3,11},{4,12},{5,13},{6,14},{7,15},{8,0},{9,1},... | collective-permute-start | bytes 1105928 | tf_op jit(solution)/shard_map/ppermute | solution.py:488
  377.6 40.7 %collective-permute-start.17 = (bf16[240,768]{1,0:T(8,128)(2,1)}, bf16[240,768]{1,0:T(8,128)(2,1)}, u32[]{:S(2)}, u32[]{:S(2)}) collective-permute-start(bf16[240,768]{1,0:T(8,128)(2,1)} %get-tuple-element.231.refs_3_), channel_id=1, source_target_pairs={{0,12},{1,13},{2,14},{3,15},{4,8},{5,9},{6,10},{7,11},{8,4},{9,5},... | collective-permute-start | bytes 1105928 | tf_op jit(solution)/shard_map/ppermute | solution.py:488
  399.9 23.3 %collective-permute-start.19 = (bf16[4,2,72,768]{3,2,1,0:T(8,128)(2,1)}, bf16[4,2,72,768]{3,2,1,0:T(8,128)(2,1)}, u32[]{:S(2)}, u32[]{:S(2)}) collective-permute-start(bf16[4,2,72,768]{3,2,1,0:T(8,128)(2,1)} %fusion.5.refs_4_), channel_id=1, source_target_pairs={{0,16},{16,0},{1,17},{17,1},{2,18},{18,2},{3,19},{19,3},{4,20},{20... | collective-permute-start | bytes 2654216 | tf_op jit(solution)/shard_map/ppermute | solution.py:488
  431.4 21.6 %collective-permute-start.25 = (bf16[8,64,1024]{2,1,0:T(8,128)(2,1)}, bf16[8,64,1024]{2,1,0:T(8,128)(2,1)}, u32[]{:S(2)}, u32[]{:S(2)}) collective-permute-start(bf16[8,64,1024]{2,1,0:T(8,128)(2,1)} %get-tuple-element.150), channel_id=1, source_target_pairs={{0,1},{1,0},{2,3},{3,2},{4,5},{5,4},{6,7},{7,6},{8,9},{9,8},{10,11... | collective-permute-start | bytes 3145736 | tf_op jit(solution)/shard_map/ppermute | solution.py:495
  431.4 10.6 %collective-permute-start.11 = (bf16[120,768]{1,0:T(8,128)(2,1)S(1)}, bf16[120,768]{1,0:T(8,128)(2,1)S(1)}, u32[]{:S(2)}, u32[]{:S(2)}) collective-permute-start(bf16[120,768]{1,0:T(8,128)(2,1)S(1)} %copy-done.30), channel_id=1, source_target_pairs={{0,4},{1,5},{2,6},{3,7},{4,0},{5,1},{6,2},{7,3},{8,12},{9,13},{10,... | collective-permute-start | bytes 552968 | tf_op jit(solution)/shard_map/ppermute | solution.py:488
  432.0 16.7 %collective-permute-start.12 = (bf16[120,768]{1,0:T(8,128)(2,1)S(1)}, bf16[120,768]{1,0:T(8,128)(2,1)S(1)}, u32[]{:S(2)}, u32[]{:S(2)}) collective-permute-start(bf16[120,768]{1,0:T(8,128)(2,1)S(1)} %copy-done.29), channel_id=1, source_target_pairs={{0,8},{1,9},{2,10},{3,11},{4,12},{5,13},{6,14},{7,15},{8,0},{9,1},... | collective-permute-start | bytes 552968 | tf_op jit(solution)/shard_map/ppermute | solution.py:488
  435.3 13.4 %collective-permute-start.13 = (bf16[120,768]{1,0:T(8,128)(2,1)S(1)}, bf16[120,768]{1,0:T(8,128)(2,1)S(1)}, u32[]{:S(2)}, u32[]{:S(2)}) collective-permute-start(bf16[120,768]{1,0:T(8,128)(2,1)S(1)} %copy-done.28), channel_id=1, source_target_pairs={{0,12},{1,13},{2,14},{3,15},{4,8},{5,9},{6,10},{7,11},{8,4},{9,5},... | collective-permute-start | bytes 552968 | tf_op jit(solution)/shard_map/ppermute | solution.py:488
  449.9 7.6 %collective-permute-start.14 = (bf16[120,768]{1,0:T(8,128)(2,1)S(1)}, bf16[120,768]{1,0:T(8,128)(2,1)S(1)}, u32[]{:S(2)}, u32[]{:S(2)}) collective-permute-start(bf16[120,768]{1,0:T(8,128)(2,1)S(1)} %fusion.16), channel_id=1, source_target_pairs={{0,16},{16,0},{1,17},{17,1},{2,18},{18,2},{3,19},{19,3},{4,20},{20... | collective-permute-start | bytes 552968 | tf_op jit(solution)/shard_map/ppermute | solution.py:500
  451.4 12.1 %collective-permute-start.18 = (bf16[240,768]{1,0:T(8,128)(2,1)}, bf16[240,768]{1,0:T(8,128)(2,1)S(1)}, u32[]{:S(2)}, u32[]{:S(2)}) collective-permute-start(bf16[240,768]{1,0:T(8,128)(2,1)} %add_convert_fusion.7.refs_8_), channel_id=1, source_target_pairs={{0,16},{16,0},{1,17},{17,1},{2,18},{18,2},{3,19},{19,3},{4,20},{20... | collective-permute-start | bytes 1105928 | tf_op jit(solution)/shard_map/ppermute | solution.py:500
  452.0 13.3 %collective-permute-start.20 = (bf16[4,72,768]{2,1,0:T(8,128)(2,1)}, bf16[4,72,768]{2,1,0:T(8,128)(2,1)S(1)}, u32[]{:S(2)}, u32[]{:S(2)}) collective-permute-start(bf16[4,72,768]{2,1,0:T(8,128)(2,1)} %fusion.10.refs_9_), channel_id=1, source_target_pairs={{0,2},{1,3},{2,0},{3,1},{4,6},{5,7},{6,4},{7,5},{8,10},{9,11},{10,... | collective-permute-start | bytes 1327112 | tf_op jit(solution)/shard_map/ppermute | solution.py:488
  454.4 19.7 %collective-permute-start.26 = (bf16[4,64,1024]{2,1,0:T(8,128)(2,1)S(1)}, bf16[4,64,1024]{2,1,0:T(8,128)(2,1)S(1)}, u32[]{:S(2)}, u32[]{:S(2)}) collective-permute-start(bf16[4,64,1024]{2,1,0:T(8,128)(2,1)S(1)} %fusion.9), channel_id=1, source_target_pairs={{0,2},{1,3},{2,0},{3,1},{4,6},{5,7},{6,4},{7,5},{8,10},{9,11},{10,... | collective-permute-start | bytes 1572872 | tf_op jit(solution)/shard_map/ppermute | solution.py:488
  466.5 14.5 %collective-permute-start.21 = (bf16[72,768]{1,0:T(8,128)(2,1)S(1)}, bf16[72,768]{1,0:T(8,128)(2,1)S(1)}, u32[]{:S(2)}, u32[]{:S(2)}) collective-permute-start(bf16[72,768]{1,0:T(8,128)(2,1)S(1)} %get-tuple-element.234), channel_id=1, source_target_pairs={{0,4},{1,5},{2,6},{3,7},{4,0},{5,1},{6,2},{7,3},{8,12},{9,13},{10,... | collective-permute-start | bytes 331784 | tf_op jit(solution)/shard_map/ppermute | solution.py:488
  470.6 11.8 %collective-permute-start.22 = (bf16[72,768]{1,0:T(8,128)(2,1)S(1)}, bf16[72,768]{1,0:T(8,128)(2,1)S(1)}, u32[]{:S(2)}, u32[]{:S(2)}) collective-permute-start(bf16[72,768]{1,0:T(8,128)(2,1)S(1)} %get-tuple-element.236), channel_id=1, source_target_pairs={{0,8},{1,9},{2,10},{3,11},{4,12},{5,13},{6,14},{7,15},{8,0},{9,1},... | collective-permute-start | bytes 331784 | tf_op jit(solution)/shard_map/ppermute | solution.py:488
  471.7 10.7 %collective-permute-start.23 = (bf16[72,768]{1,0:T(8,128)(2,1)S(1)}, bf16[72,768]{1,0:T(8,128)(2,1)S(1)}, u32[]{:S(2)}, u32[]{:S(2)}) collective-permute-start(bf16[72,768]{1,0:T(8,128)(2,1)S(1)} %get-tuple-element.235), channel_id=1, source_target_pairs={{0,12},{1,13},{2,14},{3,15},{4,8},{5,9},{6,10},{7,11},{8,4},{9,5},... | collective-permute-start | bytes 331784 | tf_op jit(solution)/shard_map/ppermute | solution.py:488
  475.3 9.7 %collective-permute-start.27 = (bf16[64,1024]{1,0:T(8,128)(2,1)S(1)}, bf16[64,1024]{1,0:T(8,128)(2,1)S(1)}, u32[]{:S(2)}, u32[]{:S(2)}) collective-permute-start(bf16[64,1024]{1,0:T(8,128)(2,1)S(1)} %get-tuple-element.244), channel_id=1, source_target_pairs={{0,4},{1,5},{2,6},{3,7},{4,0},{5,1},{6,2},{7,3},{8,12},{9,13},{10,... | collective-permute-start | bytes 393224 | tf_op jit(solution)/shard_map/ppermute | solution.py:488
  480.0 11.3 %collective-permute-start.28 = (bf16[64,1024]{1,0:T(8,128)(2,1)S(1)}, bf16[64,1024]{1,0:T(8,128)(2,1)S(1)}, u32[]{:S(2)}, u32[]{:S(2)}) collective-permute-start(bf16[64,1024]{1,0:T(8,128)(2,1)S(1)} %get-tuple-element.246), channel_id=1, source_target_pairs={{0,8},{1,9},{2,10},{3,11},{4,12},{5,13},{6,14},{7,15},{8,0},{9,1},... | collective-permute-start | bytes 393224 | tf_op jit(solution)/shard_map/ppermute | solution.py:488
  481.0 10.3 %collective-permute-start.29 = (bf16[64,1024]{1,0:T(8,128)(2,1)S(1)}, bf16[64,1024]{1,0:T(8,128)(2,1)S(1)}, u32[]{:S(2)}, u32[]{:S(2)}) collective-permute-start(bf16[64,1024]{1,0:T(8,128)(2,1)S(1)} %get-tuple-element.245), channel_id=1, source_target_pairs={{0,12},{1,13},{2,14},{3,15},{4,8},{5,9},{6,10},{7,11},{8,4},{9,5},... | collective-permute-start | bytes 393224 | tf_op jit(solution)/shard_map/ppermute | solution.py:488
  483.4 10.5 %collective-permute-start.24 = (bf16[72,768]{1,0:T(8,128)(2,1)S(1)}, bf16[72,768]{1,0:T(8,128)(2,1)S(1)}, u32[]{:S(2)}, u32[]{:S(2)}) collective-permute-start(bf16[72,768]{1,0:T(8,128)(2,1)S(1)} %fusion.30), channel_id=1, source_target_pairs={{0,16},{16,0},{1,17},{17,1},{2,18},{18,2},{3,19},{19,3},{4,20},{20... | collective-permute-start | bytes 331784 | tf_op jit(solution)/shard_map/ppermute | solution.py:500
  492.4 5.0 collective-permute-start.30
  505.7 6.1 %collective-permute-start.33 = (f32[8,128]{1,0:T(8,128)S(1)}, f32[8,128]{1,0:T(8,128)S(1)}, u32[]{:S(2)}, u32[]{:S(2)}) collective-permute-start(f32[8,128]{1,0:T(8,128)S(1)} %add.657), channel_id=1, source_target_pairs={{0,4},{1,5},{2,6},{3,7},{4,0},{5,1},{6,2},{7,3},{8,12},{9,13},{10,... | collective-permute-start | bytes 12296 | tf_op jit(solution)/shard_map/ppermute | solution.py:89
  511.9 4.5 collective-permute-start.34
  (57 other events, 632.3 us)
Sparse Core Ops, SparseCore 0:
  12.6 92.3 all-gather.2

commit v4 on v3

--- a/solution.py
+++ b/solution.py
@@ -91,46 +91,6 @@
     return value
 
 
-def pack_weights(embedder, positions, widener, narrower, projector, scales, biases):
-    model_width = embedder.shape[1]
-    blocks = widener.shape[1] // model_width
-    rows = [embedder]
-    rows += [widener[:, k * model_width : (k + 1) * model_width] for k in range(blocks)]
-    rows += [narrower, projector]
-    small = jnp.concatenate([positions.reshape(-1), scales.reshape(-1), biases.reshape(-1)])
-    small_rows = -(-small.shape[0] // (16 * model_width)) * 16
-    small = jnp.pad(small, (0, small_rows * model_width - small.shape[0]))
-    rows.append(small.reshape(small_rows, model_width))
-    return jnp.concatenate(rows, axis=0)
-
-
-def unpack_weights(full, shapes):
-    owners, _, width = full.shape
-    (e_rows, _), (slots, p_cols), (w_rows, w_cols), (n_rows, _), (j_rows, _), (s_rows, s_cols), (
-        b_len,
-    ) = shapes
-    at = 0
-    embed = full[:, at : at + e_rows].reshape(owners * e_rows, width)
-    at += e_rows
-    wide = []
-    for _ in range(w_cols // width):
-        wide.append(full[:, at : at + w_rows].reshape(owners * w_rows, width))
-        at += w_rows
-    narrow = full[:, at : at + n_rows].reshape(owners * n_rows, width)
-    at += n_rows
-    project = full[:, at : at + j_rows].reshape(owners * j_rows, width)
-    at += j_rows
-    small = full[:, at:].reshape(owners, -1)
-    place = small[:, : slots * p_cols].reshape(owners, slots, p_cols)
-    place = jnp.swapaxes(place, 0, 1).reshape(slots, owners * p_cols)
-    at = slots * p_cols
-    scale = small[:, at : at + s_rows * s_cols].reshape(owners, s_rows, s_cols)
-    scale = jnp.swapaxes(scale, 0, 1).reshape(s_rows, owners * s_cols)
-    at += s_rows * s_cols
-    bias = small[:, at : at + b_len].reshape(owners * b_len)
-    return embed, place, wide, narrow, project, scale, bias
-
-
 def padded_rows(rows):
     return -(-rows // 16) * 16
 
@@ -161,9 +121,9 @@
 
 
 def embed_kernel(
-    counts_ref, pixel_ref, map_ref, row_ref, column_ref, embed_ref, place_ref, gain_ref,
-    merged_ref, normed_ref,
+    counts_ref, pixel_ref, map_ref, row_ref, column_ref, embed_ref, place_ref, gain_ref, *refs
 ):
+    merged_ref, normed_ref = refs[-2:]
     live_count = counts_ref[pl.program_id(0)]
     slots = merged_ref.shape[1]
     patches = product(pixel_ref[0], embed_ref[...]) + place_ref[...]
@@ -198,61 +158,65 @@
     return values * share, share + values * (bell * 0.3989422804014327)
 
 
-def widen_kernel(
-    normed_ref, wide_ref, gain_ref, bias_ref, qkv_ref, rstd_ref, hidden_ref, slope_ref, *, chunk,
-    head_size,
+def widen_heads_kernel(
+    place_ref, normed_ref, gain_ref, *refs, found, chunk, head_size
 ):
+    heads_ref, rstd_ref, wide_hbm, held_ref, sem, out_sem = refs[-6:]
+    sources = refs[: len(found)]
     step = pl.program_id(0)
+    keep = pltpu.make_async_copy(held_ref, wide_hbm, out_sem)
+
+    @pl.when(step == 0)
+    def _():
+        fetch(place_ref, sources, found, held_ref, sem)
+        fetched(place_ref, sources, found, held_ref, sem)
+        keep.start()
+
     chunks = normed_ref.shape[0] // chunk
-
-    def rows_of(index):
-        return pl.ds(pl.multiple_of(index * chunk, chunk), chunk)
-
-    @pl.when(step < 2)
+    mixer = head_mixer(head_size)
+    gain = gain_ref[0]
+    for index in range(chunks):
+        rows = slice(index * chunk, (index + 1) * chunk)
+        values = product(normed_ref[rows, :], held_ref[step])
+        center = values - head_mean(values, mixer)
+        rstd = lax.rsqrt(head_mean(center * center, mixer) + norm_eps)
+        rstd_ref[0, rows, :] = rstd
+        heads_ref[0, rows, :] = (center * rstd * gain).astype(jnp.bfloat16)
+
+    pl.when(step == pl.num_programs(0) - 1)(keep.wait)
+
+
+def widen_value_kernel(normed_ref, wide_ref, *refs):
+    values_ref = refs[-1]
+    values_ref[0] = product(normed_ref[...], wide_ref[0]).astype(jnp.bfloat16)
+
+
+def widen_hidden_kernel(place_ref, normed_ref, bias_ref, *refs, found, chunk):
+    hidden_ref, slope_ref, wide_hbm, held_ref, sem, out_sem = refs[-6:]
+    sources = refs[: len(found)]
+    step = pl.program_id(0)
+    keep = pltpu.make_async_copy(held_ref, wide_hbm, out_sem)
+
+    @pl.when(step == 0)
     def _():
-        mixer = head_mixer(head_size)
-        gain = gain_ref[0]
-
-        @pl.loop(0, chunks, unroll=True)
-        def _(index):
-            rows = rows_of(index)
-            values = product(normed_ref[rows, :], wide_ref[0])
-            center = values - head_mean(values, mixer)
-            rstd = lax.rsqrt(head_mean(center * center, mixer) + norm_eps)
-            rstd_ref[0, rows, :] = rstd
-            qkv_ref[0, rows, :] = (center * rstd * gain).astype(jnp.bfloat16)
-
-    @pl.when(step == 2)
-    def _():
-        @pl.loop(0, chunks, unroll=True)
-        def _(index):
-            rows = rows_of(index)
-            qkv_ref[0, rows, :] = product(normed_ref[rows, :], wide_ref[0]).astype(jnp.bfloat16)
-
-    @pl.when(step > 2)
-    def _():
-        @pl.loop(0, chunks, unroll=True)
-        def _(index):
-            rows = rows_of(index)
-            values = product(normed_ref[rows, :], wide_ref[0]) + bias_ref[0]
-            hidden, slope = gelu_pair(values)
-            hidden_ref[0, rows, :] = hidden.astype(jnp.bfloat16)
-            slope_ref[0, rows, :] = slope.astype(jnp.bfloat16)
-
-
-def attend_kernel(
-    counts_ref, qkv_ref, hidden_ref, merged_ref, narrow_hbm, bias_ref, gain_ref,
-    attended_ref, stream_ref, pooled_ref, narrow_ref, sem, *, head_size,
-):
-    image = pl.program_id(0)
-    live_count = counts_ref[image]
-    slots, width = merged_ref.shape[1:]
-    copy = pltpu.make_async_copy(narrow_hbm, narrow_ref, sem)
-
-    @pl.when(image == 0)
-    def _():
-        copy.start()
-
+        fetch(place_ref, sources, found, held_ref, sem)
+        fetched(place_ref, sources, found, held_ref, sem)
+        keep.start()
+
+    for index in range(normed_ref.shape[0] // chunk):
+        rows = slice(index * chunk, (index + 1) * chunk)
+        values = product(normed_ref[rows, :], held_ref[step]) + bias_ref[0]
+        hidden, slope = gelu_pair(values)
+        hidden_ref[0, rows, :] = hidden.astype(jnp.bfloat16)
+        slope_ref[0, rows, :] = slope.astype(jnp.bfloat16)
+
+    pl.when(step == pl.num_programs(0) - 1)(keep.wait)
+
+
+def attend_kernel(counts_ref, heads_ref, values_ref, *refs, head_size):
+    attended_ref = refs[-1]
+    live_count = counts_ref[pl.program_id(0)]
+    slots, width = attended_ref.shape[1:]
     factor = head_size ** (-0.5) * 1.4426950408889634
     key_live = jnp.where(
         lax.broadcasted_iota(jnp.int32, (1, slots), 1) < live_count, 1.0, 0.0
@@ -261,7 +225,8 @@
     zero = jnp.zeros((slots, 2 * head_size), jnp.bfloat16)
     for at in range(0, width, 2 * head_size):
         columns = slice(at, at + 2 * head_size)
-        queries, keys, values = (qkv_ref[part, :, columns] for part in range(3))
+        queries, keys = (heads_ref[part, :, columns] for part in range(2))
+        values = values_ref[0, :, columns]
         outs = []
         for half in range(2):
             own = jnp.where(first_half, queries, zero) if half == 0 else jnp.where(first_half, zero, queries)
@@ -270,20 +235,34 @@
             outs.append(product(share.astype(jnp.bfloat16), values))
         attended_ref[0, :, columns] = jnp.where(first_half, outs[0], outs[1]).astype(jnp.bfloat16)
 
+
+def join_kernel(
+    counts_ref, place_ref, attended_ref, hidden_ref, merged_ref, bias_ref, gain_ref, *refs, found
+):
+    stream_ref, pooled_ref, narrow_hbm, held_ref, sem, out_sem = refs[-6:]
+    sources = refs[: len(found)]
+    image = pl.program_id(0)
+    live_count = counts_ref[image]
+    slots, width = merged_ref.shape[1:]
+    keep = pltpu.make_async_copy(held_ref, narrow_hbm, out_sem)
+
     @pl.when(image == 0)
     def _():
-        copy.wait()
-
-    stream = merged_ref[0] + bias_ref[...] + product(attended_ref[0], narrow_ref[:width, :])
-    for part in range(hidden_ref.shape[0]):
-        stream = stream + product(
-            hidden_ref[part], narrow_ref[(part + 1) * width : (part + 2) * width, :]
-        )
+        fetch(place_ref, sources, found, held_ref, sem)
+        fetched(place_ref, sources, found, held_ref, sem)
+        keep.start()
+
+    stream = merged_ref[0] + bias_ref[...]
+    for k in range(1 + hidden_ref.shape[0]):
+        left = attended_ref[0] if k == 0 else hidden_ref[k - 1]
+        stream = stream + product(left, held_ref[0, k * width : (k + 1) * width, :])
     stream_ref[0] = stream
     unit, _ = normal_rows(stream)
     live = lax.broadcasted_iota(jnp.int32, (slots, 1), 0) < live_count
     total = jnp.sum(jnp.where(live, unit, 0.0), axis=0, keepdims=True)
     pooled_ref[0] = total * gain_ref[...] / live_count.astype(jnp.float32)
+
+    pl.when(image == pl.num_programs(0) - 1)(keep.wait)
 
 
 def branch_kernel(
@@ -330,7 +309,7 @@
 
 
 def attend_back_kernel(
-    counts_ref, qkv_ref, rstd_ref, grad_attended_ref, gain_ref, *refs, base, head_size
+    counts_ref, heads_ref, values_ref, rstd_ref, grad_attended_ref, gain_ref, *refs, base, head_size
 ):
     grad_qkv_ref, sums_ref, grad_ref = refs[-3:]
     image = pl.program_id(0)
@@ -347,7 +326,8 @@
     zero = jnp.zeros((slots, 2 * head_size), jnp.bfloat16)
     for at in range(0, width, 2 * head_size):
         columns = slice(at, at + 2 * head_size)
-        queries, keys, values = (qkv_ref[part, :, columns] for part in range(3))
+        queries, keys = (heads_ref[part, :, columns] for part in range(2))
+        values = values_ref[0, :, columns]
         above = grad_attended_ref[0, :, columns]
         grad_queries, grad_keys, grad_values = [], [], []
         for half in range(2):
@@ -369,7 +349,7 @@
     for part in range(2):
         gain = gain_ref[part]
         above = grad_ref[part]
-        unit = qkv_ref[part].astype(jnp.float32) / gain
+        unit = heads_ref[part].astype(jnp.float32) / gain
         sums_ref[part : part + 1, :] += jnp.sum(above * unit, axis=0, keepdims=True)
         slanted = above * gain
         back = slanted - head_mean(slanted, mixer) - unit * head_mean(slanted * unit, mixer)
@@ -377,7 +357,7 @@
 
 
 def merge_back_kernel(
-    counts_ref, grad_qkv_ref, grad_act_ref, wide_hbm, merged_ref, grad_stream_ref, gain_ref,
+    counts_ref, grad_qkv_ref, grad_act_ref, wide_hbm, wide_hidden_hbm, merged_ref, grad_stream_ref, gain_ref,
     map_ref, row_ref, column_ref, *refs, base,
 ):
     grad_patch_ref, grad_place_ref, sums_ref, wide_ref, sem = refs[-5:]
@@ -386,7 +366,11 @@
     slots, width = merged_ref.shape[1:]
     blocks = wide_ref.shape[0]
     copies = [
-        pltpu.make_async_copy(wide_hbm.at[part], wide_ref.at[part], sem.at[part])
+        pltpu.make_async_copy(
+            wide_hbm.at[part] if part < 3 else wide_hidden_hbm.at[part - 3],
+            wide_ref.at[part],
+            sem.at[part],
+        )
         for part in range(blocks)
     ]
 
@@ -537,6 +521,164 @@
     return lax.psum(own, "rep")
 
 
+def core_swap(own):
+    return lax.ppermute(own, "fsdp", bit_swap(lax.axis_size("fsdp"), 1))
+
+
+def middle_swap(own):
+    return lax.ppermute(own, "fsdp", bit_swap(lax.axis_size("fsdp"), 2))
+
+
+def high_gather(own):
+    owners = lax.axis_size("fsdp")
+    after = yield [own]
+    got = [lax.ppermute(own, "fsdp", bit_swap(owners, turn)) for turn in range(4, owners, 4)]
+    return [own] + behind(got, after)
+
+
+def with_cores(found):
+    after = yield [item[0] for item in found]
+    got = behind([core_swap(item[0]) for item in found], after)
+    return found + [
+        (array, [turn + 1 for turn in turns], parts)
+        for array, (_, turns, parts) in zip(got, found, strict=True)
+    ]
+
+
+def gather_plain(own):
+    after_high = yield from high_gather(own)
+    near = jnp.stack(after_high)
+    turns = list(range(0, lax.axis_size("fsdp"), 4))
+    after = yield [near]
+    far = behind([middle_swap(near)], after)[0]
+    whole_rows = [None] * len(turns)
+    found = [(near, turns, whole_rows), (far, [turn + 2 for turn in turns], whole_rows)]
+    return (yield from with_cores(found))
+
+
+def own_columns(own):
+    half = own.shape[-1] // 2
+    return lax.dynamic_slice_in_dim(own, lax.axis_index("rep") * half, half, own.ndim - 1)
+
+
+def gather_split(own):
+    if lax.axis_size("rep") != 2:
+        return (yield from gather_plain(own))
+    after_high = yield from high_gather(own_columns(own))
+    turns = list(range(0, lax.axis_size("fsdp"), 4))
+    cut = len(turns) // 2
+    early, late = jnp.stack(after_high[:cut]), jnp.stack(after_high[cut:])
+    after = yield [early, late]
+    got = behind([rep_swap(early), middle_swap(late)], after)
+    early, late = (jnp.concatenate(pair) for pair in zip((early, late), got, strict=True))
+    after = yield [early, late]
+    got = [middle_swap(early), rep_swap(late)]
+    early, late, *got = behind([early, late, *got], after if after is not None else ())
+    far = lambda some: [turn + 2 for turn in some]
+    first, second = turns[:cut], turns[cut:]
+    near_parts, all_parts = [0] * cut + [1] * cut, [0] * (2 * cut)
+    found = [
+        (early, first + first, near_parts),
+        (got[0], far(first + first), near_parts),
+        (late, second + far(second), all_parts),
+        (got[1], second + far(second), [1] * (2 * cut)),
+    ]
+    return (yield from with_cores(found))
+
+
+def assemble_copies(place_ref, sources, found, out_ref, columns, sem):
+    copies = []
+    for source, (turns, parts) in zip(sources, found, strict=True):
+        rows, width = source.shape[2:]
+        for slot, (turn, part) in enumerate(zip(turns, parts, strict=True)):
+            owner = place_ref[0] ^ turn
+            row = pl.ds(pl.multiple_of(owner * rows, rows), rows)
+            if part is None:
+                piece, target = source.at[slot, :, :, columns], out_ref.at[:, row, :]
+            else:
+                side = pl.ds(pl.multiple_of((place_ref[1] ^ part) * width, width), width)
+                piece, target = source.at[slot], out_ref.at[:, row, side]
+            copies.append(pltpu.make_async_copy(piece, target, sem.at[len(copies)]))
+    return copies
+
+
+def gathered(items):
+    arrays = [item[0] for item in items]
+    found = tuple((tuple(item[1]), tuple(item[2])) for item in items)
+    segments, rows, width = arrays[0].shape[1:]
+    if found[0][1][0] is not None:
+        width = 2 * width
+    owners = sum(len(item[0]) for item in found) * arrays[0].shape[3] // width
+    return arrays, found, (segments, owners * rows, width)
+
+
+def gather_scratch(found, size):
+    return [
+        pltpu.VMEM(size, jnp.bfloat16),
+        pltpu.SemaphoreType.DMA((sum(len(item[0]) for item in found),)),
+        pltpu.SemaphoreType.DMA,
+    ]
+
+
+def fetch(place_ref, sources, found, held_ref, sem):
+    for copy in assemble_copies(place_ref, sources, found, held_ref, slice(None), sem):
+        copy.start()
+
+
+def fetched(place_ref, sources, found, held_ref, sem):
+    for copy in assemble_copies(place_ref, sources, found, held_ref, slice(None), sem):
+        copy.wait()
+
+
+def assemble_small_kernel(place_ref, *refs, found, width):
+    embed_ref, beside_out_ref, beside_ref, sem, beside_sem = refs[-5:]
+    sources = refs[: len(found)]
+    first = slice(0, width)
+    second = slice(width, sources[0].shape[3])
+    copies = assemble_copies(place_ref, sources, found, embed_ref, first, sem)
+    copies += assemble_copies(place_ref, sources, found, beside_ref, second, beside_sem)
+    for copy in copies:
+        copy.start()
+    for copy in copies:
+        copy.wait()
+    beside_out_ref[...] = beside_ref[0].astype(jnp.float32).T
+
+
+def assembled_small(place, items, owners, width, guards):
+    arrays, found, _ = gathered(items)
+    rows, whole_width = arrays[0].shape[2:]
+    beside = whole_width - width
+    count = sum(len(item[0]) for item in found)
+    embed, table = pl.pallas_call(
+        lambda place_ref, *refs: assemble_small_kernel(
+            place_ref, *refs[: len(arrays)], *refs[-5:], found=found, width=width
+        ),
+        grid_spec=pltpu.PrefetchScalarGridSpec(
+            num_scalar_prefetch=1,
+            grid=(1,),
+            in_specs=[anywhere] * (len(arrays) + len(guards)),
+            out_specs=[whole(1, owners * rows, width), whole(beside, owners * rows)],
+            scratch_shapes=[
+                pltpu.VMEM((1, owners * rows, beside), jnp.bfloat16),
+                pltpu.SemaphoreType.DMA((count,)),
+                pltpu.SemaphoreType.DMA((count,)),
+            ],
+        ),
+        out_shape=[
+            jax.ShapeDtypeStruct((1, owners * rows, width), jnp.bfloat16),
+            jax.ShapeDtypeStruct((beside, owners * rows), jnp.float32),
+        ],
+        compiler_params=roomy,
+        cost_estimate=long,
+        name="assemble_small",
+    )(place, *arrays, *guards)
+    return embed[0], table
+
+
+def first_behind(value, after):
+    return lax.optimization_barrier((value, after))[0]
+
+
 class Flow:
     def __init__(self, steps):
         self.steps, self.result = steps, None
@@ -626,7 +768,7 @@
 
 
 def embed_grad_kernel(core_ref, pixel_ref, *refs):
-    *grad_refs, extra_ref, mine_ref, other_ref = refs
+    *grad_refs, table_ref, mine_ref, other_ref = refs
     parts = len(grad_refs) // 2
     total, place = None, None
     for part in range(parts):
@@ -635,19 +777,11 @@
         total = term if total is None else total + term
         own = grad_refs[parts + part][...]
         place = own if place is None else place + own
-    width, wide_rows = total.shape[1], mine_ref.shape[1] - extra_ref.shape[1]
+    width = total.shape[1]
     beside = mine_ref.shape[2] - width
-    spare = jnp.zeros((beside - place.shape[0], width), jnp.float32)
-    place = jnp.concatenate([place, spare], axis=0).T
-    core = core_ref[0]
-    top = jnp.concatenate([total, place], axis=1).astype(jnp.bfloat16)
-    chips = mine_ref.shape[0]
-    pairs = top.reshape(chips, 2, wide_rows, width + beside)
-    mine_ref[:, :wide_rows, :] = jnp.where(core == 0, pairs[:, 0], pairs[:, 1])
-    other_ref[:, :wide_rows, :] = jnp.where(core == 0, pairs[:, 1], pairs[:, 0])
-    extra = extra_ref[...].reshape(chips, 2, extra_ref.shape[1], width + beside)
-    mine_ref[:, wide_rows:, :] = jnp.where(core == 0, extra[:, 0], extra[:, 1])
-    other_ref[:, wide_rows:, :] = jnp.where(core == 0, extra[:, 1], extra[:, 0])
+    spare = jnp.zeros((beside - place.shape[0] - table_ref.shape[0], width), jnp.float32)
+    place = jnp.concatenate([place, table_ref[...], spare], axis=0).T
+    split_cores(jnp.concatenate([total, place], axis=1), core_ref[0], mine_ref, other_ref)
 
 
 def square_kernel(*refs):
@@ -681,7 +815,7 @@
         clips[index][at] = clipped
 
     everything = (None,)
-    update(0, everything, everything, embed_ref[:wide_rows, :width])
+    update(0, everything, everything, embed_ref[:, :width])
     blocks = weights[2].shape[1] // width
     for k in range(blocks):
         source, at = (qkv_ref, k) if k < 3 else (hidden_ref, k - 3)
@@ -693,12 +827,14 @@
         )
     update(3, everything, everything, narrow_ref[...])
     update(4, everything, everything, hidden_ref[(blocks - 3) * wide_rows :, :])
-    beside = embed_ref[:wide_rows, width:].astype(jnp.float32).T
-    update(1, everything, everything, beside[: weights[1].shape[0], :])
-    scale_rows, scale_columns = weights[5].shape
-    extra = embed_ref[wide_rows:, :].astype(jnp.float32)
-    update(5, everything, everything, extra[1 : 1 + scale_rows, :scale_columns])
-    update(6, everything, everything, extra[:1, : weights[6].shape[1]])
+    beside = embed_ref[:, width:].astype(jnp.float32).T
+    slots = weights[1].shape[0]
+    update(1, everything, everything, beside[:slots, :])
+    at = padded_rows(slots)
+    scale_rows = weights[5].shape[0]
+    update(5, everything, everything, beside[at : at + scale_rows, :])
+    at += scale_rows
+    update(6, everything, everything, beside[at : at + weights[6].shape[0], :])
 
 
 def per_device(
@@ -731,19 +867,12 @@
     square_biases,
 ):
     weights = (embedder, positions, widener, narrower, projector, scales, biases)
-    shapes = tuple(weight.shape for weight in weights)
     owners = lax.axis_size("fsdp")
-    packed = pack_weights(*(weight.astype(jnp.bfloat16) for weight in weights))
-    full = lax.all_gather(packed, "fsdp", axis=0)
-    embed_full, place_full, wide_blocks, narrow_full, project_full, scale_full, bias_full = (
-        unpack_weights(full, shapes)
-    )
-    place_float = place_full.astype(jnp.float32)
-    scale_float = scale_full.astype(jnp.float32)
-    bias_float = bias_full.astype(jnp.float32)
     micro_count, images_dev, slot_total, patch_size = pixels.shape
-    model_width = embed_full.shape[1]
-    hidden_width = narrow_full.shape[0] - model_width
+    model_width = embedder.shape[1]
+    wide_rows = embedder.shape[0]
+    narrow_rows = narrower.shape[0]
+    hidden_width = narrow_rows * owners - model_width
     hidden_blocks = hidden_width // model_width
     head_size = model_width // HEADS
     images_all = pairing.shape[1]
@@ -761,13 +890,50 @@
     row_weight = jnp.pad(merge_weight.reshape(images, 1, slot_total), ((0, 0), (0, 0), (0, spare)))
     column_weight = row_weight.reshape(images, slots, 1)
     live_counts = counts.reshape(images)
-    place_bias = jnp.pad(
-        place_float + bias_float[hidden_width + model_width :], ((0, spare), (0, 0))
-    )
-    out_bias = bias_float[hidden_width : hidden_width + model_width].reshape(1, model_width)
-    wide_stack = jnp.stack(wide_blocks)
     f32, low = jnp.float32, jnp.bfloat16
     shape = jax.ShapeDtypeStruct
+    place = jnp.stack([lax.axis_index("fsdp"), lax.axis_index("rep")]).astype(jnp.int32)
+    bias_rows = biases.shape[0] // wide_rows
+    scale_rows = scales.shape[0]
+    table_rows = padded_rows(scale_rows + bias_rows)
+    small_rows = -(-(slots + table_rows) // 128) * 128
+    beside = jnp.concatenate(
+        [
+            jnp.pad(positions, ((0, spare), (0, 0))),
+            scales,
+            biases.reshape(bias_rows, wide_rows),
+        ]
+    )
+    beside = jnp.pad(beside, ((0, small_rows - beside.shape[0]), (0, 0))).astype(low)
+    small_piece = jnp.concatenate([embedder.astype(low), beside.T], axis=1)
+    wide_low = widener.astype(low)
+    blocks_of = lambda first, count: [
+        wide_low[:, k * model_width : (k + 1) * model_width] for k in range(first, first + count)
+    ]
+    qkv_piece = jnp.stack(blocks_of(0, 3))
+    hidden_piece = jnp.stack(blocks_of(3, hidden_blocks) + [projector.astype(low)])
+    narrow_piece = narrower.astype(low)[None]
+    small_get = Flow(gather_plain(small_piece[None]))
+    small_get.go()
+    sent = small_get.go()
+    qkv_get = Flow(gather_split(first_behind(qkv_piece, sent)))
+    sent = qkv_get.go()
+    sent = small_get.go()
+    guards = qkv_get.go(sent)
+    embed_full, table = assembled_small(place, small_get.finish(), owners, model_width, guards)
+    scale_float = table[slots : slots + scale_rows]
+    bias_float = jnp.swapaxes(
+        table[slots + scale_rows : slots + scale_rows + bias_rows].reshape(
+            bias_rows, owners, wide_rows
+        ),
+        0,
+        1,
+    ).reshape(-1)
+    out_bias = bias_float[hidden_width : hidden_width + model_width].reshape(1, model_width)
+    place_bias = table[:slots] + bias_float[hidden_width + model_width :]
+    guards = qkv_get.go()
+    hidden_get = Flow(gather_split(first_behind(hidden_piece, guards)))
+    guards += hidden_get.go()
     merged, normed = image_call(
         embed_kernel,
         images,
@@ -779,69 +945,121 @@
             whole(patch_size, model_width),
             whole(slots, model_width),
             whole(1, model_width),
-        ],
+        ]
+        + [anywhere] * len(guards),
         [per_image(slots, model_width)] * 2,
         [shape((images, slots, model_width), f32), shape((images, slots, model_width), low)],
         name="embed",
     )(
         live_counts, pixel_rows, slot_map, row_weight, column_weight, embed_full, place_bias,
-        scale_float[0:1],
-    )
+        scale_float[0:1], *guards,
+    )
+    qkv_get.go()
+    qkv_parts = qkv_get.finish()
+    guards = hidden_get.go(qkv_parts[-1][0])
+    narrow_get = Flow(gather_split(first_behind(narrow_piece, guards)))
+    guards += narrow_get.go()
+    arrays, found, size = gathered(qkv_parts)
     normed_rows = normed.reshape(rows, model_width)
     column_block = lambda index_map: block((1, rows, model_width), index_map)
-    qkv, rstd, hidden, slope = pl.pallas_call(
-        functools.partial(widen_kernel, chunk=slots, head_size=head_size),
-        grid=(3 + hidden_blocks,),
-        in_specs=[
-            whole(rows, model_width),
-            block((1, model_width, model_width), lambda k: (k, 0, 0)),
-            block((1, 1, model_width), lambda k: (jnp.minimum(k, 1), 0, 0)),
-            block((1, 1, model_width), lambda k: (jnp.maximum(k - 3, 0), 0, 0)),
-        ],
-        out_specs=[
-            column_block(lambda k: (jnp.minimum(k, 2), 0, 0)),
-            column_block(lambda k: (jnp.minimum(k, 1), 0, 0)),
-            column_block(lambda k: (jnp.maximum(k - 3, 0), 0, 0)),
-            column_block(lambda k: (jnp.maximum(k - 3, 0), 0, 0)),
-        ],
+    heads, rstd, wide_qkv = pl.pallas_call(
+        functools.partial(widen_heads_kernel, found=found, chunk=slots, head_size=head_size),
+        grid_spec=pltpu.PrefetchScalarGridSpec(
+            num_scalar_prefetch=1,
+            grid=(2,),
+            in_specs=[whole(rows, model_width), block((1, 1, model_width), lambda k, _: (k, 0, 0))]
+            + [anywhere] * (len(arrays) + len(guards)),
+            out_specs=[column_block(lambda k, _: (k, 0, 0))] * 2 + [anywhere],
+            scratch_shapes=gather_scratch(found, size),
+        ),
         out_shape=[
-            shape((3, rows, model_width), low),
-            shape((2, rows, model_width), f32),
-            shape((hidden_blocks, rows, model_width), low),
-            shape((hidden_blocks, rows, model_width), low),
+            shape((2, rows, model_width), low), shape((2, rows, model_width), f32), shape(size, low)
         ],
         compiler_params=roomy,
-        name="widen",
-    )(
-        normed_rows, wide_stack, scale_float[2:4].reshape(2, 1, model_width),
-        bias_float[:hidden_width].reshape(hidden_blocks, 1, model_width),
-    )
+        cost_estimate=long,
+        name="widen_heads",
+    )(place, normed_rows, scale_float[2:4].reshape(2, 1, model_width), *arrays, *guards)
+    guards = hidden_get.go(heads)
+    values = pl.pallas_call(
+        widen_value_kernel,
+        grid=(1,),
+        in_specs=[whole(rows, model_width), block((1, model_width, model_width), lambda k: (2, 0, 0))]
+        + [anywhere] * (1 + len(guards)),
+        out_specs=column_block(lambda k: (0, 0, 0)),
+        out_shape=shape((1, rows, model_width), low),
+        compiler_params=roomy,
+        cost_estimate=long,
+        name="widen_values",
+    )(normed_rows, wide_qkv, heads, *guards)
     image_columns = lambda parts: block(
         (parts, slots, model_width), lambda image, counts: (0, image, 0)
     )
+    guards = narrow_get.go(heads)
+    (attended,) = image_call(
+        functools.partial(attend_kernel, head_size=head_size),
+        images,
+        [image_columns(2), image_columns(1)] + [anywhere] * len(guards),
+        [per_image(slots, model_width)],
+        [shape((images, slots, model_width), low)],
+        name="attend",
+    )(live_counts, heads, values, *guards)
+    guards = narrow_get.go() + [attended]
+    hidden_get.go(guards)
+    arrays, found, size = gathered(hidden_get.finish())
+    hidden, slope, wide_hidden = pl.pallas_call(
+        functools.partial(widen_hidden_kernel, found=found, chunk=slots),
+        grid_spec=pltpu.PrefetchScalarGridSpec(
+            num_scalar_prefetch=1,
+            grid=(hidden_blocks,),
+            in_specs=[whole(rows, model_width), block((1, 1, model_width), lambda k, _: (k, 0, 0))]
+            + [anywhere] * (len(arrays) + len(guards)),
+            out_specs=[column_block(lambda k, _: (k, 0, 0))] * 2 + [anywhere],
+            scratch_shapes=gather_scratch(found, size),
+        ),
+        out_shape=[shape((hidden_blocks, rows, model_width), low)] * 2 + [shape(size, low)],
+        compiler_params=roomy,
+        cost_estimate=long,
+        name="widen_hidden",
+    )(
+        place, normed_rows, bias_float[:hidden_width].reshape(hidden_blocks, 1, model_width),
+        *arrays, *guards,
+    )
+    project_full = wide_hidden[hidden_blocks]
+    narrow_get.go(hidden)
+    arrays, found, size = gathered(narrow_get.finish())
     narrow_scratch = [
         pltpu.VMEM((hidden_width + model_width, model_width), low), pltpu.SemaphoreType.DMA
     ]
-    attended, stream, pooled = image_call(
-        functools.partial(attend_kernel, head_size=head_size),
-        images,
-        [
-            image_columns(3),
-            image_columns(hidden_blocks),
-            per_image(slots, model_width),
-            anywhere,
-            whole(1, model_width),
-            whole(1, model_width),
-        ],
-        [per_image(slots, model_width), per_image(slots, model_width), per_image(1, model_width)],
-        [
-            shape((images, slots, model_width), low),
+    stream, pooled, narrow_full = pl.pallas_call(
+        functools.partial(join_kernel, found=found),
+        grid_spec=pltpu.PrefetchScalarGridSpec(
+            num_scalar_prefetch=2,
+            grid=(images,),
+            in_specs=[
+                block((1, slots, model_width), lambda image, *_: (image, 0, 0)),
+                block((hidden_blocks, slots, model_width), lambda image, *_: (0, image, 0)),
+                block((1, slots, model_width), lambda image, *_: (image, 0, 0)),
+                whole(1, model_width),
+                whole(1, model_width),
+            ]
+            + [anywhere] * len(arrays),
+            out_specs=[
+                block((1, slots, model_width), lambda image, *_: (image, 0, 0)),
+                block((1, 1, model_width), lambda image, *_: (image, 0, 0)),
+                anywhere,
+            ],
+            scratch_shapes=gather_scratch(found, size),
+        ),
+        out_shape=[
             shape((images, slots, model_width), f32),
             shape((images, 1, model_width), f32),
+            shape(size, low),
         ],
-        narrow_scratch,
-        name="attend",
-    )(live_counts, qkv, hidden, merged, narrow_full, out_bias, scale_float[1:2])
+        compiler_params=roomy,
+        cost_estimate=long,
+        name="join",
+    )(live_counts, place, attended, hidden, merged, out_bias, scale_float[1:2], *arrays)
+    narrow_full = narrow_full[0]
     pooled_low = pooled.reshape(images, model_width).astype(low)
     embeds = product(pooled_low, project_full).astype(low)
     embeds = embeds.reshape(micro_count, images_dev, -1)
@@ -923,8 +1141,6 @@
     )
     core = (lax.axis_index("fsdp") % 2).reshape(1)
     chips = owners // 2
-    wide_rows = model_width // owners
-    narrow_rows = narrower.shape[0]
     branch_rows = grad_branch.reshape(rows, model_width)
     halves = lambda count, width: [shape((chips, count, width), low)] * 2
     narrow_halves = pl.pallas_call(
@@ -996,7 +1212,8 @@
             functools.partial(attend_back_kernel, base=base, head_size=head_size),
             per_part,
             [
-                shifted_columns(base, 3),
+                shifted_columns(base, 2),
+                shifted_columns(base, 1),
                 shifted_columns(base, 2),
                 shifted(base, slots),
                 whole(2, 1, model_width),
@@ -1006,7 +1223,7 @@
             [shape((3, part_rows, model_width), low), shape((8, model_width), f32)],
             [pltpu.VMEM((2, slots, model_width), f32)],
             name="attend_back",
-        )(live_counts, qkv, rstd, grad_attended, head_gains, *guards)
+        )(live_counts, heads, values, rstd, grad_attended, head_gains, *guards)
         grad_qkv.append(grads)
         head_sums = head_sums + sums_part
         guards = [grads]
@@ -1042,6 +1259,7 @@
                 image_columns(3),
                 shifted_columns(base, hidden_blocks),
                 anywhere,
+                anywhere,
                 shifted(base, slots),
                 shifted(base, slots),
                 whole(1, model_width),
@@ -1062,7 +1280,7 @@
             ],
             name="merge_back",
         )(
-            live_counts, grad_qkv[part], grad_act, wide_stack, merged, grad_stream,
+            live_counts, grad_qkv[part], grad_act, wide_qkv, wide_hidden, merged, grad_stream,
             scale_float[0:1], slot_map, row_weight, column_weight, *guards,
         )
         grad_patches.append(grads.reshape(part_rows, model_width))
@@ -1074,24 +1292,14 @@
         elif part == 1:
             guards += narrow_flow.go(grads)
     guards += hidden_flow.go(grads) + qkv_flow.go(grads)
-    scale_rows, scale_columns = scales.shape
-    bias_count = biases.shape[0]
     grad_scale = jnp.stack([merge_sums[0], out_sums[hidden_blocks + 1], head_sums[0], head_sums[1]])
-    grad_bias = jnp.concatenate([out_sums[: hidden_blocks + 1].reshape(-1), merge_sums[1]])
-    beside = -(-slots // 128) * 128
-    piece_width = model_width + beside
-    fill = lambda values: jnp.pad(
-        values, ((0, 0), (0, 0), (0, piece_width - values.shape[2]))
-    )
-    extra_rows = 16
-    extra = jnp.concatenate(
-        [
-            fill(grad_bias.reshape(owners, 1, bias_count)),
-            fill(jnp.swapaxes(grad_scale.reshape(scale_rows, owners, scale_columns), 0, 1)),
-            jnp.zeros((owners, extra_rows - 1 - scale_rows, piece_width), f32),
-        ],
-        axis=1,
-    ).astype(low)
+    grad_bias = jnp.concatenate([out_sums[: hidden_blocks + 1], merge_sums[1:2]]).reshape(
+        owners, bias_rows, wide_rows
+    )
+    grad_bias = jnp.swapaxes(grad_bias, 0, 1).reshape(bias_rows, model_width)
+    table = jnp.concatenate([grad_scale, grad_bias])
+    table = jnp.pad(table, ((0, padded_rows(table.shape[0]) - table.shape[0]), (0, 0)))
+    piece_width = small_piece.shape[1]
     embed_halves = pl.pallas_call(
         lambda core_ref, pixel_ref, *refs: embed_grad_kernel(
             core_ref, pixel_ref, *refs[: 2 * parts + 1], *refs[-2:]
@@ -1102,15 +1310,15 @@
             in_specs=[whole(rows, patch_size)]
             + [whole(part_rows, model_width)] * parts
             + [whole(slots, model_width)] * parts
-            + [whole(owners, extra_rows, piece_width)]
+            + [whole(*table.shape)]
             + [anywhere] * len(guards),
-            out_specs=[whole(chips, wide_rows + extra_rows, piece_width)] * 2,
+            out_specs=[whole(chips, wide_rows, piece_width)] * 2,
         ),
-        out_shape=halves(wide_rows + extra_rows, piece_width),
+        out_shape=halves(wide_rows, piece_width),
         compiler_params=roomy,
         cost_estimate=long,
         name="embed_grad",
-    )(core, pixel_rows.reshape(rows, patch_size), *grad_patches, *grad_places, extra, *guards)
+    )(core, pixel_rows.reshape(rows, patch_size), *grad_patches, *grad_places, table, *guards)
     embed_flow = Flow(reduce_rows_last(*embed_halves))
     flows = (narrow_flow, hidden_flow, qkv_flow, embed_flow)
     while any(flow.result is None for flow in flows):
@@ -1145,7 +1353,7 @@
         square_biases,
     )
     as_rows = lambda arrays: [
-        array.reshape(1, -1) if array.ndim == 1 else array for array in arrays
+        array.reshape(-1, wide_rows) if array.ndim == 1 else array for array in arrays
     ]
     outs = pl.pallas_call(
         functools.partial(update_kernel, wide_rows=wide_rows),

time: 546 us -> 493 us (0.903)
  waiting for transfers between devices: 135 us -> 73 us
  starting transfers between devices: 44.8 us -> 70.3 us
  local copies, waits for them, and re-layouts: 71.7 us -> 46.3 us
  between operations: 18.8 us -> 5.65 us
  Pallas kernels: 227 us -> 239 us
  other arithmetic: 41.3 us -> 49.1 us
    all_gather x1 -> x0, waiting for transfers between devices: 87.8 us -> none  [per_device(): full = lax.all_gather(packed, 'fsdp', axis=0)]
    pallas_call x1 -> x5, Pallas kernels: 32.1 us -> 63.9 us  [the longest x1 23.5 us: per_device(): pl.pallas_call(functools.partial(widen_hidden_kernel, found=found, chunk=...]
    ppermute x0 -> x33, starting transfers between devices: none -> 29.5 us  [the longest x12 19.5 us: high_gather(): lax.ppermute(own, 'fsdp', bit_swap(owners, turn))]
    ppermute x0 -> x33, waiting for transfers between devices: none -> 22.6 us  [the longest x12 15.8 us: high_gather(): lax.ppermute(own, 'fsdp', bit_swap(owners, turn))]
    pallas_call x1, Pallas kernels: 30.3 us -> 10.3 us  [per_device(): image_call(functools.partial(attend_kernel, head_size=head_size), images,...]
    slice x5 -> x4, local copies, waits for them, and re-layouts: 14.7 us -> 1.52 us  [the longest x1 0.81 us: per_device(): table[slots + scale_rows:slots + scale_rows + bias_rows]]
    ppermute x4 -> x10, waiting for transfers between devices: 9.99 us -> 19 us  [rep_swap(): return lax.ppermute(own, 'rep', bit_swap(2, 1))]
    ppermute x18, waiting for transfers between devices: 21.2 us -> 12.3 us  [traded(): kept.append(lax.ppermute(send, mesh_axis, bit_swap(size, turn * stride)))]
  transfers between devices with their start and end apart: 36 -> 74, of which waited for: 17 -> 29; matrix products, arithmetic and copies ran while one was open for 11% -> 15% of each run, Pallas kernels for 19% -> 37%
where the time goes in v4:
time: 493 us; the launch traced here: 487 us
  Pallas kernels  239 us (48%)
  waiting for transfers between devices  73 us (15%)
  starting transfers between devices  70.3 us (14%)
  other arithmetic  49.1 us (10%)
  local copies, waits for them, and re-layouts  46.3 us (9%)
  between operations  5.65 us (1%)
    pallas_call x3, Pallas kernels, per_device(): image_call(functools.partial(merge_back_kernel, base=base), per_part, [im...  43.2 us
    pallas_call x3, Pallas kernels, per_device(): image_call(functools.partial(attend_back_kernel, base=base, head_size=hea...  40.3 us
    pallas_call x1, Pallas kernels, per_device(): pl.pallas_call(functools.partial(widen_hidden_kernel, found=found, chunk=...  23.5 us
    ppermute x18, starting transfers between devices, traded(): kept.append(lax.ppermute(send, mesh_axis, bit_swap(size, turn * stride)))  23 us
    pallas_call x1, Pallas kernels, per_device(): image_call(branch_kernel, images, [per_image(slots, model_width), per_ima...  20.9 us
    ppermute x12, starting transfers between devices, high_gather(): lax.ppermute(own, 'fsdp', bit_swap(owners, turn))  19.5 us
    ppermute x10, waiting for transfers between devices, rep_swap(): return lax.ppermute(own, 'rep', bit_swap(2, 1))  19 us
    convert_element_type x9, other arithmetic, traded(): added(picked(terms, axis, index ^ turn)).astype(jnp.bfloat16)  16.9 us
  transfers between devices with their start and end apart: 74, of which 29 were waited for; matrix products, arithmetic and copies ran while one was open for 15% of the time, Pallas kernels for 37%

profile of v4, /device:TPU:0, one launch (start us, length us, event | category | flops | bytes accessed | tf_op | source)
XLA Modules:
  0.0 487.1 jit_solution(1972260368938969564)
XLA Ops:
  4.9 3.1 collective-permute-start
  12.0 6.3 %collective-permute-done.1 = bf16[1,48,1024]{2,1,0:T(8,128)(2,1)S(1)} collective-permute-done((bf16[1,48,1024]{2,1,0:T(8,128)(2,1)S(1)}, bf16[1,48,1024]{2,1,0:T(8,128)(2,1)S(1)}, u32[]{:S(2)}, u32[]{:S(2)}) %collective-permute-start.1) | collective-permute-done | bytes 98336 | tf_op jit(solution)/shard_map/ppermute | solution.py:535
  27.0 6.0 %collective-permute-done.7 = bf16[3,48,384]{2,1,0:T(8,128)(2,1)S(1)} collective-permute-done((bf16[3,48,384]{2,1,0:T(8,128)(2,1)S(1)}, bf16[3,48,384]{2,1,0:T(8,128)(2,1)S(1)}, u32[]{:S(2)}, u32[]{:S(2)}) %collective-permute-start.7) | collective-permute-done | bytes 110624 | tf_op jit(solution)/shard_map/ppermute | solution.py:535
  50.9 3.7 assemble_small.1
  62.6 10.3 %embed.1 = (f32[6,208,768]{2,1,0:T(8,128)}, bf16[6,208,768]{2,1,0:T(8,128)(2,1)}) custom-call(s32[6]{0:T(128)} %reshape.315.counts_ref, bf16[6,208,768]{2,1,0:T(8,128)(2,1)} %pad.37.pixel_ref, s32[6,1,208]{2,1,0:T(1,128)} %pad.38.map_ref, f32[6,1,208]{2,1,0:T(1,128)} %get-tuple-element.339.row_ref, f32[6,208,1]{2,1,0:T(8,128)} %copy.99.column_ref, ...), custom_call_target="tpu_custom_call" | custom-call | flops 60000002048 | bytes 1000 | tf_op jit(solution)/shard_map/embed/pallas_call | solution.py:937
  81.7 15.1 %widen_heads.1 = (bf16[2,1248,768]{2,1,0:T(8,128)(2,1)}, f32[2,1248,768]{2,1,0:T(8,128)}, bf16[3,768,768]{2,1,0:T(8,128)(2,1)}) custom-call(s32[2]{0:T(128)} %pad_add_fusion.place_ref, bf16[1248,768]{1,0:T(8,128)(2,1)} %bitcast.263, f32[2,1,768]{2,1,0:T(1,128)} %reshape.324.gain_ref, bf16[4,3,48,384]{3,2,1,0:T(8,128)(2,1)} %copy-done.25, ...), custom_call_target="tpu_custom_call" | custom-call | flops 60000002048 | bytes 1000 | tf_op jit(solution)/shard_map/widen_heads/pallas_call | solution.py:965
  103.8 4.8 widen_values.1.values_ref
  108.6 10.3 %attend.1.refs_10_.attended_ref = bf16[6,208,768]{2,1,0:T(8,128)(2,1)} custom-call(s32[6]{0:T(128)} %reshape.315.counts_ref, bf16[2,1248,768]{2,1,0:T(8,128)(2,1)} %get-tuple-element.137.refs_0_.heads_ref, bf16[1,1248,768]{2,1,0:T(8,128)(2,1)} %widen_values.1.values_ref, bf16[2,1,240,384]{3,2,1,0:T(8,128)(2,1)} %pad_maximum_fusion.9.refs_0_, ...), custom_call_target="tpu_custom_call" | custom-call | flops 60000002048 | bytes 1000 | tf_op jit(solution)/shard_map/attend/pallas_call | solution.py:998
  121.3 3.4 collective-permute-done.26.refs_3_
  130.5 23.5 %widen_hidden.1 = (bf16[4,1248,768]{2,1,0:T(8,128)(2,1)}, bf16[4,1248,768]{2,1,0:T(8,128)(2,1)}, bf16[5,768,768]{2,1,0:T(8,128)(2,1)}) custom-call(s32[2]{0:T(128)} %pad_add_fusion.place_ref, bf16[1248,768]{1,0:T(8,128)(2,1)} %bitcast.265, f32[4,1,768]{2,1,0:T(1,128)} %slice.244.bias_ref, bf16[4,5,48,384]{3,2,1,0:T(8,128)(2,1)} %pad_maximum_fusion.refs_1_.refs_0_, ...), custom_call_target="tpu_custom_call" | custom-call | flops 60000002048 | bytes 1000 | tf_op jit(solution)/shard_map/widen_hidden/pallas_call | solution.py:1009
  159.6 16.8 %join.1 = (f32[6,208,768]{2,1,0:T(8,128)}, f32[6,1,768]{2,1,0:T(1,128)}, bf16[1,3840,768]{2,1,0:T(8,128)(2,1)}) custom-call(s32[6]{0:T(128)} %reshape.315.counts_ref, s32[2]{0:T(128)} %pad_add_fusion.place_ref, bf16[6,208,768]{2,1,0:T(8,128)(2,1)} %attend.1.refs_10_.attended_ref, bf16[4,1248,768]{2,1,0:T(8,128)(2,1)} %get-tuple-element.148.hidden_ref, ...), custom_call_target="tpu_custom_call" | custom-call | flops 60000002048 | bytes 1000 | tf_op jit(solution)/shard_map/join/pallas_call | solution.py:1033
  181.3 3.1 collective-permute-done.40
  184.5 3.6 collective-permute-done.41
  189.2 3.5 collective-permute-done.42
  201.1 20.9 %branch.1 = (f32[6,208,768]{2,1,0:T(8,128)}, bf16[6,208,768]{2,1,0:T(8,128)(2,1)}, bf16[6,208,768]{2,1,0:T(8,128)(2,1)}, bf16[4,1248,768]{2,1,0:T(8,128)(2,1)}, f32[8,768]{1,0:T(8,128)}) custom-call(s32[6]{0:T(128)} %reshape.315.counts_ref, f32[6,208,768]{2,1,0:T(8,128)} %get-tuple-element.156.stream_ref, f32[6,1,768]{2,1,0:T(1,128)} %reshape.330.grad_pooled_ref, ...), custom_call_target="tpu_custom_call" | custom-call | flops 60000002048 | bytes 1000 | tf_op jit(solution)/shard_map/branch/pallas_call | solution.py:1112
  222.0 14.1 %narrow_grad.1 = (bf16[8,240,768]{2,1,0:T(8,128)(2,1)}, bf16[8,240,768]{2,1,0:T(8,128)(2,1)}) custom-call(s32[1]{0:T(128)} %bitcast.40.core_ref, bf16[1248,768]{1,0:T(8,128)(2,1)} %bitcast.268, bf16[4,1248,768]{2,1,0:T(8,128)(2,1)} %get-tuple-element.148.hidden_ref, bf16[1248,768]{1,0:T(8,128)(2,1)} %bitcast.269), custom_call_target="tpu_custom_call" | custom-call | flops 60000002048 | bytes 1000 | tf_op jit(solution)/shard_map/narrow_grad/pallas_call | solution.py:1146
  236.2 11.3 %hidden_grad.1 = (bf16[8,240,768]{2,1,0:T(8,128)(2,1)}, bf16[8,240,768]{2,1,0:T(8,128)(2,1)}) custom-call(s32[1]{0:T(128)} %bitcast.40.core_ref, bf16[1248,768]{1,0:T(8,128)(2,1)} %bitcast.266, bf16[4,1248,768]{2,1,0:T(8,128)(2,1)} %get-tuple-element.165.grad_ref.grad_act_ref, bf16[16,768]{1,0:T(8,128)(2,1)} %pad.43.pooled_ref, bf16[16,768]{1,0:T(8,128)(2,1)} %pad.44.embeds_ref), custom_call_target="tpu_custom_call" | custom-call | flops 60000002048 | bytes 1000 | tf_op jit(solution)/shard_map/hidden_grad/pallas_call | solution.py:1171
  258.6 13.4 %attend_back.3 = (bf16[3,416,768]{2,1,0:T(8,128)(2,1)}, f32[8,768]{1,0:T(8,128)}) custom-call(s32[6]{0:T(128)} %reshape.315.counts_ref, bf16[2,1248,768]{2,1,0:T(8,128)(2,1)} %get-tuple-element.137.refs_0_.heads_ref, bf16[1,1248,768]{2,1,0:T(8,128)(2,1)} %widen_values.1.values_ref, f32[2,1248,768]{2,1,0:T(8,128)} %get-tuple-element.162.rstd_ref, ...), custom_call_target="tpu_custom_call" | custom-call | flops 60000002048 | bytes 1000 | tf_op jit(solution)/shard_map/attend_back/pallas_call | solution.py:1211
  272.0 2.9 fusion.1.refs_1_
  274.9 13.7 %attend_back.4 = (bf16[3,416,768]{2,1,0:T(8,128)(2,1)}, f32[8,768]{1,0:T(8,128)}) custom-call(s32[6]{0:T(128)} %reshape.315.counts_ref, bf16[2,1248,768]{2,1,0:T(8,128)(2,1)} %get-tuple-element.137.refs_0_.heads_ref, bf16[1,1248,768]{2,1,0:T(8,128)(2,1)} %widen_values.1.values_ref, f32[2,1248,768]{2,1,0:T(8,128)} %get-tuple-element.162.rstd_ref, ...), custom_call_target="tpu_custom_call" | custom-call | flops 60000002048 | bytes 1000 | tf_op jit(solution)/shard_map/attend_back/pallas_call | solution.py:1211
  289.1 13.3 %attend_back.5 = (bf16[3,416,768]{2,1,0:T(8,128)(2,1)}, f32[8,768]{1,0:T(8,128)}) custom-call(s32[6]{0:T(128)} %reshape.315.counts_ref, bf16[2,1248,768]{2,1,0:T(8,128)(2,1)} %get-tuple-element.137.refs_0_.heads_ref, bf16[1,1248,768]{2,1,0:T(8,128)(2,1)} %widen_values.1.values_ref, f32[2,1248,768]{2,1,0:T(8,128)} %get-tuple-element.162.rstd_ref, ...), custom_call_target="tpu_custom_call" | custom-call | flops 60000002048 | bytes 1000 | tf_op jit(solution)/shard_map/attend_back/pallas_call | solution.py:1211
  309.2 9.8 %qkv_grad.1 = (bf16[8,144,768]{2,1,0:T(8,128)(2,1)}, bf16[8,144,768]{2,1,0:T(8,128)(2,1)}) custom-call(s32[1]{0:T(128)} %bitcast.40.core_ref, bf16[1248,768]{1,0:T(8,128)(2,1)} %bitcast.267, bf16[3,416,768]{2,1,0:T(8,128)(2,1)} %get-tuple-element.164.refs_0_.grad_qkv_ref, bf16[3,416,768]{2,1,0:T(8,128)(2,1)} %get-tuple-element.170.refs_0_.refs_1_.grad_qkv_ref, ...), custom_call_target="tpu_custom_call" | custom-call | flops 60000002048 | bytes 1000 | tf_op jit(solution)/shard_map/qkv_grad/pallas_call | solution.py:1233
  320.6 14.3 %merge_back.3 = (bf16[2,208,768]{2,1,0:T(8,128)(2,1)}, f32[208,768]{1,0:T(8,128)}, f32[8,768]{1,0:T(8,128)}) custom-call(s32[6]{0:T(128)} %reshape.315.counts_ref, bf16[3,416,768]{2,1,0:T(8,128)(2,1)} %get-tuple-element.164.refs_0_.grad_qkv_ref, bf16[4,1248,768]{2,1,0:T(8,128)(2,1)} %get-tuple-element.165.grad_ref.grad_act_ref, ...), custom_call_target="tpu_custom_call" | custom-call | flops 60000002048 | bytes 1000 | tf_op jit(solution)/shard_map/merge_back/pallas_call | solution.py:1255
  350.3 14.5 %merge_back.4 = (bf16[2,208,768]{2,1,0:T(8,128)(2,1)}, f32[208,768]{1,0:T(8,128)}, f32[8,768]{1,0:T(8,128)}) custom-call(s32[6]{0:T(128)} %reshape.315.counts_ref, bf16[3,416,768]{2,1,0:T(8,128)(2,1)} %get-tuple-element.170.refs_0_.refs_1_.grad_qkv_ref, bf16[4,1248,768]{2,1,0:T(8,128)(2,1)} %get-tuple-element.165.grad_ref.grad_act_ref, ...), custom_call_target="tpu_custom_call" | custom-call | flops 60000002048 | bytes 1000 | tf_op jit(solution)/shard_map/merge_back/pallas_call | solution.py:1255
  367.4 14.5 %merge_back.5 = (bf16[2,208,768]{2,1,0:T(8,128)(2,1)}, f32[208,768]{1,0:T(8,128)}, f32[8,768]{1,0:T(8,128)}) custom-call(s32[6]{0:T(128)} %reshape.315.counts_ref, bf16[3,416,768]{2,1,0:T(8,128)(2,1)} %get-tuple-element.171.refs_2_.refs_3_.grad_qkv_ref, bf16[4,1248,768]{2,1,0:T(8,128)(2,1)} %get-tuple-element.165.grad_ref.grad_act_ref, ...), custom_call_target="tpu_custom_call" | custom-call | flops 60000002048 | bytes 1000 | tf_op jit(solution)/shard_map/merge_back/pallas_call | solution.py:1255
  382.9 3.0 collective-permute-start.51
  394.8 5.9 %embed_grad.1 = (bf16[8,48,1024]{2,1,0:T(8,128)(2,1)}, bf16[8,48,1024]{2,1,0:T(8,128)(2,1)}) custom-call(s32[1]{0:T(128)} %bitcast.40.core_ref, bf16[1248,768]{1,0:T(8,128)(2,1)} %bitcast.229, bf16[416,768]{1,0:T(8,128)(2,1)} %bitcast.271, bf16[416,768]{1,0:T(8,128)(2,1)} %bitcast.272, bf16[416,768]{1,0:T(8,128)(2,1)} %bitcast.273, ...), custom_call_target="tpu_custom_call" | custom-call | flops 60000002048 | bytes 1000 | tf_op jit(solution)/shard_map/embed_grad/pallas_call | solution.py:1303
  404.6 5.0 %collective-permute-done.53 = bf16[120,768]{1,0:T(8,128)(2,1)} collective-permute-done((bf16[120,768]{1,0:T(8,128)(2,1)S(1)}, bf16[120,768]{1,0:T(8,128)(2,1)}, u32[]{:S(2)}, u32[]{:S(2)}) %collective-permute-start.53) | collective-permute-done | bytes 184352 | tf_op jit(solution)/shard_map/ppermute | solution.py:484
  410.7 6.5 %collective-permute-done.57 = bf16[240,768]{1,0:T(8,128)(2,1)} collective-permute-done((bf16[240,768]{1,0:T(8,128)(2,1)}, bf16[240,768]{1,0:T(8,128)(2,1)}, u32[]{:S(2)}, u32[]{:S(2)}) %collective-permute-start.57) | collective-permute-done | bytes 368672 | tf_op jit(solution)/shard_map/ppermute | solution.py:484
  427.8 5.5 %collective-permute-done.61 = bf16[72,768]{1,0:T(8,128)(2,1)S(1)} collective-permute-done((bf16[72,768]{1,0:T(8,128)(2,1)S(1)}, bf16[72,768]{1,0:T(8,128)(2,1)S(1)}, u32[]{:S(2)}, u32[]{:S(2)}) %collective-permute-start.61) | collective-permute-done | bytes 110624 | tf_op jit(solution)/shard_map/ppermute | solution.py:472
  441.2 5.5 %collective-permute-done.67 = bf16[48,1024]{1,0:T(8,128)(2,1)S(1)} collective-permute-done((bf16[48,1024]{1,0:T(8,128)(2,1)S(1)}, bf16[48,1024]{1,0:T(8,128)(2,1)S(1)}, u32[]{:S(2)}, u32[]{:S(2)}) %collective-permute-start.67) | collective-permute-done | bytes 98336 | tf_op jit(solution)/shard_map/ppermute | solution.py:472
  470.9 7.2 %update.1 = (f32[48,768]{1,0:T(8,128)}, f32[196,48]{1,0:T(8,128)}, f32[48,5376]{1,0:T(8,128)}, f32[240,768]{1,0:T(8,128)}, f32[48,768]{1,0:T(8,128)}, /*index=5*...) custom-call(f32[8,128]{1,0:T(8,128)} %copy-done.40, ...), custom_call_target="tpu_custom_call" | custom-call | tf_op jit(solution)/shard_map/update/pallas_call | solution.py:1358
  (407 shorter events, 186.8 us)
Async XLA Ops:
  41.9 17.7 %collective-permute-start.12 = (bf16[4,3,48,384]{3,2,1,0:T(8,128)(2,1)S(1)}, bf16[4,3,48,384]{3,2,1,0:T(8,128)(2,1)}, u32[]{:S(2)}, u32[]{:S(2)}) collective-permute-start(bf16[4,3,48,384]{3,2,1,0:T(8,128)(2,1)S(1)} %pad_maximum_fusion.5.refs_1_.refs_2_), channel_id=1, source_target_pairs={{0,16},{16,0},{1,17},{17,1},{2,18},{18,2},{3,19},{19,3},{4,20},{20... | collective-permute-start | bytes 1327112 | tf_op jit(solution)/shard_map/ppermute | solution.py:484
  44.3 15.3 %collective-permute-start.11 = (bf16[4,3,48,384]{3,2,1,0:T(8,128)(2,1)S(1)}, bf16[4,3,48,384]{3,2,1,0:T(8,128)(2,1)}, u32[]{:S(2)}, u32[]{:S(2)}) collective-permute-start(bf16[4,3,48,384]{3,2,1,0:T(8,128)(2,1)S(1)} %pad_maximum_fusion.4.refs_0_), channel_id=1, source_target_pairs={{0,2},{1,3},{2,0},{3,1},{4,6},{5,7},{6,4},{7,5},{8,10},{9,11},{10,... | collective-permute-start | bytes 1327112 | tf_op jit(solution)/shard_map/ppermute | solution.py:529
  47.8 14.8 %collective-permute-start.18 = (bf16[5,48,384]{2,1,0:T(8,128)(2,1)S(1)}, bf16[5,48,384]{2,1,0:T(8,128)(2,1)S(1)}, u32[]{:S(2)}, u32[]{:S(2)}) collective-permute-start(bf16[5,48,384]{2,1,0:T(8,128)(2,1)S(1)} %constant_dynamic-slice_fusion.6.refs_2_), channel_id=1, source_target_pairs={{0,8},{1,9},{2,10},{3,11},{4,12},{5,13},{6,14},{7,15},{8,0},{9,1},... | collective-permute-start | bytes 552968 | tf_op jit(solution)/shard_map/ppermute | solution.py:535
  49.4 24.9 %collective-permute-start.19 = (bf16[5,48,384]{2,1,0:T(8,128)(2,1)S(1)}, bf16[5,48,384]{2,1,0:T(8,128)(2,1)S(1)}, u32[]{:S(2)}, u32[]{:S(2)}) collective-permute-start(bf16[5,48,384]{2,1,0:T(8,128)(2,1)S(1)} %constant_dynamic-slice_fusion.6.refs_2_), channel_id=1, source_target_pairs={{0,12},{1,13},{2,14},{3,15},{4,8},{5,9},{6,10},{7,11},{8,4},{9,5},... | collective-permute-start | bytes 552968 | tf_op jit(solution)/shard_map/ppermute | solution.py:535
  59.7 18.4 %collective-permute-start.13 = (bf16[4,3,48,384]{3,2,1,0:T(8,128)(2,1)S(1)}, bf16[4,3,48,384]{3,2,1,0:T(8,128)(2,1)}, u32[]{:S(2)}, u32[]{:S(2)}) collective-permute-start(bf16[4,3,48,384]{3,2,1,0:T(8,128)(2,1)S(1)} %pad_maximum_fusion.4.refs_0_), channel_id=1, source_target_pairs={{0,1},{1,0},{2,3},{3,2},{4,5},{5,4},{6,7},{7,6},{8,9},{9,8},{10,11... | collective-permute-start | bytes 1327112 | tf_op jit(solution)/shard_map/ppermute | solution.py:525
  60.2 19.5 %collective-permute-start.14 = (bf16[4,3,48,384]{3,2,1,0:T(8,128)(2,1)}, bf16[4,3,48,384]{3,2,1,0:T(8,128)(2,1)}, u32[]{:S(2)}, u32[]{:S(2)}) collective-permute-start(bf16[4,3,48,384]{3,2,1,0:T(8,128)(2,1)} %collective-permute-done.11.refs_1_), channel_id=1, source_target_pairs={{0,1},{1,0},{2,3},{3,2},{4,5},{5,4},{6,7},{7,6},{8,9},{9,8},{10,11... | collective-permute-start | bytes 1327112 | tf_op jit(solution)/shard_map/ppermute | solution.py:525
  62.6 17.6 %collective-permute-start.15 = (bf16[4,3,48,384]{3,2,1,0:T(8,128)(2,1)S(1)}, bf16[4,3,48,384]{3,2,1,0:T(8,128)(2,1)}, u32[]{:S(2)}, u32[]{:S(2)}) collective-permute-start(bf16[4,3,48,384]{3,2,1,0:T(8,128)(2,1)S(1)} %pad_maximum_fusion.5.refs_1_.refs_2_), channel_id=1, source_target_pairs={{0,1},{1,0},{2,3},{3,2},{4,5},{5,4},{6,7},{7,6},{8,9},{9,8},{10,11... | collective-permute-start | bytes 1327112 | tf_op jit(solution)/shard_map/ppermute | solution.py:525
  75.2 21.6 %collective-permute-start.22 = (bf16[1,240,384]{2,1,0:T(8,128)(2,1)S(1)}, bf16[1,240,384]{2,1,0:T(8,128)(2,1)S(1)}, u32[]{:S(2)}, u32[]{:S(2)}) collective-permute-start(bf16[1,240,384]{2,1,0:T(8,128)(2,1)S(1)} %constant_dynamic-slice_fusion.5.refs_10_), channel_id=1, source_target_pairs={{0,4},{1,5},{2,6},{3,7},{4,0},{5,1},{6,2},{7,3},{8,12},{9,13},{10,... | collective-permute-start | bytes 552968 | tf_op jit(solution)/shard_map/ppermute | solution.py:535
  75.3 21.6 %collective-permute-start.23 = (bf16[1,240,384]{2,1,0:T(8,128)(2,1)S(1)}, bf16[1,240,384]{2,1,0:T(8,128)(2,1)S(1)}, u32[]{:S(2)}, u32[]{:S(2)}) collective-permute-start(bf16[1,240,384]{2,1,0:T(8,128)(2,1)S(1)} %constant_dynamic-slice_fusion.5.refs_10_), channel_id=1, source_target_pairs={{0,8},{1,9},{2,10},{3,11},{4,12},{5,13},{6,14},{7,15},{8,0},{9,1},... | collective-permute-start | bytes 552968 | tf_op jit(solution)/shard_map/ppermute | solution.py:535
  78.1 18.8 %collective-permute-start.24 = (bf16[1,240,384]{2,1,0:T(8,128)(2,1)S(1)}, bf16[1,240,384]{2,1,0:T(8,128)(2,1)S(1)}, u32[]{:S(2)}, u32[]{:S(2)}) collective-permute-start(bf16[1,240,384]{2,1,0:T(8,128)(2,1)S(1)} %constant_dynamic-slice_fusion.5.refs_10_), channel_id=1, source_target_pairs={{0,12},{1,13},{2,14},{3,15},{4,8},{5,9},{6,10},{7,11},{8,4},{9,5},... | collective-permute-start | bytes 552968 | tf_op jit(solution)/shard_map/ppermute | solution.py:535
  79.7 20.2 %collective-permute-start.21 = (bf16[2,5,48,384]{3,2,1,0:T(8,128)(2,1)S(1)}, bf16[2,5,48,384]{3,2,1,0:T(8,128)(2,1)S(1)}, u32[]{:S(2)}, u32[]{:S(2)}) collective-permute-start(bf16[2,5,48,384]{3,2,1,0:T(8,128)(2,1)S(1)} %pad_maximum_fusion.8.refs_9_), channel_id=1, source_target_pairs={{0,2},{1,3},{2,0},{3,1},{4,6},{5,7},{6,4},{7,5},{8,10},{9,11},{10,... | collective-permute-start | bytes 1105928 | tf_op jit(solution)/shard_map/ppermute | solution.py:529
  80.2 19.7 %collective-permute-start.20 = (bf16[2,5,48,384]{3,2,1,0:T(8,128)(2,1)S(1)}, bf16[2,5,48,384]{3,2,1,0:T(8,128)(2,1)S(1)}, u32[]{:S(2)}, u32[]{:S(2)}) collective-permute-start(bf16[2,5,48,384]{3,2,1,0:T(8,128)(2,1)S(1)} %pad_maximum_fusion.7.refs_8_), channel_id=1, source_target_pairs={{0,16},{16,0},{1,17},{17,1},{2,18},{18,2},{3,19},{19,3},{4,20},{20... | collective-permute-start | bytes 1105928 | tf_op jit(solution)/shard_map/ppermute | solution.py:484
  96.9 21.9 %collective-permute-start.28 = (bf16[2,1,240,384]{3,2,1,0:T(8,128)(2,1)S(1)}, bf16[2,1,240,384]{3,2,1,0:T(8,128)(2,1)}, u32[]{:S(2)}, u32[]{:S(2)}) collective-permute-start(bf16[2,1,240,384]{3,2,1,0:T(8,128)(2,1)S(1)} %pad_maximum_fusion.10.refs_1_), channel_id=1, source_target_pairs={{0,2},{1,3},{2,0},{3,1},{4,6},{5,7},{6,4},{7,5},{8,10},{9,11},{10,... | collective-permute-start | bytes 1105928 | tf_op jit(solution)/shard_map/ppermute | solution.py:529
  99.3 20.7 %collective-permute-start.27 = (bf16[2,1,240,384]{3,2,1,0:T(8,128)(2,1)}, bf16[2,1,240,384]{3,2,1,0:T(8,128)(2,1)}, u32[]{:S(2)}, u32[]{:S(2)}) collective-permute-start(bf16[2,1,240,384]{3,2,1,0:T(8,128)(2,1)} %pad_maximum_fusion.9.refs_0_), channel_id=1, source_target_pairs={{0,16},{16,0},{1,17},{17,1},{2,18},{18,2},{3,19},{19,3},{4,20},{20... | collective-permute-start | bytes 1105928 | tf_op jit(solution)/shard_map/ppermute | solution.py:484
  101.8 23.0 %collective-permute-start.26 = (bf16[4,5,48,384]{3,2,1,0:T(8,128)(2,1)}, bf16[4,5,48,384]{3,2,1,0:T(8,128)(2,1)}, u32[]{:S(2)}, u32[]{:S(2)}) collective-permute-start(bf16[4,5,48,384]{3,2,1,0:T(8,128)(2,1)} %pad_maximum_fusion.1.refs_2_), channel_id=1, source_target_pairs={{0,16},{16,0},{1,17},{17,1},{2,18},{18,2},{3,19},{19,3},{4,20},{20... | collective-permute-start | bytes 2211848 | tf_op jit(solution)/shard_map/ppermute | solution.py:484
  103.2 21.5 %collective-permute-start.25 = (bf16[4,5,48,384]{3,2,1,0:T(8,128)(2,1)}, bf16[4,5,48,384]{3,2,1,0:T(8,128)(2,1)}, u32[]{:S(2)}, u32[]{:S(2)}) collective-permute-start(bf16[4,5,48,384]{3,2,1,0:T(8,128)(2,1)} %pad_maximum_fusion.refs_1_.refs_0_), channel_id=1, source_target_pairs={{0,2},{1,3},{2,0},{3,1},{4,6},{5,7},{6,4},{7,5},{8,10},{9,11},{10,... | collective-permute-start | bytes 2211848 | tf_op jit(solution)/shard_map/ppermute | solution.py:529
  126.5 27.5 %collective-permute-start.34 = (bf16[4,1,240,384]{3,2,1,0:T(8,128)(2,1)S(1)}, bf16[4,1,240,384]{3,2,1,0:T(8,128)(2,1)S(1)}, u32[]{:S(2)}, u32[]{:S(2)}) collective-permute-start(bf16[4,1,240,384]{3,2,1,0:T(8,128)(2,1)S(1)} %pad_maximum_fusion.3.refs_9_.refs_2_), channel_id=1, source_target_pairs={{0,16},{16,0},{1,17},{17,1},{2,18},{18,2},{3,19},{19,3},{4,20},{20... | collective-permute-start | bytes 2211848 | tf_op jit(solution)/shard_map/ppermute | solution.py:484
  127.3 26.7 %collective-permute-start.33 = (bf16[4,1,240,384]{3,2,1,0:T(8,128)(2,1)S(1)}, bf16[4,1,240,384]{3,2,1,0:T(8,128)(2,1)S(1)}, u32[]{:S(2)}, u32[]{:S(2)}) collective-permute-start(bf16[4,1,240,384]{3,2,1,0:T(8,128)(2,1)S(1)} %pad_maximum_fusion.2.refs_8_.refs_0_), channel_id=1, source_target_pairs={{0,2},{1,3},{2,0},{3,1},{4,6},{5,7},{6,4},{7,5},{8,10},{9,11},{10,... | collective-permute-start | bytes 2211848 | tf_op jit(solution)/shard_map/ppermute | solution.py:529
  236.1 16.4 %collective-permute-start.44 = (bf16[8,240,768]{2,1,0:T(8,128)(2,1)}, bf16[8,240,768]{2,1,0:T(8,128)(2,1)S(1)}, u32[]{:S(2)}, u32[]{:S(2)}) collective-permute-start(bf16[8,240,768]{2,1,0:T(8,128)(2,1)} %get-tuple-element.161), channel_id=1, source_target_pairs={{0,1},{1,0},{2,3},{3,2},{4,5},{5,4},{6,7},{7,6},{8,9},{9,8},{10,11... | collective-permute-start | bytes 8847368 | tf_op jit(solution)/shard_map/ppermute | solution.py:479
  247.5 24.5 %collective-permute-start.46 = (bf16[8,240,768]{2,1,0:T(8,128)(2,1)}, bf16[8,240,768]{2,1,0:T(8,128)(2,1)}, u32[]{:S(2)}, u32[]{:S(2)}) collective-permute-start(bf16[8,240,768]{2,1,0:T(8,128)(2,1)} %get-tuple-element.167), channel_id=1, source_target_pairs={{0,1},{1,0},{2,3},{3,2},{4,5},{5,4},{6,7},{7,6},{8,9},{9,8},{10,11... | collective-permute-start | bytes 8847368 | tf_op jit(solution)/shard_map/ppermute | solution.py:479
  258.1 48.8 %collective-permute-start.45 = (bf16[4,2,120,768]{3,2,0,1:T(8,128)(2,1)}, bf16[4,2,120,768]{3,2,0,1:T(8,128)(2,1)}, u32[]{:S(2)}, u32[]{:S(2)}) collective-permute-start(bf16[4,2,120,768]{3,2,0,1:T(8,128)(2,1)} %fusion), channel_id=1, source_target_pairs={{0,16},{16,0},{1,17},{17,1},{2,18},{18,2},{3,19},{19,3},{4,20},{20... | collective-permute-start | bytes 4423688 | tf_op jit(solution)/shard_map/ppermute | solution.py:472
  288.6 46.3 %collective-permute-start.48 = (bf16[4,240,768]{2,1,0:T(8,128)(2,1)}, bf16[4,240,768]{2,1,0:T(8,128)(2,1)}, u32[]{:S(2)}, u32[]{:S(2)}) collective-permute-start(bf16[4,240,768]{2,1,0:T(8,128)(2,1)} %fusion.1.refs_1_), channel_id=1, source_target_pairs={{0,2},{1,3},{2,0},{3,1},{4,6},{5,7},{6,4},{7,5},{8,10},{9,11},{10,... | collective-permute-start | bytes 4423688 | tf_op jit(solution)/shard_map/ppermute | solution.py:472
  319.0 47.3 %collective-permute-start.47 = (bf16[4,120,768]{2,1,0:T(8,128)(2,1)}, bf16[4,120,768]{2,1,0:T(8,128)(2,1)S(1)}, u32[]{:S(2)}, u32[]{:S(2)}) collective-permute-start(bf16[4,120,768]{2,1,0:T(8,128)(2,1)} %fusion.12.refs_4_), channel_id=1, source_target_pairs={{0,2},{1,3},{2,0},{3,1},{4,6},{5,7},{6,4},{7,5},{8,10},{9,11},{10,... | collective-permute-start | bytes 2211848 | tf_op jit(solution)/shard_map/ppermute | solution.py:472
  320.6 25.8 %collective-permute-start.49 = (bf16[8,144,768]{2,1,0:T(8,128)(2,1)}, bf16[8,144,768]{2,1,0:T(8,128)(2,1)}, u32[]{:S(2)}, u32[]{:S(2)}) collective-permute-start(bf16[8,144,768]{2,1,0:T(8,128)(2,1)} %get-tuple-element.176.refs_0_), channel_id=1, source_target_pairs={{0,1},{1,0},{2,3},{3,2},{4,5},{5,4},{6,7},{7,6},{8,9},{9,8},{10,11... | collective-permute-start | bytes 5308424 | tf_op jit(solution)/shard_map/ppermute | solution.py:479
  337.4 45.5 %collective-permute-start.54 = (bf16[240,768]{1,0:T(8,128)(2,1)}, bf16[240,768]{1,0:T(8,128)(2,1)}, u32[]{:S(2)}, u32[]{:S(2)}) collective-permute-start(bf16[240,768]{1,0:T(8,128)(2,1)} %get-tuple-element.299.refs_1_), channel_id=1, source_target_pairs={{0,4},{1,5},{2,6},{3,7},{4,0},{5,1},{6,2},{7,3},{8,12},{9,13},{10,... | collective-permute-start | bytes 1105928 | tf_op jit(solution)/shard_map/ppermute | solution.py:472
  337.4 48.5 %collective-permute-start.55 = (bf16[240,768]{1,0:T(8,128)(2,1)}, bf16[240,768]{1,0:T(8,128)(2,1)}, u32[]{:S(2)}, u32[]{:S(2)}) collective-permute-start(bf16[240,768]{1,0:T(8,128)(2,1)} %get-tuple-element.298.refs_2_), channel_id=1, source_target_pairs={{0,8},{1,9},{2,10},{3,11},{4,12},{5,13},{6,14},{7,15},{8,0},{9,1},... | collective-permute-start | bytes 1105928 | tf_op jit(solution)/shard_map/ppermute | solution.py:472
  340.2 47.1 %collective-permute-start.56 = (bf16[240,768]{1,0:T(8,128)(2,1)}, bf16[240,768]{1,0:T(8,128)(2,1)}, u32[]{:S(2)}, u32[]{:S(2)}) collective-permute-start(bf16[240,768]{1,0:T(8,128)(2,1)} %get-tuple-element.297.refs_3_), channel_id=1, source_target_pairs={{0,12},{1,13},{2,14},{3,15},{4,8},{5,9},{6,10},{7,11},{8,4},{9,5},... | collective-permute-start | bytes 1105928 | tf_op jit(solution)/shard_map/ppermute | solution.py:472
  364.8 28.1 %collective-permute-start.58 = (bf16[4,2,72,768]{3,2,1,0:T(8,128)(2,1)}, bf16[4,2,72,768]{3,2,1,0:T(8,128)(2,1)}, u32[]{:S(2)}, u32[]{:S(2)}) collective-permute-start(bf16[4,2,72,768]{3,2,1,0:T(8,128)(2,1)} %fusion.11.refs_4_), channel_id=1, source_target_pairs={{0,16},{16,0},{1,17},{17,1},{2,18},{18,2},{3,19},{19,3},{4,20},{20... | collective-permute-start | bytes 2654216 | tf_op jit(solution)/shard_map/ppermute | solution.py:472
  367.4 33.3 %collective-permute-start.50 = (bf16[120,768]{1,0:T(8,128)(2,1)}, bf16[120,768]{1,0:T(8,128)(2,1)}, u32[]{:S(2)}, u32[]{:S(2)}) collective-permute-start(bf16[120,768]{1,0:T(8,128)(2,1)} %get-tuple-element.303.refs_1_), channel_id=1, source_target_pairs={{0,4},{1,5},{2,6},{3,7},{4,0},{5,1},{6,2},{7,3},{8,12},{9,13},{10,... | collective-permute-start | bytes 552968 | tf_op jit(solution)/shard_map/ppermute | solution.py:472
  382.9 17.8 %collective-permute-start.51 = (bf16[120,768]{1,0:T(8,128)(2,1)}, bf16[120,768]{1,0:T(8,128)(2,1)S(1)}, u32[]{:S(2)}, u32[]{:S(2)}) collective-permute-start(bf16[120,768]{1,0:T(8,128)(2,1)} %get-tuple-element.305.refs_2_), channel_id=1, source_target_pairs={{0,8},{1,9},{2,10},{3,11},{4,12},{5,13},{6,14},{7,15},{8,0},{9,1},... | collective-permute-start | bytes 552968 | tf_op jit(solution)/shard_map/ppermute | solution.py:472
  400.7 18.4 %collective-permute-start.64 = (bf16[8,48,1024]{2,1,0:T(8,128)(2,1)}, bf16[8,48,1024]{2,1,0:T(8,128)(2,1)}, u32[]{:S(2)}, u32[]{:S(2)}) collective-permute-start(bf16[8,48,1024]{2,1,0:T(8,128)(2,1)} %get-tuple-element.210), channel_id=1, source_target_pairs={{0,1},{1,0},{2,3},{3,2},{4,5},{5,4},{6,7},{7,6},{8,9},{9,8},{10,11... | collective-permute-start | bytes 2359304 | tf_op jit(solution)/shard_map/ppermute | solution.py:479
  404.1 16.6 %collective-permute-start.59 = (bf16[4,72,768]{2,1,0:T(8,128)(2,1)}, bf16[4,72,768]{2,1,0:T(8,128)(2,1)S(1)}, u32[]{:S(2)}, u32[]{:S(2)}) collective-permute-start(bf16[4,72,768]{2,1,0:T(8,128)(2,1)} %fusion.13.refs_9_), channel_id=1, source_target_pairs={{0,2},{1,3},{2,0},{3,1},{4,6},{5,7},{6,4},{7,5},{8,10},{9,11},{10,... | collective-permute-start | bytes 1327112 | tf_op jit(solution)/shard_map/ppermute | solution.py:472
  (100 other events, 1173.6 us)

commit v5 on v4

--- a/solution.py
+++ b/solution.py
@@ -56,39 +56,47 @@
     return jnp.where(low_side, own, other), jnp.where(low_side, other, own)
 
 
-def exchange_steps():
-    steps = []
-    for axis in ("fsdp", "rep"):
-        size = lax.axis_size(axis)
-        bit = 1
-        while bit < size:
-            steps.append((axis, size, bit))
-            bit *= 2
-    return steps
+def combined(first, second, micro_count):
+    top_a, top_b = first[:micro_count], second[:micro_count]
+    top = jnp.maximum(top_a, top_b)
+    parts = slice(micro_count, 2 * micro_count)
+    total = first[parts] * jnp.exp(top_a - top) + second[parts] * jnp.exp(top_b - top)
+    return jnp.concatenate([top, total, first[2 * micro_count :] + second[2 * micro_count :]])
 
 
 def column_totals(top, total, sums):
     micro_count = top.shape[0]
-    for axis, size, bit in exchange_steps():
-        packed = jnp.concatenate([top, total, sums], axis=0)
+    packed = jnp.concatenate([top, total, sums], axis=0)
+    owners, reps = lax.axis_size("fsdp"), lax.axis_size("rep")
+    steps = [("fsdp", owners, 1), ("fsdp", owners, 2)]
+    steps += [("rep", reps, 1 << bit) for bit in range(reps.bit_length() - 1)]
+    for axis, size, bit in steps:
         other = lax.ppermute(packed, axis, bit_swap(size, bit))
-        first, second = ordered_pair(packed, other, axis, bit)
-        top_a, top_b = first[:micro_count], second[:micro_count]
-        top = jnp.maximum(top_a, top_b)
-        total = first[micro_count : 2 * micro_count] * jnp.exp(top_a - top) + second[
-            micro_count : 2 * micro_count
-        ] * jnp.exp(top_b - top)
-        sums = first[2 * micro_count :] + second[2 * micro_count :]
-    return top, total, sums
+        packed = combined(*ordered_pair(packed, other, axis, bit), micro_count)
+    turns = [packed] + [
+        lax.ppermute(packed, "fsdp", bit_swap(owners, turn)) for turn in range(4, owners, 4)
+    ]
+    bit = 4
+    while len(turns) > 1:
+        turns = [
+            combined(*ordered_pair(first, second, "fsdp", bit), micro_count)
+            for first, second in zip(turns[::2], turns[1::2], strict=True)
+        ]
+        bit *= 2
+    packed = turns[0]
+    return packed[:micro_count], packed[micro_count : 2 * micro_count], packed[2 * micro_count :]
 
 
 def sum_over(value, axis):
     size = lax.axis_size(axis)
-    bit = 1
-    while bit < size:
+    for bit in (1, 2):
         value = value + lax.ppermute(value, axis, bit_swap(size, bit))
-        bit *= 2
-    return value
+    turns = [value] + [
+        lax.ppermute(value, axis, bit_swap(size, turn)) for turn in range(4, size, 4)
+    ]
+    while len(turns) > 1:
+        turns = [first + second for first, second in zip(turns[::2], turns[1::2], strict=True)]
+    return turns[0]
 
 
 def padded_rows(rows):
@@ -141,21 +149,9 @@
 
 
 def gelu_pair(values):
-    size = jnp.abs(values)
-    turn = 1.0 / (1.0 + (0.3275911 * 0.7071067811865476) * size)
+    share = 0.5 + 0.5 * lax.erf(values * 0.7071067811865476)
     bell = jnp.exp(-0.5 * values * values)
-    poly = turn * (
-        0.5 * 0.254829592
-        + turn
-        * (
-            0.5 * -0.284496736
-            + turn
-            * (0.5 * 1.421413741 + turn * (0.5 * -1.453152027 + turn * (0.5 * 1.061405429)))
-        )
-    )
-    tail = poly * bell
-    share = jnp.where(values >= 0, 1.0 - tail, tail)
-    return values * share, share + values * (bell * 0.3989422804014327)
+    return values * share, share + values * bell * 0.3989422804014327
 
 
 def widen_heads_kernel(
@@ -213,6 +209,19 @@
     pl.when(step == pl.num_programs(0) - 1)(keep.wait)
 
 
+def head_groups(width, pair):
+    starts = range(0, width, 2 * pair)
+    return [[slice(at, at + pair), slice(at + pair, at + 2 * pair)] for at in starts]
+
+
+def by_head(pairs, first_half):
+    items = []
+    for both in pairs:
+        zero = jnp.zeros_like(both)
+        items += [jnp.where(first_half, both, zero), jnp.where(first_half, zero, both)]
+    return items
+
+
 def attend_kernel(counts_ref, heads_ref, values_ref, *refs, head_size):
     attended_ref = refs[-1]
     live_count = counts_ref[pl.program_id(0)]
@@ -221,19 +230,23 @@
     key_live = jnp.where(
         lax.broadcasted_iota(jnp.int32, (1, slots), 1) < live_count, 1.0, 0.0
     )
-    first_half = lax.broadcasted_iota(jnp.int32, (slots, 2 * head_size), 1) < head_size
-    zero = jnp.zeros((slots, 2 * head_size), jnp.bfloat16)
-    for at in range(0, width, 2 * head_size):
-        columns = slice(at, at + 2 * head_size)
-        queries, keys = (heads_ref[part, :, columns] for part in range(2))
-        values = values_ref[0, :, columns]
-        outs = []
-        for half in range(2):
-            own = jnp.where(first_half, queries, zero) if half == 0 else jnp.where(first_half, zero, queries)
-            weights = jnp.exp2(product_along(own, keys) * factor) * key_live
-            share = weights * (1.0 / jnp.sum(weights, axis=1, keepdims=True))
-            outs.append(product(share.astype(jnp.bfloat16), values))
-        attended_ref[0, :, columns] = jnp.where(first_half, outs[0], outs[1]).astype(jnp.bfloat16)
+    pair = 2 * head_size
+    first_half = lax.broadcasted_iota(jnp.int32, (slots, pair), 1) < head_size
+    for columns in head_groups(width, pair):
+        queries, keys = ([heads_ref[part, :, at] for at in columns] for part in range(2))
+        values = [values_ref[0, :, at] for at in columns]
+        own = by_head(queries, first_half)
+        each = range(len(own))
+        weights = [product_along(own[h], keys[h // 2]) for h in each]
+        weights = [jnp.exp2(weights[h] * factor) * key_live for h in each]
+        share = [
+            weights[h] * (1.0 / jnp.sum(weights[h], axis=1, keepdims=True)) for h in each
+        ]
+        outs = [product(share[h].astype(jnp.bfloat16), values[h // 2]) for h in each]
+        for index, at in enumerate(columns):
+            attended_ref[0, :, at] = jnp.where(
+                first_half, outs[2 * index], outs[2 * index + 1]
+            ).astype(jnp.bfloat16)
 
 
 def join_kernel(
@@ -322,29 +335,39 @@
 
     factor = head_size ** (-0.5)
     key_live = lax.broadcasted_iota(jnp.int32, (slots, 1), 0) < live_count
-    first_half = lax.broadcasted_iota(jnp.int32, (slots, 2 * head_size), 1) < head_size
-    zero = jnp.zeros((slots, 2 * head_size), jnp.bfloat16)
-    for at in range(0, width, 2 * head_size):
-        columns = slice(at, at + 2 * head_size)
-        queries, keys = (heads_ref[part, :, columns] for part in range(2))
-        values = values_ref[0, :, columns]
-        above = grad_attended_ref[0, :, columns]
-        grad_queries, grad_keys, grad_values = [], [], []
-        for half in range(2):
-            pick = lambda both: jnp.where(first_half, both, zero) if half == 0 else jnp.where(first_half, zero, both)
-            own_queries, own_above = pick(queries), pick(above)
-            weights = jnp.exp2(product_along(keys, own_queries) * (factor * 1.4426950408889634))
-            weights = jnp.where(key_live, weights, 0.0)
-            share = weights * (1.0 / jnp.sum(weights, axis=0, keepdims=True))
-            grad_share = product_along(values, own_above)
-            dot_row = jnp.sum(share * grad_share, axis=0, keepdims=True)
-            grad_raw = (share * (grad_share - dot_row) * factor).astype(jnp.bfloat16)
-            grad_values.append(product(share.astype(jnp.bfloat16), own_above))
-            grad_keys.append(product(grad_raw, own_queries))
-            grad_queries.append(product_across(grad_raw, keys))
-        grad_qkv_ref[2, :, columns] = (grad_values[0] + grad_values[1]).astype(jnp.bfloat16)
-        grad_ref[1, :, columns] = grad_keys[0] + grad_keys[1]
-        grad_ref[0, :, columns] = jnp.where(first_half, grad_queries[0], grad_queries[1])
+    pair = 2 * head_size
+    first_half = lax.broadcasted_iota(jnp.int32, (slots, pair), 1) < head_size
+    for columns in head_groups(width, pair):
+        queries, keys = ([heads_ref[part, :, at] for at in columns] for part in range(2))
+        values = [values_ref[0, :, at] for at in columns]
+        own_queries = by_head(queries, first_half)
+        own_above = by_head([grad_attended_ref[0, :, at] for at in columns], first_half)
+        each = range(len(own_queries))
+        weights = [product_along(keys[h // 2], own_queries[h]) for h in each]
+        grad_share = [product_along(values[h // 2], own_above[h]) for h in each]
+        weights = [
+            jnp.where(key_live, jnp.exp2(weights[h] * (factor * 1.4426950408889634)), 0.0)
+            for h in each
+        ]
+        share = [weights[h] * (1.0 / jnp.sum(weights[h], axis=0, keepdims=True)) for h in each]
+        dot_row = [jnp.sum(share[h] * grad_share[h], axis=0, keepdims=True) for h in each]
+        grad_raw = [
+            (share[h] * (grad_share[h] - dot_row[h]) * factor).astype(jnp.bfloat16) for h in each
+        ]
+        share = [share[h].astype(jnp.bfloat16) for h in each]
+        for index, at in enumerate(columns):
+            one, two = 2 * index, 2 * index + 1
+            grad_qkv_ref[2, :, at] = (
+                product(share[one], own_above[one]) + product(share[two], own_above[two])
+            ).astype(jnp.bfloat16)
+            grad_ref[1, :, at] = product(grad_raw[one], own_queries[one]) + product(
+                grad_raw[two], own_queries[two]
+            )
+            grad_ref[0, :, at] = jnp.where(
+                first_half,
+                product_across(grad_raw[one], keys[index]),
+                product_across(grad_raw[two], keys[index]),
+            )
     mixer = head_mixer(head_size)
     for part in range(2):
         gain = gain_ref[part]
@@ -356,8 +379,26 @@
         grad_qkv_ref[part] = (rstd_ref[part] * back).astype(jnp.bfloat16)
 
 
+def hidden_back_kernel(grad_act_ref, wide_ref, *refs):
+    out_ref, total_ref = refs[-2:]
+    step = pl.program_id(0)
+    term = product_along(grad_act_ref[0], wide_ref[0])
+
+    @pl.when(step == 0)
+    def _():
+        total_ref[...] = term
+
+    @pl.when(step > 0)
+    def _():
+        total_ref[...] += term
+
+    @pl.when(step == pl.num_programs(0) - 1)
+    def _():
+        out_ref[...] = total_ref[...]
+
+
 def merge_back_kernel(
-    counts_ref, grad_qkv_ref, grad_act_ref, wide_hbm, wide_hidden_hbm, merged_ref, grad_stream_ref, gain_ref,
+    counts_ref, grad_qkv_ref, grad_hidden_ref, wide_hbm, merged_ref, grad_stream_ref, gain_ref,
     map_ref, row_ref, column_ref, *refs, base,
 ):
     grad_patch_ref, grad_place_ref, sums_ref, wide_ref, sem = refs[-5:]
@@ -366,11 +407,7 @@
     slots, width = merged_ref.shape[1:]
     blocks = wide_ref.shape[0]
     copies = [
-        pltpu.make_async_copy(
-            wide_hbm.at[part] if part < 3 else wide_hidden_hbm.at[part - 3],
-            wide_ref.at[part],
-            sem.at[part],
-        )
+        pltpu.make_async_copy(wide_hbm.at[part], wide_ref.at[part], sem.at[part])
         for part in range(blocks)
     ]
 
@@ -381,11 +418,10 @@
         sums_ref[...] = jnp.zeros_like(sums_ref)
         grad_place_ref[...] = jnp.zeros_like(grad_place_ref)
 
-    grad_normed = jnp.zeros((slots, width), jnp.float32)
+    grad_normed = grad_hidden_ref[...]
     for part in range(blocks):
         pl.when(image == 0)(copies[part].wait)
-        grads = grad_qkv_ref[part] if part < 3 else grad_act_ref[part - 3]
-        grad_normed = grad_normed + product_along(grads, wide_ref[part])
+        grad_normed = grad_normed + product_along(grad_qkv_ref[part], wide_ref[part])
     unit, rstd = normal_rows(merged_ref[0])
     sums_ref[0:1, :] += jnp.sum(grad_normed * unit, axis=0, keepdims=True)
     slanted = grad_normed * gain_ref[...]
@@ -467,17 +503,20 @@
         added(picked(terms, axis, index ^ turn)).astype(jnp.bfloat16) for turn in range(1, count)
     ]
     after = yield sends
-    kept = picked(terms, axis, index)
-    for turn, send in enumerate(sends, 1):
-        kept.append(lax.ppermute(send, mesh_axis, bit_swap(size, turn * stride)))
-    return behind(kept, after)
+    got = [
+        lax.ppermute(send, mesh_axis, bit_swap(size, turn * stride))
+        for turn, send in enumerate(sends, 1)
+    ]
+    return picked(terms, axis, index) + behind(got, after)
 
 
 def core_terms(mine, other):
-    chips, rows, width = mine.shape
     after = yield [other]
-    got = lax.ppermute(other, "fsdp", bit_swap(lax.axis_size("fsdp"), 1))
-    return [term.reshape(chips // 2, 2, rows, width) for term in behind([mine, got], after)]
+    got = behind([core_swap(other)], after)[0]
+    return [
+        term.reshape(*term.shape[:-3], term.shape[-3] // 2, 2, *term.shape[-2:])
+        for term in (mine, got)
+    ]
 
 
 def rep_swap(own):
@@ -489,23 +528,30 @@
     return place // 4, (place // 2) % 2
 
 
-def reduce_rows_first(mine, other):
+def column_parts(width):
+    reps = lax.axis_size("rep")
+    return reps if width % (128 * reps) == 0 else 1
+
+
+def reduce_columns(mine, other):
     high, middle = places()
-    reps = lax.axis_size("rep")
-    count = mine.shape[0] // 2
+    parts, count = mine.shape[0], mine.shape[1] // 2
     terms = yield from core_terms(mine, other)
-    terms = [
-        term.reshape(count, 2, reps, term.shape[2] // reps, term.shape[3]) for term in terms
-    ]
-    terms = yield from traded(terms, 2, lax.axis_index("rep"), reps, "rep", 1)
+    if parts > 1:
+        terms = yield from traded(terms, 0, lax.axis_index("rep"), parts, "rep", 1)
+    else:
+        terms = [term[0] for term in terms]
     terms = yield from traded(terms, 1, middle, 2, "fsdp", 2)
     terms = yield from traded(terms, 0, high, count, "fsdp", 4)
     own = added(terms).astype(jnp.bfloat16)
-    yield [own]
-    if reps == 2:
-        first, second = ordered_pair(own, rep_swap(own), "rep", 1)
-        return jnp.concatenate([first, second], axis=0)
-    return lax.all_gather(own, "rep", axis=0, tiled=True)
+    after = yield [own]
+    if parts == 1:
+        return lax.psum(own, "rep")
+    if parts == 2:
+        got = behind([rep_swap(own)], after)[0]
+        first, second = ordered_pair(own, got, "rep", 1)
+        return jnp.concatenate([first, second], axis=1)
+    return lax.all_gather(own, "rep", axis=1, tiled=True)
 
 
 def reduce_rows_last(mine, other):
@@ -515,9 +561,10 @@
     terms = yield from traded(terms, 1, middle, 2, "fsdp", 2)
     terms = yield from traded(terms, 0, high, count, "fsdp", 4)
     own = added(terms).astype(jnp.bfloat16)
-    yield [own]
+    after = yield [own]
     if lax.axis_size("rep") == 2:
-        return added([own, rep_swap(own)]).astype(jnp.bfloat16)
+        got = behind([rep_swap(own)], after)
+        return added([own, *got]).astype(jnp.bfloat16)
     return lax.psum(own, "rep")
 
 
@@ -697,11 +744,16 @@
 
 
 def split_cores(result, core, mine_ref, other_ref):
-    chips, rows = mine_ref.shape[:2]
+    chips, rows, width = mine_ref.shape[-3:]
     pairs = result.astype(jnp.bfloat16).reshape(chips, 2, rows, result.shape[1])
     first, second = pairs[:, 0], pairs[:, 1]
-    mine_ref[...] = jnp.where(core == 0, first, second)
-    other_ref[...] = jnp.where(core == 0, second, first)
+    for ref, (left, right) in ((mine_ref, (first, second)), (other_ref, (second, first))):
+        values = jnp.where(core == 0, left, right)
+        if len(ref.shape) == 3:
+            ref[...] = values
+        else:
+            for part in range(ref.shape[0]):
+                ref[part] = values[:, :, part * width : (part + 1) * width]
 
 
 def narrow_grad_kernel(
@@ -709,7 +761,7 @@
 ):
     step = pl.program_id(0)
     width = branch_ref.shape[1]
-    chips, rows = mine_hbm.shape[:2]
+    parts, chips, rows, columns = mine_hbm.shape
 
     @pl.when(step == 0)
     def _():
@@ -731,10 +783,12 @@
         for chip in range(chips):
             for side, out in enumerate((mine_hbm, other_hbm)):
                 owner = 2 * chip + (core ^ side)
-                source = total_ref.at[pl.ds(pl.multiple_of(owner * rows, rows), rows), :]
-                copies.append(
-                    pltpu.make_async_copy(source, out.at[chip], sem.at[2 * chip + side])
-                )
+                at = pl.ds(pl.multiple_of(owner * rows, rows), rows)
+                for part in range(parts):
+                    source = total_ref.at[at, part * columns : (part + 1) * columns]
+                    copies.append(
+                        pltpu.make_async_copy(source, out.at[part, chip], sem.at[len(copies)])
+                    )
         for copy in copies:
             copy.start()
         for copy in copies:
@@ -827,9 +881,10 @@
         )
     update(3, everything, everything, narrow_ref[...])
     update(4, everything, everything, hidden_ref[(blocks - 3) * wide_rows :, :])
-    beside = embed_ref[:, width:].astype(jnp.float32).T
-    slots = weights[1].shape[0]
-    update(1, everything, everything, beside[:slots, :])
+    beside = embed_ref[:, width:].astype(jnp.float32)
+    slots = weights[1].shape[1]
+    update(1, everything, everything, beside[:, :slots])
+    beside = beside.T
     at = padded_rows(slots)
     scale_rows = weights[5].shape[0]
     update(5, everything, everything, beside[at : at + scale_rows, :])
@@ -899,13 +954,14 @@
     small_rows = -(-(slots + table_rows) // 128) * 128
     beside = jnp.concatenate(
         [
-            jnp.pad(positions, ((0, spare), (0, 0))),
-            scales,
-            biases.reshape(bias_rows, wide_rows),
-        ]
-    )
-    beside = jnp.pad(beside, ((0, small_rows - beside.shape[0]), (0, 0))).astype(low)
-    small_piece = jnp.concatenate([embedder.astype(low), beside.T], axis=1)
+            jnp.pad(positions.T, ((0, 0), (0, spare))),
+            scales.T,
+            biases.reshape(bias_rows, wide_rows).T,
+        ],
+        axis=1,
+    )
+    beside = jnp.pad(beside, ((0, 0), (0, small_rows - beside.shape[1]))).astype(low)
+    small_piece = jnp.concatenate([embedder.astype(low), beside], axis=1)
     wide_low = widener.astype(low)
     blocks_of = lambda first, count: [
         wide_low[:, k * model_width : (k + 1) * model_width] for k in range(first, first + count)
@@ -1143,6 +1199,9 @@
     chips = owners // 2
     branch_rows = grad_branch.reshape(rows, model_width)
     halves = lambda count, width: [shape((chips, count, width), low)] * 2
+    parts_wide = column_parts(model_width)
+    part_width = model_width // parts_wide
+    split_halves = lambda count: [shape((parts_wide, chips, count, part_width), low)] * 2
     narrow_halves = pl.pallas_call(
         narrow_grad_kernel,
         grid_spec=pltpu.PrefetchScalarGridSpec(
@@ -1156,15 +1215,15 @@
             out_specs=[anywhere] * 2,
             scratch_shapes=[
                 pltpu.VMEM((hidden_width + model_width, model_width), low),
-                pltpu.SemaphoreType.DMA((2 * chips,)),
+                pltpu.SemaphoreType.DMA((2 * parts_wide * chips,)),
             ],
         ),
-        out_shape=halves(narrow_rows, model_width),
+        out_shape=split_halves(narrow_rows),
         compiler_params=roomy,
         cost_estimate=long,
         name="narrow_grad",
     )(core, attended.reshape(rows, model_width), hidden, branch_rows)
-    narrow_flow = Flow(reduce_rows_first(*narrow_halves))
+    narrow_flow = Flow(reduce_columns(*narrow_halves))
     narrow_flow.go()
     owner_block = block((chips, wide_rows, model_width), lambda k, _: (0, k, 0))
     few = padded_rows(images)
@@ -1205,6 +1264,22 @@
 
     head_gains = scale_float[2:4].reshape(2, 1, model_width)
     guards = narrow_flow.go()
+    grad_hidden = pl.pallas_call(
+        hidden_back_kernel,
+        grid=(hidden_blocks,),
+        in_specs=[
+            block((1, rows, model_width), lambda k: (k, 0, 0)),
+            block((1, model_width, model_width), lambda k: (k, 0, 0)),
+        ]
+        + [anywhere] * len(guards),
+        out_specs=whole(rows, model_width),
+        out_shape=shape((rows, model_width), f32),
+        scratch_shapes=[pltpu.VMEM((rows, model_width), f32)],
+        compiler_params=roomy,
+        cost_estimate=long,
+        name="hidden_back",
+    )(grad_act, wide_hidden, *guards)
+    guards = [grad_hidden] + hidden_flow.go()
     grad_qkv, head_sums = [], 0.0
     for part in range(parts):
         base = part * per_part
@@ -1227,8 +1302,6 @@
         grad_qkv.append(grads)
         head_sums = head_sums + sums_part
         guards = [grads]
-        if part == 0:
-            guards += hidden_flow.go(grads)
     guards += narrow_flow.go(grads)
     qkv_halves = pl.pallas_call(
         lambda core_ref, normed_ref, *refs: wide_grad_kernel(
@@ -1240,14 +1313,14 @@
             in_specs=[whole(rows, model_width)]
             + [block((1, part_rows, model_width), lambda k, _: (k, 0, 0))] * parts
             + [anywhere] * len(guards),
-            out_specs=[owner_block] * 2,
+            out_specs=[block((parts_wide, chips, wide_rows, part_width), lambda k, _: (0, 0, k, 0))] * 2,
         ),
-        out_shape=halves(3 * wide_rows, model_width),
+        out_shape=split_halves(3 * wide_rows),
         compiler_params=roomy,
         cost_estimate=long,
         name="qkv_grad",
     )(core, normed_rows, *grad_qkv, *guards)
-    qkv_flow = Flow(reduce_rows_first(*qkv_halves))
+    qkv_flow = Flow(reduce_columns(*qkv_halves))
     guards = qkv_flow.go()
     grad_patches, grad_places, merge_sums = [], [], 0.0
     for part in range(parts):
@@ -1257,8 +1330,7 @@
             per_part,
             [
                 image_columns(3),
-                shifted_columns(base, hidden_blocks),
-                anywhere,
+                block((slots, model_width), lambda image, counts, base=base: (base + image, 0)),
                 anywhere,
                 shifted(base, slots),
                 shifted(base, slots),
@@ -1275,12 +1347,12 @@
                 shape((8, model_width), f32),
             ],
             [
-                pltpu.VMEM((3 + hidden_blocks, model_width, model_width), low),
-                pltpu.SemaphoreType.DMA((3 + hidden_blocks,)),
+                pltpu.VMEM((3, model_width, model_width), low),
+                pltpu.SemaphoreType.DMA((3,)),
             ],
             name="merge_back",
         )(
-            live_counts, grad_qkv[part], grad_act, wide_qkv, wide_hidden, merged, grad_stream,
+            live_counts, grad_qkv[part], grad_hidden, wide_qkv, merged, grad_stream,
             scale_float[0:1], slot_map, row_weight, column_weight, *guards,
         )
         grad_patches.append(grads.reshape(part_rows, model_width))
@@ -1291,7 +1363,7 @@
             guards += hidden_flow.go(grads) + qkv_flow.go(grads)
         elif part == 1:
             guards += narrow_flow.go(grads)
-    guards += hidden_flow.go(grads) + qkv_flow.go(grads)
+    guards += hidden_flow.go(grads) + qkv_flow.go(grads) + narrow_flow.go(grads)
     grad_scale = jnp.stack([merge_sums[0], out_sums[hidden_blocks + 1], head_sums[0], head_sums[1]])
     grad_bias = jnp.concatenate([out_sums[: hidden_blocks + 1], merge_sums[1:2]]).reshape(
         owners, bias_rows, wide_rows
@@ -1320,12 +1392,16 @@
         name="embed_grad",
     )(core, pixel_rows.reshape(rows, patch_size), *grad_patches, *grad_places, table, *guards)
     embed_flow = Flow(reduce_rows_last(*embed_halves))
+    embed_flow.go()
+    sent = embed_flow.go()
+    sent = qkv_flow.go(sent)
+    narrow_flow.go(sent)
+    hidden_flow.go(sent)
+    embed_flow.go()
+    sent = embed_flow.go(qkv_flow.go())
+    qkv_flow.go(sent)
     flows = (narrow_flow, hidden_flow, qkv_flow, embed_flow)
-    while any(flow.result is None for flow in flows):
-        for flow in flows:
-            if flow.result is None:
-                flow.go()
-    shards = [flow.result for flow in flows]
+    shards = [flow.finish() for flow in flows]
     squares_sum = pl.pallas_call(
         square_kernel,
         out_shape=shape((8, 128), f32),
@@ -1353,7 +1429,8 @@
         square_biases,
     )
     as_rows = lambda arrays: [
-        array.reshape(-1, wide_rows) if array.ndim == 1 else array for array in arrays
+        array.reshape(-1, wide_rows) if array.ndim == 1 else array.T if index % 7 == 1 else array
+        for index, array in enumerate(arrays)
     ]
     outs = pl.pallas_call(
         functools.partial(update_kernel, wide_rows=wide_rows),
@@ -1362,7 +1439,8 @@
         name="update",
     )(squares_sum, *shards, *as_rows(weights), *as_rows(moments), *as_rows(squares))
     outs = [
-        out.reshape(array.shape) for out, array in zip(outs, weights * 2, strict=True)
+        out.T if index % 7 == 1 else out.reshape(array.shape)
+        for index, (out, array) in enumerate(zip(outs, weights * 2, strict=True))
     ]
     return (objective, weight_total_all, total_norm, *outs)
 

time: 493 us -> 458 us (0.929)
  local copies, waits for them, and re-layouts: 46.3 us -> 21.9 us
  Pallas kernels: 239 us -> 220 us
  starting transfers between devices: 70.3 us -> 80.1 us
    ppermute x22 -> x24, waiting for transfers between devices: 12.3 us -> 30.6 us  [the longest x18 24.7 us: traded(): lax.ppermute(send, mesh_axis, bit_swap(size, turn * stride))]
    pallas_call x3, Pallas kernels: 43.2 us -> 28.7 us  [per_device(): image_call(functools.partial(merge_back_kernel, base=base), per_part, [im...]
    pallas_call x0 -> x1, Pallas kernels: none -> 12.4 us  [per_device(): pl.pallas_call(hidden_back_kernel, grid=(hidden_blocks,), in_specs=[block...]
    ppermute x22 -> x24, starting transfers between devices: 23.5 us -> 35.5 us  [the longest x18 26.8 us: traded(): lax.ppermute(send, mesh_axis, bit_swap(size, turn * stride))]
    pallas_call x3, Pallas kernels: 40.3 us -> 29.2 us  [per_device(): image_call(functools.partial(attend_back_kernel, base=base, head_size=hea...]
    ppermute x10, waiting for transfers between devices: 19 us -> 7.96 us  [rep_swap(): return lax.ppermute(own, 'rep', bit_swap(2, 1))]
    squeeze x10 -> x0, local copies, waits for them, and re-layouts: 9.25 us -> none  [picked(): lax.dynamic_index_in_dim(term, index, axis, keepdims=False)]
    unnamed x128 -> x105, local copies, waits for them, and re-layouts: 9.68 us -> 1.92 us
  transfers between devices with their start and end apart: 74 -> 76, of which waited for: 29 -> 29; matrix products, arithmetic and copies ran while one was open for 15% -> 12% of each run, Pallas kernels for 37% -> 34%
where the time goes in v5:
time: 458 us; the launch traced here: 453 us
  Pallas kernels  220 us (48%)
  starting transfers between devices  80.1 us (17%)
  waiting for transfers between devices  71 us (16%)
  other arithmetic  50.1 us (11%)
  local copies, waits for them, and re-layouts  21.9 us (5%)
  between operations  5.81 us (1%)
    pallas_call x3, Pallas kernels, per_device(): image_call(functools.partial(attend_back_kernel, base=base, head_size=hea...  29.2 us
    pallas_call x3, Pallas kernels, per_device(): image_call(functools.partial(merge_back_kernel, base=base), per_part, [im...  28.7 us
    ppermute x18, starting transfers between devices, traded(): lax.ppermute(send, mesh_axis, bit_swap(size, turn * stride))  26.8 us
    ppermute x18, waiting for transfers between devices, traded(): lax.ppermute(send, mesh_axis, bit_swap(size, turn * stride))  24.7 us
    ppermute x12, starting transfers between devices, high_gather(): lax.ppermute(own, 'fsdp', bit_swap(owners, turn))  21.4 us
    pallas_call x1, Pallas kernels, per_device(): image_call(branch_kernel, images, [per_image(slots, model_width), per_ima...  20.9 us
    convert_element_type x10, other arithmetic, traded(): added(picked(terms, axis, index ^ turn)).astype(jnp.bfloat16)  20.9 us
    pallas_call x1, Pallas kernels, per_device(): pl.pallas_call(functools.partial(widen_hidden_kernel, found=found, chunk=...  17.8 us
  transfers between devices with their start and end apart: 76, of which 29 were waited for; matrix products, arithmetic and copies ran while one was open for 12% of the time, Pallas kernels for 34%

profile of v5, /device:TPU:0, one launch (start us, length us, event | category | flops | bytes accessed | tf_op | source)
XLA Modules:
  0.0 452.9 jit_solution(5552172631217683143)
XLA Ops:
  4.9 4.1 collective-permute-start.1
  12.0 4.8 %collective-permute-done.1 = bf16[1,48,1024]{2,1,0:T(8,128)(2,1)S(1)} collective-permute-done((bf16[1,48,1024]{2,1,0:T(8,128)(2,1)S(1)}, bf16[1,48,1024]{2,1,0:T(8,128)(2,1)S(1)}, u32[]{:S(2)}, u32[]{:S(2)}) %collective-permute-start.1) | collective-permute-done | bytes 98336 | tf_op jit(solution)/shard_map/ppermute | solution.py:582
  26.7 6.3 %collective-permute-done.7 = bf16[3,48,384]{2,1,0:T(8,128)(2,1)S(1)} collective-permute-done((bf16[3,48,384]{2,1,0:T(8,128)(2,1)S(1)}, bf16[3,48,384]{2,1,0:T(8,128)(2,1)S(1)}, u32[]{:S(2)}, u32[]{:S(2)}) %collective-permute-start.7) | collective-permute-done | bytes 110624 | tf_op jit(solution)/shard_map/ppermute | solution.py:582
  52.5 3.7 assemble_small.1
  64.1 10.1 %embed.1 = (f32[6,208,768]{2,1,0:T(8,128)}, bf16[6,208,768]{2,1,0:T(8,128)(2,1)}) custom-call(s32[6]{0:T(128)} %reshape.380.counts_ref, bf16[6,208,768]{2,1,0:T(8,128)(2,1)} %pad.37.pixel_ref, s32[6,1,208]{2,1,0:T(1,128)} %pad.38.map_ref, f32[6,1,208]{2,1,0:T(1,128)} %get-tuple-element.276.row_ref, f32[6,208,1]{2,1,0:T(8,128)} %copy.66.column_ref, ...), custom_call_target="tpu_custom_call" | custom-call | flops 60000002048 | bytes 1000 | tf_op jit(solution)/shard_map/embed/pallas_call | solution.py:993
  83.0 15.2 %widen_heads.1 = (bf16[2,1248,768]{2,1,0:T(8,128)(2,1)}, f32[2,1248,768]{2,1,0:T(8,128)}, bf16[3,768,768]{2,1,0:T(8,128)(2,1)}) custom-call(s32[2]{0:T(128)} %pad_add_fusion.place_ref, bf16[1248,768]{1,0:T(8,128)(2,1)} %bitcast.296, f32[2,1,768]{2,1,0:T(1,128)} %reshape.389.gain_ref, bf16[4,3,48,384]{3,2,1,0:T(8,128)(2,1)} %copy-done.19, ...), custom_call_target="tpu_custom_call" | custom-call | flops 60000002048 | bytes 1000 | tf_op jit(solution)/shard_map/widen_heads/pallas_call | solution.py:1021
  105.1 4.8 %widen_values.1.values_ref = bf16[1,1248,768]{2,1,0:T(8,128)(2,1)} custom-call(bf16[1248,768]{1,0:T(8,128)(2,1)} %bitcast.297, bf16[3,768,768]{2,1,0:T(8,128)(2,1)} %get-tuple-element.133.wide_ref.wide_hbm, bf16[2,1248,768]{2,1,0:T(8,128)(2,1)} %get-tuple-element.132.refs_0_.heads_ref, bf16[4,5,48,384]{3,2,1,0:T(8,128)(2,1)} %pad_maximum_fusion.refs_1_.refs_0_, ...), custom_call_target="tpu_custom_call" | custom-call | flops 60000002048 | bytes 1000 | tf_op jit(solution)/shard_map/widen_values/pallas_call | solution.py:1039
  109.9 10.1 %attend.1.refs_10_.attended_ref = bf16[6,208,768]{2,1,0:T(8,128)(2,1)} custom-call(s32[6]{0:T(128)} %reshape.380.counts_ref, bf16[2,1248,768]{2,1,0:T(8,128)(2,1)} %get-tuple-element.132.refs_0_.heads_ref, bf16[1,1248,768]{2,1,0:T(8,128)(2,1)} %widen_values.1.values_ref, bf16[2,1,240,384]{3,2,1,0:T(8,128)(2,1)} %pad_maximum_fusion.9.refs_0_, ...), custom_call_target="tpu_custom_call" | custom-call | flops 60000002048 | bytes 1000 | tf_op jit(solution)/shard_map/attend/pallas_call | solution.py:1054
  122.5 3.6 collective-permute-done.26.refs_3_
  131.8 17.8 %widen_hidden.1 = (bf16[4,1248,768]{2,1,0:T(8,128)(2,1)}, bf16[4,1248,768]{2,1,0:T(8,128)(2,1)}, bf16[5,768,768]{2,1,0:T(8,128)(2,1)}) custom-call(s32[2]{0:T(128)} %pad_add_fusion.place_ref, bf16[1248,768]{1,0:T(8,128)(2,1)} %bitcast.298, f32[4,1,768]{2,1,0:T(1,128)} %slice.268.bias_ref, bf16[4,5,48,384]{3,2,1,0:T(8,128)(2,1)} %pad_maximum_fusion.refs_1_.refs_0_, ...), custom_call_target="tpu_custom_call" | custom-call | flops 60000002048 | bytes 1000 | tf_op jit(solution)/shard_map/widen_hidden/pallas_call | solution.py:1065
  155.2 16.8 %join.1 = (f32[6,208,768]{2,1,0:T(8,128)}, f32[6,1,768]{2,1,0:T(1,128)}, bf16[1,3840,768]{2,1,0:T(8,128)(2,1)}) custom-call(s32[6]{0:T(128)} %reshape.380.counts_ref, s32[2]{0:T(128)} %pad_add_fusion.place_ref, bf16[6,208,768]{2,1,0:T(8,128)(2,1)} %attend.1.refs_10_.attended_ref, bf16[4,1248,768]{2,1,0:T(8,128)(2,1)} %get-tuple-element.143.hidden_ref, ...), custom_call_target="tpu_custom_call" | custom-call | flops 60000002048 | bytes 1000 | tf_op jit(solution)/shard_map/join/pallas_call | solution.py:1089
  176.9 3.1 collective-permute-done.40
  180.7 3.1 collective-permute-done.41
  189.1 3.6 collective-permute-done.44
  197.4 20.9 %branch.1 = (f32[6,208,768]{2,1,0:T(8,128)}, bf16[6,208,768]{2,1,0:T(8,128)(2,1)}, bf16[6,208,768]{2,1,0:T(8,128)(2,1)}, bf16[4,1248,768]{2,1,0:T(8,128)(2,1)}, f32[8,768]{1,0:T(8,128)}) custom-call(s32[6]{0:T(128)} %reshape.380.counts_ref, f32[6,208,768]{2,1,0:T(8,128)} %get-tuple-element.151.stream_ref, f32[6,1,768]{2,1,0:T(1,128)} %reshape.395.grad_pooled_ref, ...), custom_call_target="tpu_custom_call" | custom-call | flops 60000002048 | bytes 1000 | tf_op jit(solution)/shard_map/branch/pallas_call | solution.py:1168
  218.3 14.4 %narrow_grad.1 = (bf16[2,8,240,384]{3,2,1,0:T(8,128)(2,1)}, bf16[2,8,240,384]{3,2,1,0:T(8,128)(2,1)}) custom-call(s32[1]{0:T(128)} %bitcast.42.core_ref, bf16[1248,768]{1,0:T(8,128)(2,1)} %bitcast.301, bf16[4,1248,768]{2,1,0:T(8,128)(2,1)} %get-tuple-element.143.hidden_ref, bf16[1248,768]{1,0:T(8,128)(2,1)} %bitcast.302), custom_call_target="tpu_custom_call" | custom-call | flops 60000002048 | bytes 1000 | tf_op jit(solution)/shard_map/narrow_grad/pallas_call | solution.py:1205
  232.8 11.4 %hidden_grad.1 = (bf16[8,240,768]{2,1,0:T(8,128)(2,1)}, bf16[8,240,768]{2,1,0:T(8,128)(2,1)}) custom-call(s32[1]{0:T(128)} %bitcast.42.core_ref, bf16[1248,768]{1,0:T(8,128)(2,1)} %bitcast.299, bf16[4,1248,768]{2,1,0:T(8,128)(2,1)} %get-tuple-element.159.grad_act_ref.grad_ref, bf16[16,768]{1,0:T(8,128)(2,1)} %pad.43.pooled_ref, bf16[16,768]{1,0:T(8,128)(2,1)} %pad.44.embeds_ref), custom_call_target="tpu_custom_call" | custom-call | flops 60000002048 | bytes 1000 | tf_op jit(solution)/shard_map/hidden_grad/pallas_call | solution.py:1230
  249.4 12.4 %hidden_back.1.refs_0_.grad_hidden_ref = f32[1248,768]{1,0:T(8,128)} custom-call(bf16[4,1248,768]{2,1,0:T(8,128)(2,1)} %get-tuple-element.159.grad_act_ref.grad_ref, bf16[5,768,768]{2,1,0:T(8,128)(2,1)} %get-tuple-element.150.wide_ref, bf16[4,2,240,384]{3,2,1,0:T(8,128)(2,1)} %fusion.refs_0_), custom_call_target="tpu_custom_call" | custom-call | flops 60000002048 | bytes 1000 | tf_op jit(solution)/shard_map/hidden_back/pallas_call | solution.py:1267
  265.3 9.7 %attend_back.3 = (bf16[3,416,768]{2,1,0:T(8,128)(2,1)}, f32[8,768]{1,0:T(8,128)}) custom-call(s32[6]{0:T(128)} %reshape.380.counts_ref, bf16[2,1248,768]{2,1,0:T(8,128)(2,1)} %get-tuple-element.132.refs_0_.heads_ref, bf16[1,1248,768]{2,1,0:T(8,128)(2,1)} %widen_values.1.values_ref, f32[2,1248,768]{2,1,0:T(8,128)} %get-tuple-element.157.rstd_ref, ...), custom_call_target="tpu_custom_call" | custom-call | flops 60000002048 | bytes 1000 | tf_op jit(solution)/shard_map/attend_back/pallas_call | solution.py:1286
  274.9 9.7 %attend_back.4 = (bf16[3,416,768]{2,1,0:T(8,128)(2,1)}, f32[8,768]{1,0:T(8,128)}) custom-call(s32[6]{0:T(128)} %reshape.380.counts_ref, bf16[2,1248,768]{2,1,0:T(8,128)(2,1)} %get-tuple-element.132.refs_0_.heads_ref, bf16[1,1248,768]{2,1,0:T(8,128)(2,1)} %widen_values.1.values_ref, f32[2,1248,768]{2,1,0:T(8,128)} %get-tuple-element.157.rstd_ref, ...), custom_call_target="tpu_custom_call" | custom-call | flops 60000002048 | bytes 1000 | tf_op jit(solution)/shard_map/attend_back/pallas_call | solution.py:1286
  284.6 9.9 %attend_back.5 = (bf16[3,416,768]{2,1,0:T(8,128)(2,1)}, f32[8,768]{1,0:T(8,128)}) custom-call(s32[6]{0:T(128)} %reshape.380.counts_ref, bf16[2,1248,768]{2,1,0:T(8,128)(2,1)} %get-tuple-element.132.refs_0_.heads_ref, bf16[1,1248,768]{2,1,0:T(8,128)(2,1)} %widen_values.1.values_ref, f32[2,1248,768]{2,1,0:T(8,128)} %get-tuple-element.157.rstd_ref, ...), custom_call_target="tpu_custom_call" | custom-call | flops 60000002048 | bytes 1000 | tf_op jit(solution)/shard_map/attend_back/pallas_call | solution.py:1286
  298.6 9.8 %qkv_grad.1 = (bf16[2,8,144,384]{3,2,1,0:T(8,128)(2,1)}, bf16[2,8,144,384]{3,2,1,0:T(8,128)(2,1)}) custom-call(s32[1]{0:T(128)} %bitcast.42.core_ref, bf16[1248,768]{1,0:T(8,128)(2,1)} %bitcast.300, bf16[3,416,768]{2,1,0:T(8,128)(2,1)} %get-tuple-element.162.refs_0_.grad_qkv_ref, bf16[3,416,768]{2,1,0:T(8,128)(2,1)} %get-tuple-element.163.refs_0_.refs_1_.grad_qkv_ref, ...), custom_call_target="tpu_custom_call" | custom-call | flops 60000002048 | bytes 1000 | tf_op jit(solution)/shard_map/qkv_grad/pallas_call | solution.py:1306
  310.0 9.6 %merge_back.3 = (bf16[2,208,768]{2,1,0:T(8,128)(2,1)}, f32[208,768]{1,0:T(8,128)}, f32[8,768]{1,0:T(8,128)}) custom-call(s32[6]{0:T(128)} %reshape.380.counts_ref, bf16[3,416,768]{2,1,0:T(8,128)(2,1)} %get-tuple-element.162.refs_0_.grad_qkv_ref, f32[1248,768]{1,0:T(8,128)} %hidden_back.1.refs_0_.grad_hidden_ref, ...), custom_call_target="tpu_custom_call" | custom-call | flops 60000002048 | bytes 1000 | tf_op jit(solution)/shard_map/merge_back/pallas_call | solution.py:1328
  319.6 2.9 fusion.18
  329.3 9.5 %merge_back.4 = (bf16[2,208,768]{2,1,0:T(8,128)(2,1)}, f32[208,768]{1,0:T(8,128)}, f32[8,768]{1,0:T(8,128)}) custom-call(s32[6]{0:T(128)} %reshape.380.counts_ref, bf16[3,416,768]{2,1,0:T(8,128)(2,1)} %get-tuple-element.163.refs_0_.refs_1_.grad_qkv_ref, f32[1248,768]{1,0:T(8,128)} %hidden_back.1.refs_0_.grad_hidden_ref, ...), custom_call_target="tpu_custom_call" | custom-call | flops 60000002048 | bytes 1000 | tf_op jit(solution)/shard_map/merge_back/pallas_call | solution.py:1328
  342.7 9.7 %merge_back.5 = (bf16[2,208,768]{2,1,0:T(8,128)(2,1)}, f32[208,768]{1,0:T(8,128)}, f32[8,768]{1,0:T(8,128)}) custom-call(s32[6]{0:T(128)} %reshape.380.counts_ref, bf16[3,416,768]{2,1,0:T(8,128)(2,1)} %get-tuple-element.164.refs_2_.refs_3_.grad_qkv_ref, f32[1248,768]{1,0:T(8,128)} %hidden_back.1.refs_0_.grad_hidden_ref, ...), custom_call_target="tpu_custom_call" | custom-call | flops 60000002048 | bytes 1000 | tf_op jit(solution)/shard_map/merge_back/pallas_call | solution.py:1328
  361.1 9.7 %collective-permute-done.52 = bf16[240,384]{1,0:T(8,128)(2,1)} collective-permute-done((bf16[240,384]{1,0:T(8,128)(2,1)}, bf16[240,384]{1,0:T(8,128)(2,1)}, u32[]{:S(2)}, u32[]{:S(2)}) %collective-permute-start.52) | collective-permute-done | bytes 184352 | tf_op jit(solution)/shard_map/ppermute | solution.py:507
  375.0 5.9 %embed_grad.1 = (bf16[8,48,1024]{2,1,0:T(8,128)(2,1)}, bf16[8,48,1024]{2,1,0:T(8,128)(2,1)}) custom-call(s32[1]{0:T(128)} %bitcast.42.core_ref, bf16[1248,768]{1,0:T(8,128)(2,1)} %bitcast.251, bf16[416,768]{1,0:T(8,128)(2,1)} %bitcast.304, bf16[416,768]{1,0:T(8,128)(2,1)} %bitcast.305, bf16[416,768]{1,0:T(8,128)(2,1)} %bitcast.306, ...), custom_call_target="tpu_custom_call" | custom-call | flops 60000002048 | bytes 1000 | tf_op jit(solution)/shard_map/embed_grad/pallas_call | solution.py:1375
  386.3 7.7 %collective-permute-done.56 = bf16[4,144,384]{2,1,0:T(8,128)(2,1)S(1)} collective-permute-done((bf16[4,144,384]{2,1,0:T(8,128)(2,1)S(1)}, bf16[4,144,384]{2,1,0:T(8,128)(2,1)S(1)}, u32[]{:S(2)}, u32[]{:S(2)}) %collective-permute-start.56) | collective-permute-done | bytes 442400 | tf_op jit(solution)/shard_map/ppermute | solution.py:507
  395.2 4.2 collective-permute-start.62
  412.8 5.5 %collective-permute-done.68 = bf16[48,1024]{1,0:T(8,128)(2,1)S(1)} collective-permute-done((bf16[48,1024]{1,0:T(8,128)(2,1)S(1)}, bf16[48,1024]{1,0:T(8,128)(2,1)S(1)}, u32[]{:S(2)}, u32[]{:S(2)}) %collective-permute-start.68) | collective-permute-done | bytes 98336 | tf_op jit(solution)/shard_map/ppermute | solution.py:507
  439.8 7.0 %update.1 = (f32[48,768]{1,0:T(8,128)}, f32[48,196]{1,0:T(8,128)}, f32[48,5376]{1,0:T(8,128)}, f32[240,768]{1,0:T(8,128)}, f32[48,768]{1,0:T(8,128)}, /*index=5*...) custom-call(f32[8,128]{1,0:T(8,128)} %copy-done.31, ...), custom_call_target="tpu_custom_call" | custom-call | tf_op jit(solution)/shard_map/update/pallas_call | solution.py:1435
  (374 shorter events, 170.0 us)
Async XLA Ops:
  42.0 19.2 %collective-permute-start.12 = (bf16[4,3,48,384]{3,2,1,0:T(8,128)(2,1)S(1)}, bf16[4,3,48,384]{3,2,1,0:T(8,128)(2,1)}, u32[]{:S(2)}, u32[]{:S(2)}) collective-permute-start(bf16[4,3,48,384]{3,2,1,0:T(8,128)(2,1)S(1)} %pad_maximum_fusion.5.refs_1_.refs_2_), channel_id=1, source_target_pairs={{0,16},{16,0},{1,17},{17,1},{2,18},{18,2},{3,19},{19,3},{4,20},{20... | collective-permute-start | bytes 1327112 | tf_op jit(solution)/shard_map/ppermute | solution.py:523
  44.4 16.8 %collective-permute-start.11 = (bf16[4,3,48,384]{3,2,1,0:T(8,128)(2,1)S(1)}, bf16[4,3,48,384]{3,2,1,0:T(8,128)(2,1)}, u32[]{:S(2)}, u32[]{:S(2)}) collective-permute-start(bf16[4,3,48,384]{3,2,1,0:T(8,128)(2,1)S(1)} %pad_maximum_fusion.4.refs_0_), channel_id=1, source_target_pairs={{0,2},{1,3},{2,0},{3,1},{4,6},{5,7},{6,4},{7,5},{8,10},{9,11},{10,... | collective-permute-start | bytes 1327112 | tf_op jit(solution)/shard_map/ppermute | solution.py:576
  50.9 24.6 %collective-permute-start.19 = (bf16[5,48,384]{2,1,0:T(8,128)(2,1)S(1)}, bf16[5,48,384]{2,1,0:T(8,128)(2,1)S(1)}, u32[]{:S(2)}, u32[]{:S(2)}) collective-permute-start(bf16[5,48,384]{2,1,0:T(8,128)(2,1)S(1)} %constant_dynamic-slice_fusion.2.refs_2_), channel_id=1, source_target_pairs={{0,12},{1,13},{2,14},{3,15},{4,8},{5,9},{6,10},{7,11},{8,4},{9,5},... | collective-permute-start | bytes 552968 | tf_op jit(solution)/shard_map/ppermute | solution.py:582
  61.3 18.2 %collective-permute-start.13 = (bf16[4,3,48,384]{3,2,1,0:T(8,128)(2,1)S(1)}, bf16[4,3,48,384]{3,2,1,0:T(8,128)(2,1)}, u32[]{:S(2)}, u32[]{:S(2)}) collective-permute-start(bf16[4,3,48,384]{3,2,1,0:T(8,128)(2,1)S(1)} %pad_maximum_fusion.4.refs_0_), channel_id=1, source_target_pairs={{0,1},{1,0},{2,3},{3,2},{4,5},{5,4},{6,7},{7,6},{8,9},{9,8},{10,11... | collective-permute-start | bytes 1327112 | tf_op jit(solution)/shard_map/ppermute | solution.py:572
  61.8 19.2 %collective-permute-start.14 = (bf16[4,3,48,384]{3,2,1,0:T(8,128)(2,1)}, bf16[4,3,48,384]{3,2,1,0:T(8,128)(2,1)}, u32[]{:S(2)}, u32[]{:S(2)}) collective-permute-start(bf16[4,3,48,384]{3,2,1,0:T(8,128)(2,1)} %collective-permute-done.11.refs_1_), channel_id=1, source_target_pairs={{0,1},{1,0},{2,3},{3,2},{4,5},{5,4},{6,7},{7,6},{8,9},{9,8},{10,11... | collective-permute-start | bytes 1327112 | tf_op jit(solution)/shard_map/ppermute | solution.py:572
  64.1 17.4 %collective-permute-start.15 = (bf16[4,3,48,384]{3,2,1,0:T(8,128)(2,1)S(1)}, bf16[4,3,48,384]{3,2,1,0:T(8,128)(2,1)}, u32[]{:S(2)}, u32[]{:S(2)}) collective-permute-start(bf16[4,3,48,384]{3,2,1,0:T(8,128)(2,1)S(1)} %pad_maximum_fusion.5.refs_1_.refs_2_), channel_id=1, source_target_pairs={{0,1},{1,0},{2,3},{3,2},{4,5},{5,4},{6,7},{7,6},{8,9},{9,8},{10,11... | collective-permute-start | bytes 1327112 | tf_op jit(solution)/shard_map/ppermute | solution.py:572
  76.5 21.7 %collective-permute-start.22 = (bf16[1,240,384]{2,1,0:T(8,128)(2,1)S(1)}, bf16[1,240,384]{2,1,0:T(8,128)(2,1)S(1)}, u32[]{:S(2)}, u32[]{:S(2)}) collective-permute-start(bf16[1,240,384]{2,1,0:T(8,128)(2,1)S(1)} %constant_dynamic-slice_fusion.1.refs_10_), channel_id=1, source_target_pairs={{0,4},{1,5},{2,6},{3,7},{4,0},{5,1},{6,2},{7,3},{8,12},{9,13},{10,... | collective-permute-start | bytes 552968 | tf_op jit(solution)/shard_map/ppermute | solution.py:582
  76.6 21.6 %collective-permute-start.23 = (bf16[1,240,384]{2,1,0:T(8,128)(2,1)S(1)}, bf16[1,240,384]{2,1,0:T(8,128)(2,1)S(1)}, u32[]{:S(2)}, u32[]{:S(2)}) collective-permute-start(bf16[1,240,384]{2,1,0:T(8,128)(2,1)S(1)} %constant_dynamic-slice_fusion.1.refs_10_), channel_id=1, source_target_pairs={{0,8},{1,9},{2,10},{3,11},{4,12},{5,13},{6,14},{7,15},{8,0},{9,1},... | collective-permute-start | bytes 552968 | tf_op jit(solution)/shard_map/ppermute | solution.py:582
  79.4 18.8 %collective-permute-start.24 = (bf16[1,240,384]{2,1,0:T(8,128)(2,1)S(1)}, bf16[1,240,384]{2,1,0:T(8,128)(2,1)S(1)}, u32[]{:S(2)}, u32[]{:S(2)}) collective-permute-start(bf16[1,240,384]{2,1,0:T(8,128)(2,1)S(1)} %constant_dynamic-slice_fusion.1.refs_10_), channel_id=1, source_target_pairs={{0,12},{1,13},{2,14},{3,15},{4,8},{5,9},{6,10},{7,11},{8,4},{9,5},... | collective-permute-start | bytes 552968 | tf_op jit(solution)/shard_map/ppermute | solution.py:582
  80.9 20.2 %collective-permute-start.21 = (bf16[2,5,48,384]{3,2,1,0:T(8,128)(2,1)S(1)}, bf16[2,5,48,384]{3,2,1,0:T(8,128)(2,1)S(1)}, u32[]{:S(2)}, u32[]{:S(2)}) collective-permute-start(bf16[2,5,48,384]{3,2,1,0:T(8,128)(2,1)S(1)} %pad_maximum_fusion.8.refs_9_), channel_id=1, source_target_pairs={{0,2},{1,3},{2,0},{3,1},{4,6},{5,7},{6,4},{7,5},{8,10},{9,11},{10,... | collective-permute-start | bytes 1105928 | tf_op jit(solution)/shard_map/ppermute | solution.py:576
  81.5 19.7 %collective-permute-start.20 = (bf16[2,5,48,384]{3,2,1,0:T(8,128)(2,1)S(1)}, bf16[2,5,48,384]{3,2,1,0:T(8,128)(2,1)S(1)}, u32[]{:S(2)}, u32[]{:S(2)}) collective-permute-start(bf16[2,5,48,384]{3,2,1,0:T(8,128)(2,1)S(1)} %pad_maximum_fusion.7.refs_8_), channel_id=1, source_target_pairs={{0,16},{16,0},{1,17},{17,1},{2,18},{18,2},{3,19},{19,3},{4,20},{20... | collective-permute-start | bytes 1105928 | tf_op jit(solution)/shard_map/ppermute | solution.py:523
  98.3 21.7 %collective-permute-start.28 = (bf16[2,1,240,384]{3,2,1,0:T(8,128)(2,1)S(1)}, bf16[2,1,240,384]{3,2,1,0:T(8,128)(2,1)}, u32[]{:S(2)}, u32[]{:S(2)}) collective-permute-start(bf16[2,1,240,384]{3,2,1,0:T(8,128)(2,1)S(1)} %pad_maximum_fusion.10.refs_1_), channel_id=1, source_target_pairs={{0,2},{1,3},{2,0},{3,1},{4,6},{5,7},{6,4},{7,5},{8,10},{9,11},{10,... | collective-permute-start | bytes 1105928 | tf_op jit(solution)/shard_map/ppermute | solution.py:576
  100.7 20.5 %collective-permute-start.27 = (bf16[2,1,240,384]{3,2,1,0:T(8,128)(2,1)}, bf16[2,1,240,384]{3,2,1,0:T(8,128)(2,1)}, u32[]{:S(2)}, u32[]{:S(2)}) collective-permute-start(bf16[2,1,240,384]{3,2,1,0:T(8,128)(2,1)} %pad_maximum_fusion.9.refs_0_), channel_id=1, source_target_pairs={{0,16},{16,0},{1,17},{17,1},{2,18},{18,2},{3,19},{19,3},{4,20},{20... | collective-permute-start | bytes 1105928 | tf_op jit(solution)/shard_map/ppermute | solution.py:523
  103.1 23.0 %collective-permute-start.26 = (bf16[4,5,48,384]{3,2,1,0:T(8,128)(2,1)}, bf16[4,5,48,384]{3,2,1,0:T(8,128)(2,1)}, u32[]{:S(2)}, u32[]{:S(2)}) collective-permute-start(bf16[4,5,48,384]{3,2,1,0:T(8,128)(2,1)} %pad_maximum_fusion.1.refs_2_), channel_id=1, source_target_pairs={{0,16},{16,0},{1,17},{17,1},{2,18},{18,2},{3,19},{19,3},{4,20},{20... | collective-permute-start | bytes 2211848 | tf_op jit(solution)/shard_map/ppermute | solution.py:523
  104.6 21.5 %collective-permute-start.25 = (bf16[4,5,48,384]{3,2,1,0:T(8,128)(2,1)}, bf16[4,5,48,384]{3,2,1,0:T(8,128)(2,1)}, u32[]{:S(2)}, u32[]{:S(2)}) collective-permute-start(bf16[4,5,48,384]{3,2,1,0:T(8,128)(2,1)} %pad_maximum_fusion.refs_1_.refs_0_), channel_id=1, source_target_pairs={{0,2},{1,3},{2,0},{3,1},{4,6},{5,7},{6,4},{7,5},{8,10},{9,11},{10,... | collective-permute-start | bytes 2211848 | tf_op jit(solution)/shard_map/ppermute | solution.py:576
  127.8 21.7 %collective-permute-start.34 = (bf16[4,1,240,384]{3,2,1,0:T(8,128)(2,1)S(1)}, bf16[4,1,240,384]{3,2,1,0:T(8,128)(2,1)S(1)}, u32[]{:S(2)}, u32[]{:S(2)}) collective-permute-start(bf16[4,1,240,384]{3,2,1,0:T(8,128)(2,1)S(1)} %pad_maximum_fusion.3.refs_9_.refs_2_), channel_id=1, source_target_pairs={{0,16},{16,0},{1,17},{17,1},{2,18},{18,2},{3,19},{19,3},{4,20},{20... | collective-permute-start | bytes 2211848 | tf_op jit(solution)/shard_map/ppermute | solution.py:523
  128.7 21.0 %collective-permute-start.33 = (bf16[4,1,240,384]{3,2,1,0:T(8,128)(2,1)S(1)}, bf16[4,1,240,384]{3,2,1,0:T(8,128)(2,1)S(1)}, u32[]{:S(2)}, u32[]{:S(2)}) collective-permute-start(bf16[4,1,240,384]{3,2,1,0:T(8,128)(2,1)S(1)} %pad_maximum_fusion.2.refs_8_.refs_0_), channel_id=1, source_target_pairs={{0,2},{1,3},{2,0},{3,1},{4,6},{5,7},{6,4},{7,5},{8,10},{9,11},{10,... | collective-permute-start | bytes 2211848 | tf_op jit(solution)/shard_map/ppermute | solution.py:576
  244.2 17.7 %collective-permute-start.47 = (bf16[8,240,768]{2,1,0:T(8,128)(2,1)}, bf16[8,240,768]{2,1,0:T(8,128)(2,1)}, u32[]{:S(2)}, u32[]{:S(2)}) collective-permute-start(bf16[8,240,768]{2,1,0:T(8,128)(2,1)} %get-tuple-element.161), channel_id=1, source_target_pairs={{0,1},{1,0},{2,3},{3,2},{4,5},{5,4},{6,7},{7,6},{8,9},{9,8},{10,11... | collective-permute-start | bytes 8847368 | tf_op jit(solution)/shard_map/ppermute | solution.py:572
  248.8 47.0 %collective-permute-start.46 = (bf16[4,2,240,384]{3,2,1,0:T(8,128)(2,1)}, bf16[4,2,240,384]{3,2,1,0:T(8,128)(2,1)}, u32[]{:S(2)}, u32[]{:S(2)}) collective-permute-start(bf16[4,2,240,384]{3,2,1,0:T(8,128)(2,1)} %fusion.refs_0_), channel_id=1, source_target_pairs={{0,16},{16,0},{1,17},{17,1},{2,18},{18,2},{3,19},{19,3},{4,20},{20... | collective-permute-start | bytes 4423688 | tf_op jit(solution)/shard_map/ppermute | solution.py:507
  264.8 54.8 %collective-permute-start.49 = (bf16[4,240,768]{2,1,0:T(8,128)(2,1)}, bf16[4,240,768]{2,1,0:T(8,128)(2,1)}, u32[]{:S(2)}, u32[]{:S(2)}) collective-permute-start(bf16[4,240,768]{2,1,0:T(8,128)(2,1)} %fusion.1.refs_1_), channel_id=1, source_target_pairs={{0,2},{1,3},{2,0},{3,1},{4,6},{5,7},{6,4},{7,5},{8,10},{9,11},{10,... | collective-permute-start | bytes 4423688 | tf_op jit(solution)/shard_map/ppermute | solution.py:507
  308.4 31.6 %collective-permute-start.48 = (bf16[4,240,384]{2,1,0:T(8,128)(2,1)}, bf16[4,240,384]{2,1,0:T(8,128)(2,1)}, u32[]{:S(2)}, u32[]{:S(2)}) collective-permute-start(bf16[4,240,384]{2,1,0:T(8,128)(2,1)} %fusion.2.refs_4_), channel_id=1, source_target_pairs={{0,2},{1,3},{2,0},{3,1},{4,6},{5,7},{6,4},{7,5},{8,10},{9,11},{10,... | collective-permute-start | bytes 2211848 | tf_op jit(solution)/shard_map/ppermute | solution.py:507
  310.0 17.0 %collective-permute-start.50 = (bf16[2,8,144,384]{3,2,1,0:T(8,128)(2,1)}, bf16[2,8,144,384]{3,2,1,0:T(8,128)(2,1)}, u32[]{:S(2)}, u32[]{:S(2)}) collective-permute-start(bf16[2,8,144,384]{3,2,1,0:T(8,128)(2,1)} %get-tuple-element.167.refs_0_), channel_id=1, source_target_pairs={{0,1},{1,0},{2,3},{3,2},{4,5},{5,4},{6,7},{7,6},{8,9},{9,8},{10,11... | collective-permute-start | bytes 5308424 | tf_op jit(solution)/shard_map/ppermute | solution.py:572
  322.6 29.8 %collective-permute-start.57 = (bf16[240,768]{1,0:T(8,128)(2,1)}, bf16[240,768]{1,0:T(8,128)(2,1)}, u32[]{:S(2)}, u32[]{:S(2)}) collective-permute-start(bf16[240,768]{1,0:T(8,128)(2,1)} %get-tuple-element.243.refs_1_), channel_id=1, source_target_pairs={{0,4},{1,5},{2,6},{3,7},{4,0},{5,1},{6,2},{7,3},{8,12},{9,13},{10,... | collective-permute-start | bytes 1105928 | tf_op jit(solution)/shard_map/ppermute | solution.py:507
  322.6 32.1 %collective-permute-start.58 = (bf16[240,768]{1,0:T(8,128)(2,1)}, bf16[240,768]{1,0:T(8,128)(2,1)}, u32[]{:S(2)}, u32[]{:S(2)}) collective-permute-start(bf16[240,768]{1,0:T(8,128)(2,1)} %get-tuple-element.242.refs_2_), channel_id=1, source_target_pairs={{0,8},{1,9},{2,10},{3,11},{4,12},{5,13},{6,14},{7,15},{8,0},{9,1},... | collective-permute-start | bytes 1105928 | tf_op jit(solution)/shard_map/ppermute | solution.py:507
  324.6 32.3 %collective-permute-start.59 = (bf16[240,768]{1,0:T(8,128)(2,1)}, bf16[240,768]{1,0:T(8,128)(2,1)}, u32[]{:S(2)}, u32[]{:S(2)}) collective-permute-start(bf16[240,768]{1,0:T(8,128)(2,1)} %get-tuple-element.241.refs_3_), channel_id=1, source_target_pairs={{0,12},{1,13},{2,14},{3,15},{4,8},{5,9},{6,10},{7,11},{8,4},{9,5},... | collective-permute-start | bytes 1105928 | tf_op jit(solution)/shard_map/ppermute | solution.py:507
  338.7 34.3 %collective-permute-start.55 = (bf16[4,2,144,384]{3,2,1,0:T(8,128)(2,1)}, bf16[4,2,144,384]{3,2,1,0:T(8,128)(2,1)S(1)}, u32[]{:S(2)}, u32[]{:S(2)}) collective-permute-start(bf16[4,2,144,384]{3,2,1,0:T(8,128)(2,1)} %fusion.12.refs_4_), channel_id=1, source_target_pairs={{0,16},{16,0},{1,17},{17,1},{2,18},{18,2},{3,19},{19,3},{4,20},{20... | collective-permute-start | bytes 2654216 | tf_op jit(solution)/shard_map/ppermute | solution.py:507
  342.6 18.5 %collective-permute-start.51 = (bf16[240,384]{1,0:T(8,128)(2,1)}, bf16[240,384]{1,0:T(8,128)(2,1)}, u32[]{:S(2)}, u32[]{:S(2)}) collective-permute-start(bf16[240,384]{1,0:T(8,128)(2,1)} %get-tuple-element.240.refs_1_), channel_id=1, source_target_pairs={{0,4},{1,5},{2,6},{3,7},{4,0},{5,1},{6,2},{7,3},{8,12},{9,13},{10,... | collective-permute-start | bytes 552968 | tf_op jit(solution)/shard_map/ppermute | solution.py:507
  352.4 18.4 %collective-permute-start.52 = (bf16[240,384]{1,0:T(8,128)(2,1)}, bf16[240,384]{1,0:T(8,128)(2,1)}, u32[]{:S(2)}, u32[]{:S(2)}) collective-permute-start(bf16[240,384]{1,0:T(8,128)(2,1)} %get-tuple-element.239.refs_2_), channel_id=1, source_target_pairs={{0,8},{1,9},{2,10},{3,11},{4,12},{5,13},{6,14},{7,15},{8,0},{9,1},... | collective-permute-start | bytes 552968 | tf_op jit(solution)/shard_map/ppermute | solution.py:507
  354.7 16.2 %collective-permute-start.53 = (bf16[240,384]{1,0:T(8,128)(2,1)}, bf16[240,384]{1,0:T(8,128)(2,1)}, u32[]{:S(2)}, u32[]{:S(2)}) collective-permute-start(bf16[240,384]{1,0:T(8,128)(2,1)} %get-tuple-element.238.refs_3_), channel_id=1, source_target_pairs={{0,12},{1,13},{2,14},{3,15},{4,8},{5,9},{6,10},{7,11},{8,4},{9,5},... | collective-permute-start | bytes 552968 | tf_op jit(solution)/shard_map/ppermute | solution.py:507
  381.5 20.3 %collective-permute-start.61 = (bf16[240,768]{1,0:T(8,128)(2,1)S(1)}, bf16[240,768]{1,0:T(8,128)(2,1)S(1)}, u32[]{:S(2)}, u32[]{:S(2)}) collective-permute-start(bf16[240,768]{1,0:T(8,128)(2,1)S(1)} %copy-done.9), channel_id=1, source_target_pairs={{0,16},{16,0},{1,17},{17,1},{2,18},{18,2},{3,19},{19,3},{4,20},{20... | collective-permute-start | bytes 1105928 | tf_op jit(solution)/shard_map/ppermute | solution.py:523
  382.7 16.8 %collective-permute-start.54 = (bf16[240,384]{1,0:T(8,128)(2,1)S(1)}, bf16[240,384]{1,0:T(8,128)(2,1)S(1)}, u32[]{:S(2)}, u32[]{:S(2)}) collective-permute-start(bf16[240,384]{1,0:T(8,128)(2,1)S(1)} %copy-done.13), channel_id=1, source_target_pairs={{0,16},{16,0},{1,17},{17,1},{2,18},{18,2},{3,19},{19,3},{4,20},{20... | collective-permute-start | bytes 552968 | tf_op jit(solution)/shard_map/ppermute | solution.py:523
  384.7 18.8 %collective-permute-start.66 = (bf16[4,48,1024]{2,1,0:T(8,128)(2,1)S(1)}, bf16[4,48,1024]{2,1,0:T(8,128)(2,1)S(1)}, u32[]{:S(2)}, u32[]{:S(2)}) collective-permute-start(bf16[4,48,1024]{2,1,0:T(8,128)(2,1)S(1)} %fusion.21), channel_id=1, source_target_pairs={{0,2},{1,3},{2,0},{3,1},{4,6},{5,7},{6,4},{7,5},{8,10},{9,11},{10,... | collective-permute-start | bytes 1179656 | tf_op jit(solution)/shard_map/ppermute | solution.py:507
  (93 other events, 1070.9 us)

commit v6 on v5

--- a/solution.py
+++ b/solution.py
@@ -120,11 +120,14 @@
     return jnp.where(row == column, 1.0 / head_size, 0.0).astype(jnp.bfloat16)
 
 
-def head_mean(values, mixer):
+def head_mean(values, mixer, fine=True):
     parts = []
     for at in range(0, values.shape[1], 256):
-        high, low = split_two(values[:, at : at + 256])
-        parts.append(product(high, mixer) + product(low, mixer))
+        if fine:
+            high, low = split_two(values[:, at : at + 256])
+            parts.append(product(high, mixer) + product(low, mixer))
+        else:
+            parts.append(product(values[:, at : at + 256].astype(jnp.bfloat16), mixer))
     return jnp.concatenate(parts, axis=1)
 
 
@@ -175,7 +178,7 @@
         rows = slice(index * chunk, (index + 1) * chunk)
         values = product(normed_ref[rows, :], held_ref[step])
         center = values - head_mean(values, mixer)
-        rstd = lax.rsqrt(head_mean(center * center, mixer) + norm_eps)
+        rstd = lax.rsqrt(head_mean(center * center, mixer, False) + norm_eps)
         rstd_ref[0, rows, :] = rstd
         heads_ref[0, rows, :] = (center * rstd * gain).astype(jnp.bfloat16)
 
@@ -375,7 +378,11 @@
         unit = heads_ref[part].astype(jnp.float32) / gain
         sums_ref[part : part + 1, :] += jnp.sum(above * unit, axis=0, keepdims=True)
         slanted = above * gain
-        back = slanted - head_mean(slanted, mixer) - unit * head_mean(slanted * unit, mixer)
+        back = (
+            slanted
+            - head_mean(slanted, mixer, False)
+            - unit * head_mean(slanted * unit, mixer, False)
+        )
         grad_qkv_ref[part] = (rstd_ref[part] * back).astype(jnp.bfloat16)
 
 
@@ -988,7 +995,7 @@
     out_bias = bias_float[hidden_width : hidden_width + model_width].reshape(1, model_width)
     place_bias = table[:slots] + bias_float[hidden_width + model_width :]
     guards = qkv_get.go()
-    hidden_get = Flow(gather_split(first_behind(hidden_piece, guards)))
+    hidden_get = Flow(gather_split(first_behind(hidden_piece, (guards, table))))
     guards += hidden_get.go()
     merged, normed = image_call(
         embed_kernel,
@@ -1264,22 +1271,6 @@
 
     head_gains = scale_float[2:4].reshape(2, 1, model_width)
     guards = narrow_flow.go()
-    grad_hidden = pl.pallas_call(
-        hidden_back_kernel,
-        grid=(hidden_blocks,),
-        in_specs=[
-            block((1, rows, model_width), lambda k: (k, 0, 0)),
-            block((1, model_width, model_width), lambda k: (k, 0, 0)),
-        ]
-        + [anywhere] * len(guards),
-        out_specs=whole(rows, model_width),
-        out_shape=shape((rows, model_width), f32),
-        scratch_shapes=[pltpu.VMEM((rows, model_width), f32)],
-        compiler_params=roomy,
-        cost_estimate=long,
-        name="hidden_back",
-    )(grad_act, wide_hidden, *guards)
-    guards = [grad_hidden] + hidden_flow.go()
     grad_qkv, head_sums = [], 0.0
     for part in range(parts):
         base = part * per_part
@@ -1302,6 +1293,8 @@
         grad_qkv.append(grads)
         head_sums = head_sums + sums_part
         guards = [grads]
+        if part == 0:
+            guards += hidden_flow.go(grads)
     guards += narrow_flow.go(grads)
     qkv_halves = pl.pallas_call(
         lambda core_ref, normed_ref, *refs: wide_grad_kernel(
@@ -1322,6 +1315,22 @@
     )(core, normed_rows, *grad_qkv, *guards)
     qkv_flow = Flow(reduce_columns(*qkv_halves))
     guards = qkv_flow.go()
+    grad_hidden = pl.pallas_call(
+        hidden_back_kernel,
+        grid=(hidden_blocks,),
+        in_specs=[
+            block((1, rows, model_width), lambda k: (k, 0, 0)),
+            block((1, model_width, model_width), lambda k: (k, 0, 0)),
+        ]
+        + [anywhere] * len(guards),
+        out_specs=whole(rows, model_width),
+        out_shape=shape((rows, model_width), f32),
+        scratch_shapes=[pltpu.VMEM((rows, model_width), f32)],
+        compiler_params=roomy,
+        cost_estimate=long,
+        name="hidden_back",
+    )(grad_act, wide_hidden, *guards)
+    guards = hidden_flow.go(grad_hidden) + qkv_flow.go(grad_hidden)
     grad_patches, grad_places, merge_sums = [], [], 0.0
     for part in range(parts):
         base = part * per_part
@@ -1359,11 +1368,9 @@
         grad_places.append(place_part)
         merge_sums = merge_sums + sums_part
         guards = [grads]
-        if part == 0:
-            guards += hidden_flow.go(grads) + qkv_flow.go(grads)
-        elif part == 1:
-            guards += narrow_flow.go(grads)
-    guards += hidden_flow.go(grads) + qkv_flow.go(grads) + narrow_flow.go(grads)
+        if part == 1:
+            guards += qkv_flow.go(grads)
+    guards += hidden_flow.go(grads) + narrow_flow.go(grads)
     grad_scale = jnp.stack([merge_sums[0], out_sums[hidden_blocks + 1], head_sums[0], head_sums[1]])
     grad_bias = jnp.concatenate([out_sums[: hidden_blocks + 1], merge_sums[1:2]]).reshape(
         owners, bias_rows, wide_rows
@@ -1394,11 +1401,12 @@
     embed_flow = Flow(reduce_rows_last(*embed_halves))
     embed_flow.go()
     sent = embed_flow.go()
+    hidden_flow.go(sent)
+    sent = qkv_flow.go(sent) + narrow_flow.go(sent)
+    sent = embed_flow.go(sent)
+    narrow_flow.go(sent)
     sent = qkv_flow.go(sent)
-    narrow_flow.go(sent)
-    hidden_flow.go(sent)
-    embed_flow.go()
-    sent = embed_flow.go(qkv_flow.go())
+    sent = embed_flow.go(sent)
     qkv_flow.go(sent)
     flows = (narrow_flow, hidden_flow, qkv_flow, embed_flow)
     shards = [flow.finish() for flow in flows]

time: 458 us -> 449 us (0.980)
  waiting for transfers between devices: 71 us -> 64.8 us
    ppermute x18, waiting for transfers between devices: 24.7 us -> 18.1 us  [traded(): lax.ppermute(send, mesh_axis, bit_swap(size, turn * stride))]
where the time goes in v6:
time: 449 us; the launch traced here: 444 us
  Pallas kernels  218 us (49%)
  starting transfers between devices  77.5 us (17%)
  waiting for transfers between devices  64.8 us (14%)
  other arithmetic  49.3 us (11%)
  local copies, waits for them, and re-layouts  24.8 us (6%)
  between operations  5.51 us (1%)
    pallas_call x3, Pallas kernels, per_device(): image_call(functools.partial(merge_back_kernel, base=base), per_part, [im...  28.6 us
    pallas_call x3, Pallas kernels, per_device(): image_call(functools.partial(attend_back_kernel, base=base, head_size=hea...  27.8 us
    ppermute x18, starting transfers between devices, traded(): lax.ppermute(send, mesh_axis, bit_swap(size, turn * stride))  24.6 us
    pallas_call x1, Pallas kernels, per_device(): image_call(branch_kernel, images, [per_image(slots, model_width), per_ima...  21 us
    ppermute x12, starting transfers between devices, high_gather(): lax.ppermute(own, 'fsdp', bit_swap(owners, turn))  20.2 us
    convert_element_type x10, other arithmetic, traded(): added(picked(terms, axis, index ^ turn)).astype(jnp.bfloat16)  19.9 us
    ppermute x18, waiting for transfers between devices, traded(): lax.ppermute(send, mesh_axis, bit_swap(size, turn * stride))  18.1 us
    pallas_call x1, Pallas kernels, per_device(): pl.pallas_call(functools.partial(widen_hidden_kernel, found=found, chunk=...  17.4 us
  transfers between devices with their start and end apart: 76, of which 29 were waited for; matrix products, arithmetic and copies ran while one was open for 12% of the time, Pallas kernels for 34%

profile of v6, /device:TPU:0, one launch (start us, length us, event | category | flops | bytes accessed | tf_op | source)
XLA Modules:
  0.0 443.8 jit_solution(7516927305488487610)
XLA Ops:
  4.3 4.1 collective-permute-start.1
  11.4 4.8 %collective-permute-done.1 = bf16[1,48,1024]{2,1,0:T(8,128)(2,1)S(1)} collective-permute-done((bf16[1,48,1024]{2,1,0:T(8,128)(2,1)S(1)}, bf16[1,48,1024]{2,1,0:T(8,128)(2,1)S(1)}, u32[]{:S(2)}, u32[]{:S(2)}) %collective-permute-start.1) | collective-permute-done | bytes 98336 | tf_op jit(solution)/shard_map/ppermute | solution.py:589
  25.6 6.3 %collective-permute-done.7 = bf16[3,48,384]{2,1,0:T(8,128)(2,1)S(1)} collective-permute-done((bf16[3,48,384]{2,1,0:T(8,128)(2,1)S(1)}, bf16[3,48,384]{2,1,0:T(8,128)(2,1)S(1)}, u32[]{:S(2)}, u32[]{:S(2)}) %collective-permute-start.7) | collective-permute-done | bytes 110624 | tf_op jit(solution)/shard_map/ppermute | solution.py:589
  41.5 4.5 %collective-permute-done.9 = bf16[2,3,48,384]{3,2,1,0:T(8,128)(2,1)S(1)} collective-permute-done((bf16[2,3,48,384]{3,2,1,0:T(8,128)(2,1)S(1)}, bf16[2,3,48,384]{3,2,1,0:T(8,128)(2,1)S(1)}, u32[]{:S(2)}, u32[]{:S(2)}) %collective-permute-start.9) | collective-permute-done | bytes 221216 | tf_op jit(solution)/shard_map/ppermute | solution.py:530
  47.7 3.7 assemble_small.1
  61.8 10.5 %embed.1 = (f32[6,208,768]{2,1,0:T(8,128)}, bf16[6,208,768]{2,1,0:T(8,128)(2,1)}) custom-call(s32[6]{0:T(128)} %reshape.380.counts_ref, bf16[6,208,768]{2,1,0:T(8,128)(2,1)} %pad.37.pixel_ref, s32[6,1,208]{2,1,0:T(1,128)} %pad.38.map_ref, f32[6,1,208]{2,1,0:T(1,128)} %get-tuple-element.286.row_ref, f32[6,208,1]{2,1,0:T(8,128)} %copy.66.column_ref, ...), custom_call_target="tpu_custom_call" | custom-call | flops 60000002048 | bytes 1000 | tf_op jit(solution)/shard_map/embed/pallas_call | solution.py:1000
  82.1 14.7 %widen_heads.1 = (bf16[2,1248,768]{2,1,0:T(8,128)(2,1)}, f32[2,1248,768]{2,1,0:T(8,128)}, bf16[3,768,768]{2,1,0:T(8,128)(2,1)}) custom-call(s32[2]{0:T(128)} %pad_add_fusion.place_ref, bf16[1248,768]{1,0:T(8,128)(2,1)} %bitcast.300, f32[2,1,768]{2,1,0:T(1,128)} %reshape.389.gain_ref, bf16[4,3,48,384]{3,2,1,0:T(8,128)(2,1)} %copy-done.16, ...), custom_call_target="tpu_custom_call" | custom-call | flops 60000002048 | bytes 1000 | tf_op jit(solution)/shard_map/widen_heads/pallas_call | solution.py:1028
  104.4 4.8 %widen_values.1.values_ref = bf16[1,1248,768]{2,1,0:T(8,128)(2,1)} custom-call(bf16[1248,768]{1,0:T(8,128)(2,1)} %bitcast.301, bf16[3,768,768]{2,1,0:T(8,128)(2,1)} %get-tuple-element.138.wide_ref.wide_hbm, bf16[2,1248,768]{2,1,0:T(8,128)(2,1)} %get-tuple-element.137.refs_0_.heads_ref, bf16[4,5,48,384]{3,2,1,0:T(8,128)(2,1)} %pad_maximum_fusion.refs_1_.refs_0_, ...), custom_call_target="tpu_custom_call" | custom-call | flops 60000002048 | bytes 1000 | tf_op jit(solution)/shard_map/widen_values/pallas_call | solution.py:1046
  109.2 10.1 %attend.1.refs_10_.attended_ref = bf16[6,208,768]{2,1,0:T(8,128)(2,1)} custom-call(s32[6]{0:T(128)} %reshape.380.counts_ref, bf16[2,1248,768]{2,1,0:T(8,128)(2,1)} %get-tuple-element.137.refs_0_.heads_ref, bf16[1,1248,768]{2,1,0:T(8,128)(2,1)} %widen_values.1.values_ref, bf16[2,1,240,384]{3,2,1,0:T(8,128)(2,1)} %pad_maximum_fusion.9.refs_0_, ...), custom_call_target="tpu_custom_call" | custom-call | flops 60000002048 | bytes 1000 | tf_op jit(solution)/shard_map/attend/pallas_call | solution.py:1061
  120.6 4.4 collective-permute-done.26.refs_3_
  130.7 17.4 %widen_hidden.1 = (bf16[4,1248,768]{2,1,0:T(8,128)(2,1)}, bf16[4,1248,768]{2,1,0:T(8,128)(2,1)}, bf16[5,768,768]{2,1,0:T(8,128)(2,1)}) custom-call(s32[2]{0:T(128)} %pad_add_fusion.place_ref, bf16[1248,768]{1,0:T(8,128)(2,1)} %bitcast.302, f32[4,1,768]{2,1,0:T(1,128)} %slice.268.bias_ref, bf16[4,5,48,384]{3,2,1,0:T(8,128)(2,1)} %pad_maximum_fusion.refs_1_.refs_0_, ...), custom_call_target="tpu_custom_call" | custom-call | flops 60000002048 | bytes 1000 | tf_op jit(solution)/shard_map/widen_hidden/pallas_call | solution.py:1072
  153.7 16.8 %join.1 = (f32[6,208,768]{2,1,0:T(8,128)}, f32[6,1,768]{2,1,0:T(1,128)}, bf16[1,3840,768]{2,1,0:T(8,128)(2,1)}) custom-call(s32[6]{0:T(128)} %reshape.380.counts_ref, s32[2]{0:T(128)} %pad_add_fusion.place_ref, bf16[6,208,768]{2,1,0:T(8,128)(2,1)} %attend.1.refs_10_.attended_ref, bf16[4,1248,768]{2,1,0:T(8,128)(2,1)} %get-tuple-element.148.hidden_ref, ...), custom_call_target="tpu_custom_call" | custom-call | flops 60000002048 | bytes 1000 | tf_op jit(solution)/shard_map/join/pallas_call | solution.py:1096
  175.4 3.1 collective-permute-done.40
  187.6 3.8 collective-permute-done.44
  196.1 21.0 %branch.1 = (f32[6,208,768]{2,1,0:T(8,128)}, bf16[6,208,768]{2,1,0:T(8,128)(2,1)}, bf16[6,208,768]{2,1,0:T(8,128)(2,1)}, bf16[4,1248,768]{2,1,0:T(8,128)(2,1)}, f32[8,768]{1,0:T(8,128)}) custom-call(s32[6]{0:T(128)} %reshape.380.counts_ref, f32[6,208,768]{2,1,0:T(8,128)} %get-tuple-element.156.stream_ref, f32[6,1,768]{2,1,0:T(1,128)} %reshape.395.grad_pooled_ref, ...), custom_call_target="tpu_custom_call" | custom-call | flops 60000002048 | bytes 1000 | tf_op jit(solution)/shard_map/branch/pallas_call | solution.py:1175
  217.1 14.3 %narrow_grad.1 = (bf16[2,8,240,384]{3,2,1,0:T(8,128)(2,1)}, bf16[2,8,240,384]{3,2,1,0:T(8,128)(2,1)}) custom-call(s32[1]{0:T(128)} %bitcast.42.core_ref, bf16[1248,768]{1,0:T(8,128)(2,1)} %bitcast.305, bf16[4,1248,768]{2,1,0:T(8,128)(2,1)} %get-tuple-element.148.hidden_ref, bf16[1248,768]{1,0:T(8,128)(2,1)} %bitcast.306), custom_call_target="tpu_custom_call" | custom-call | flops 60000002048 | bytes 1000 | tf_op jit(solution)/shard_map/narrow_grad/pallas_call | solution.py:1212
  231.5 11.2 %hidden_grad.1 = (bf16[8,240,768]{2,1,0:T(8,128)(2,1)}, bf16[8,240,768]{2,1,0:T(8,128)(2,1)}) custom-call(s32[1]{0:T(128)} %bitcast.42.core_ref, bf16[1248,768]{1,0:T(8,128)(2,1)} %bitcast.303, bf16[4,1248,768]{2,1,0:T(8,128)(2,1)} %get-tuple-element.165.grad_ref.grad_act_ref, bf16[16,768]{1,0:T(8,128)(2,1)} %pad.43.pooled_ref, bf16[16,768]{1,0:T(8,128)(2,1)} %pad.44.embeds_ref), custom_call_target="tpu_custom_call" | custom-call | flops 60000002048 | bytes 1000 | tf_op jit(solution)/shard_map/hidden_grad/pallas_call | solution.py:1237
  248.4 9.5 %attend_back.3 = (bf16[3,416,768]{2,1,0:T(8,128)(2,1)}, f32[8,768]{1,0:T(8,128)}) custom-call(s32[6]{0:T(128)} %reshape.380.counts_ref, bf16[2,1248,768]{2,1,0:T(8,128)(2,1)} %get-tuple-element.137.refs_0_.heads_ref, bf16[1,1248,768]{2,1,0:T(8,128)(2,1)} %widen_values.1.values_ref, f32[2,1248,768]{2,1,0:T(8,128)} %get-tuple-element.162.rstd_ref, ...), custom_call_target="tpu_custom_call" | custom-call | flops 60000002048 | bytes 1000 | tf_op jit(solution)/shard_map/attend_back/pallas_call | solution.py:1277
  260.8 9.2 %attend_back.4 = (bf16[3,416,768]{2,1,0:T(8,128)(2,1)}, f32[8,768]{1,0:T(8,128)}) custom-call(s32[6]{0:T(128)} %reshape.380.counts_ref, bf16[2,1248,768]{2,1,0:T(8,128)(2,1)} %get-tuple-element.137.refs_0_.heads_ref, bf16[1,1248,768]{2,1,0:T(8,128)(2,1)} %widen_values.1.values_ref, f32[2,1248,768]{2,1,0:T(8,128)} %get-tuple-element.162.rstd_ref, ...), custom_call_target="tpu_custom_call" | custom-call | flops 60000002048 | bytes 1000 | tf_op jit(solution)/shard_map/attend_back/pallas_call | solution.py:1277
  270.4 9.2 %attend_back.5 = (bf16[3,416,768]{2,1,0:T(8,128)(2,1)}, f32[8,768]{1,0:T(8,128)}) custom-call(s32[6]{0:T(128)} %reshape.380.counts_ref, bf16[2,1248,768]{2,1,0:T(8,128)(2,1)} %get-tuple-element.137.refs_0_.heads_ref, bf16[1,1248,768]{2,1,0:T(8,128)(2,1)} %widen_values.1.values_ref, f32[2,1248,768]{2,1,0:T(8,128)} %get-tuple-element.162.rstd_ref, ...), custom_call_target="tpu_custom_call" | custom-call | flops 60000002048 | bytes 1000 | tf_op jit(solution)/shard_map/attend_back/pallas_call | solution.py:1277
  284.7 9.8 %qkv_grad.1 = (bf16[2,8,144,384]{3,2,1,0:T(8,128)(2,1)}, bf16[2,8,144,384]{3,2,1,0:T(8,128)(2,1)}) custom-call(s32[1]{0:T(128)} %bitcast.42.core_ref, bf16[1248,768]{1,0:T(8,128)(2,1)} %bitcast.304, bf16[3,416,768]{2,1,0:T(8,128)(2,1)} %get-tuple-element.164.refs_0_.grad_qkv_ref, bf16[3,416,768]{2,1,0:T(8,128)(2,1)} %get-tuple-element.169.refs_0_.refs_1_.grad_qkv_ref, ...), custom_call_target="tpu_custom_call" | custom-call | flops 60000002048 | bytes 1000 | tf_op jit(solution)/shard_map/qkv_grad/pallas_call | solution.py:1299
  294.5 12.5 %hidden_back.1.grad_hidden_ref = f32[1248,768]{1,0:T(8,128)} custom-call(bf16[4,1248,768]{2,1,0:T(8,128)(2,1)} %get-tuple-element.165.grad_ref.grad_act_ref, bf16[5,768,768]{2,1,0:T(8,128)(2,1)} %get-tuple-element.155.wide_ref, bf16[2,8,144,384]{3,2,1,0:T(8,128)(2,1)} %get-tuple-element.172.refs_0_), custom_call_target="tpu_custom_call" | custom-call | flops 60000002048 | bytes 1000 | tf_op jit(solution)/shard_map/hidden_back/pallas_call | solution.py:1318
  307.6 3.1 fusion.18
  317.3 9.5 %merge_back.3 = (bf16[2,208,768]{2,1,0:T(8,128)(2,1)}, f32[208,768]{1,0:T(8,128)}, f32[8,768]{1,0:T(8,128)}) custom-call(s32[6]{0:T(128)} %reshape.380.counts_ref, bf16[3,416,768]{2,1,0:T(8,128)(2,1)} %get-tuple-element.164.refs_0_.grad_qkv_ref, f32[1248,768]{1,0:T(8,128)} %hidden_back.1.grad_hidden_ref, ...), custom_call_target="tpu_custom_call" | custom-call | flops 60000002048 | bytes 1000 | tf_op jit(solution)/shard_map/merge_back/pallas_call | solution.py:1337
  326.8 9.4 %merge_back.4 = (bf16[2,208,768]{2,1,0:T(8,128)(2,1)}, f32[208,768]{1,0:T(8,128)}, f32[8,768]{1,0:T(8,128)}) custom-call(s32[6]{0:T(128)} %reshape.380.counts_ref, bf16[3,416,768]{2,1,0:T(8,128)(2,1)} %get-tuple-element.169.refs_0_.refs_1_.grad_qkv_ref, f32[1248,768]{1,0:T(8,128)} %hidden_back.1.grad_hidden_ref, ...), custom_call_target="tpu_custom_call" | custom-call | flops 60000002048 | bytes 1000 | tf_op jit(solution)/shard_map/merge_back/pallas_call | solution.py:1337
  339.7 9.7 %merge_back.5 = (bf16[2,208,768]{2,1,0:T(8,128)(2,1)}, f32[208,768]{1,0:T(8,128)}, f32[8,768]{1,0:T(8,128)}) custom-call(s32[6]{0:T(128)} %reshape.380.counts_ref, bf16[3,416,768]{2,1,0:T(8,128)(2,1)} %get-tuple-element.170.refs_2_.refs_3_.grad_qkv_ref, f32[1248,768]{1,0:T(8,128)} %hidden_back.1.grad_hidden_ref, ...), custom_call_target="tpu_custom_call" | custom-call | flops 60000002048 | bytes 1000 | tf_op jit(solution)/shard_map/merge_back/pallas_call | solution.py:1337
  361.2 5.9 %embed_grad.1 = (bf16[8,48,1024]{2,1,0:T(8,128)(2,1)}, bf16[8,48,1024]{2,1,0:T(8,128)(2,1)}) custom-call(s32[1]{0:T(128)} %bitcast.42.core_ref, bf16[1248,768]{1,0:T(8,128)(2,1)} %bitcast.251, bf16[416,768]{1,0:T(8,128)(2,1)} %bitcast.308, bf16[416,768]{1,0:T(8,128)(2,1)} %bitcast.309, bf16[416,768]{1,0:T(8,128)(2,1)} %bitcast.310, ...), custom_call_target="tpu_custom_call" | custom-call | flops 60000002048 | bytes 1000 | tf_op jit(solution)/shard_map/embed_grad/pallas_call | solution.py:1382
  374.9 5.0 %collective-permute-done.61 = bf16[4,144,384]{2,1,0:T(8,128)(2,1)S(1)} collective-permute-done((bf16[4,144,384]{2,1,0:T(8,128)(2,1)}, bf16[4,144,384]{2,1,0:T(8,128)(2,1)S(1)}, u32[]{:S(2)}, u32[]{:S(2)}) %collective-permute-start.61) | collective-permute-done | bytes 442400 | tf_op jit(solution)/shard_map/ppermute | solution.py:514
  381.2 4.7 %collective-permute-done.53 = bf16[240,384]{1,0:T(8,128)(2,1)S(1)} collective-permute-done((bf16[240,384]{1,0:T(8,128)(2,1)}, bf16[240,384]{1,0:T(8,128)(2,1)S(1)}, u32[]{:S(2)}, u32[]{:S(2)}) %collective-permute-start.53) | collective-permute-done | bytes 184352 | tf_op jit(solution)/shard_map/ppermute | solution.py:514
  387.1 3.6 collective-permute-start.63
  398.7 3.3 collective-permute-done.64
  431.0 7.0 %update.1 = (f32[48,768]{1,0:T(8,128)}, f32[48,196]{1,0:T(8,128)}, f32[48,5376]{1,0:T(8,128)}, f32[240,768]{1,0:T(8,128)}, f32[48,768]{1,0:T(8,128)}, /*index=5*...) custom-call(f32[8,128]{1,0:T(8,128)} %copy-done.29, ...), custom_call_target="tpu_custom_call" | custom-call | tf_op jit(solution)/shard_map/update/pallas_call | solution.py:1443
  (374 shorter events, 171.3 us)
Async XLA Ops:
  17.6 14.3 %collective-permute-start.3 = (bf16[4,1,48,1024]{3,2,1,0:T(8,128)(2,1)}, bf16[4,1,48,1024]{3,2,1,0:T(8,128)(2,1)}, u32[]{:S(2)}, u32[]{:S(2)}) collective-permute-start(bf16[4,1,48,1024]{3,2,1,0:T(8,128)(2,1)} %pad_maximum_fusion.6.refs_0_), channel_id=1, source_target_pairs={{0,2},{1,3},{2,0},{3,1},{4,6},{5,7},{6,4},{7,5},{8,10},{9,11},{10,... | collective-permute-start | bytes 1179656 | tf_op jit(solution)/shard_map/ppermute | solution.py:583
  24.2 23.5 %collective-permute-start.4 = (bf16[4,1,48,1024]{3,2,1,0:T(8,128)(2,1)}, bf16[4,1,48,1024]{3,2,1,0:T(8,128)(2,1)}, u32[]{:S(2)}, u32[]{:S(2)}) collective-permute-start(bf16[4,1,48,1024]{3,2,1,0:T(8,128)(2,1)} %pad_maximum_fusion.6.refs_0_), channel_id=1, source_target_pairs={{0,1},{1,0},{2,3},{3,2},{4,5},{5,4},{6,7},{7,6},{8,9},{9,8},{10,11... | collective-permute-start | bytes 1179656 | tf_op jit(solution)/shard_map/ppermute | solution.py:579
  33.1 14.6 %collective-permute-start.5 = (bf16[4,1,48,1024]{3,2,1,0:T(8,128)(2,1)}, bf16[4,1,48,1024]{3,2,1,0:T(8,128)(2,1)}, u32[]{:S(2)}, u32[]{:S(2)}) collective-permute-start(bf16[4,1,48,1024]{3,2,1,0:T(8,128)(2,1)} %collective-permute-done.3.refs_1_), channel_id=1, source_target_pairs={{0,1},{1,0},{2,3},{3,2},{4,5},{5,4},{6,7},{7,6},{8,9},{9,8},{10,11... | collective-permute-start | bytes 1179656 | tf_op jit(solution)/shard_map/ppermute | solution.py:579
  40.9 20.8 %collective-permute-start.12 = (bf16[4,3,48,384]{3,2,1,0:T(8,128)(2,1)S(1)}, bf16[4,3,48,384]{3,2,1,0:T(8,128)(2,1)S(1)}, u32[]{:S(2)}, u32[]{:S(2)}) collective-permute-start(bf16[4,3,48,384]{3,2,1,0:T(8,128)(2,1)S(1)} %pad_maximum_fusion.5.refs_1_.refs_2_), channel_id=1, source_target_pairs={{0,16},{16,0},{1,17},{17,1},{2,18},{18,2},{3,19},{19,3},{4,20},{20... | collective-permute-start | bytes 1327112 | tf_op jit(solution)/shard_map/ppermute | solution.py:530
  46.1 15.6 %collective-permute-start.11 = (bf16[4,3,48,384]{3,2,1,0:T(8,128)(2,1)S(1)}, bf16[4,3,48,384]{3,2,1,0:T(8,128)(2,1)}, u32[]{:S(2)}, u32[]{:S(2)}) collective-permute-start(bf16[4,3,48,384]{3,2,1,0:T(8,128)(2,1)S(1)} %pad_maximum_fusion.4.refs_0_), channel_id=1, source_target_pairs={{0,2},{1,3},{2,0},{3,1},{4,6},{5,7},{6,4},{7,5},{8,10},{9,11},{10,... | collective-permute-start | bytes 1327112 | tf_op jit(solution)/shard_map/ppermute | solution.py:583
  51.5 22.7 %collective-permute-start.17 = (bf16[5,48,384]{2,1,0:T(8,128)(2,1)S(1)}, bf16[5,48,384]{2,1,0:T(8,128)(2,1)S(1)}, u32[]{:S(2)}, u32[]{:S(2)}) collective-permute-start(bf16[5,48,384]{2,1,0:T(8,128)(2,1)S(1)} %constant_dynamic-slice_fusion.2.refs_2_), channel_id=1, source_target_pairs={{0,4},{1,5},{2,6},{3,7},{4,0},{5,1},{6,2},{7,3},{8,12},{9,13},{10,... | collective-permute-start | bytes 552968 | tf_op jit(solution)/shard_map/ppermute | solution.py:589
  53.7 20.4 %collective-permute-start.18 = (bf16[5,48,384]{2,1,0:T(8,128)(2,1)S(1)}, bf16[5,48,384]{2,1,0:T(8,128)(2,1)S(1)}, u32[]{:S(2)}, u32[]{:S(2)}) collective-permute-start(bf16[5,48,384]{2,1,0:T(8,128)(2,1)S(1)} %constant_dynamic-slice_fusion.2.refs_2_), channel_id=1, source_target_pairs={{0,8},{1,9},{2,10},{3,11},{4,12},{5,13},{6,14},{7,15},{8,0},{9,1},... | collective-permute-start | bytes 552968 | tf_op jit(solution)/shard_map/ppermute | solution.py:589
  55.3 19.4 %collective-permute-start.19 = (bf16[5,48,384]{2,1,0:T(8,128)(2,1)S(1)}, bf16[5,48,384]{2,1,0:T(8,128)(2,1)S(1)}, u32[]{:S(2)}, u32[]{:S(2)}) collective-permute-start(bf16[5,48,384]{2,1,0:T(8,128)(2,1)S(1)} %constant_dynamic-slice_fusion.2.refs_2_), channel_id=1, source_target_pairs={{0,12},{1,13},{2,14},{3,15},{4,8},{5,9},{6,10},{7,11},{8,4},{9,5},... | collective-permute-start | bytes 552968 | tf_op jit(solution)/shard_map/ppermute | solution.py:589
  75.6 21.3 %collective-permute-start.22 = (bf16[1,240,384]{2,1,0:T(8,128)(2,1)S(1)}, bf16[1,240,384]{2,1,0:T(8,128)(2,1)S(1)}, u32[]{:S(2)}, u32[]{:S(2)}) collective-permute-start(bf16[1,240,384]{2,1,0:T(8,128)(2,1)S(1)} %constant_dynamic-slice_fusion.1.refs_10_), channel_id=1, source_target_pairs={{0,4},{1,5},{2,6},{3,7},{4,0},{5,1},{6,2},{7,3},{8,12},{9,13},{10,... | collective-permute-start | bytes 552968 | tf_op jit(solution)/shard_map/ppermute | solution.py:589
  76.2 20.7 %collective-permute-start.23 = (bf16[1,240,384]{2,1,0:T(8,128)(2,1)S(1)}, bf16[1,240,384]{2,1,0:T(8,128)(2,1)S(1)}, u32[]{:S(2)}, u32[]{:S(2)}) collective-permute-start(bf16[1,240,384]{2,1,0:T(8,128)(2,1)S(1)} %constant_dynamic-slice_fusion.1.refs_10_), channel_id=1, source_target_pairs={{0,8},{1,9},{2,10},{3,11},{4,12},{5,13},{6,14},{7,15},{8,0},{9,1},... | collective-permute-start | bytes 552968 | tf_op jit(solution)/shard_map/ppermute | solution.py:589
  78.6 18.2 %collective-permute-start.24 = (bf16[1,240,384]{2,1,0:T(8,128)(2,1)S(1)}, bf16[1,240,384]{2,1,0:T(8,128)(2,1)S(1)}, u32[]{:S(2)}, u32[]{:S(2)}) collective-permute-start(bf16[1,240,384]{2,1,0:T(8,128)(2,1)S(1)} %constant_dynamic-slice_fusion.1.refs_10_), channel_id=1, source_target_pairs={{0,12},{1,13},{2,14},{3,15},{4,8},{5,9},{6,10},{7,11},{8,4},{9,5},... | collective-permute-start | bytes 552968 | tf_op jit(solution)/shard_map/ppermute | solution.py:589
  80.0 20.6 %collective-permute-start.21 = (bf16[2,5,48,384]{3,2,1,0:T(8,128)(2,1)}, bf16[2,5,48,384]{3,2,1,0:T(8,128)(2,1)S(1)}, u32[]{:S(2)}, u32[]{:S(2)}) collective-permute-start(bf16[2,5,48,384]{3,2,1,0:T(8,128)(2,1)} %pad_maximum_fusion.8.refs_9_), channel_id=1, source_target_pairs={{0,2},{1,3},{2,0},{3,1},{4,6},{5,7},{6,4},{7,5},{8,10},{9,11},{10,... | collective-permute-start | bytes 1105928 | tf_op jit(solution)/shard_map/ppermute | solution.py:583
  80.5 20.1 %collective-permute-start.20 = (bf16[2,5,48,384]{3,2,1,0:T(8,128)(2,1)S(1)}, bf16[2,5,48,384]{3,2,1,0:T(8,128)(2,1)S(1)}, u32[]{:S(2)}, u32[]{:S(2)}) collective-permute-start(bf16[2,5,48,384]{3,2,1,0:T(8,128)(2,1)S(1)} %pad_maximum_fusion.7.refs_8_), channel_id=1, source_target_pairs={{0,16},{16,0},{1,17},{17,1},{2,18},{18,2},{3,19},{19,3},{4,20},{20... | collective-permute-start | bytes 1105928 | tf_op jit(solution)/shard_map/ppermute | solution.py:530
  97.7 21.6 %collective-permute-start.28 = (bf16[2,1,240,384]{3,2,1,0:T(8,128)(2,1)}, bf16[2,1,240,384]{3,2,1,0:T(8,128)(2,1)}, u32[]{:S(2)}, u32[]{:S(2)}) collective-permute-start(bf16[2,1,240,384]{3,2,1,0:T(8,128)(2,1)} %pad_maximum_fusion.10.refs_1_), channel_id=1, source_target_pairs={{0,2},{1,3},{2,0},{3,1},{4,6},{5,7},{6,4},{7,5},{8,10},{9,11},{10,... | collective-permute-start | bytes 1105928 | tf_op jit(solution)/shard_map/ppermute | solution.py:583
  100.0 20.5 %collective-permute-start.27 = (bf16[2,1,240,384]{3,2,1,0:T(8,128)(2,1)}, bf16[2,1,240,384]{3,2,1,0:T(8,128)(2,1)S(1)}, u32[]{:S(2)}, u32[]{:S(2)}) collective-permute-start(bf16[2,1,240,384]{3,2,1,0:T(8,128)(2,1)} %pad_maximum_fusion.9.refs_0_), channel_id=1, source_target_pairs={{0,16},{16,0},{1,17},{17,1},{2,18},{18,2},{3,19},{19,3},{4,20},{20... | collective-permute-start | bytes 1105928 | tf_op jit(solution)/shard_map/ppermute | solution.py:530
  102.6 22.4 %collective-permute-start.26 = (bf16[4,5,48,384]{3,2,1,0:T(8,128)(2,1)}, bf16[4,5,48,384]{3,2,1,0:T(8,128)(2,1)}, u32[]{:S(2)}, u32[]{:S(2)}) collective-permute-start(bf16[4,5,48,384]{3,2,1,0:T(8,128)(2,1)} %pad_maximum_fusion.1.refs_2_), channel_id=1, source_target_pairs={{0,16},{16,0},{1,17},{17,1},{2,18},{18,2},{3,19},{19,3},{4,20},{20... | collective-permute-start | bytes 2211848 | tf_op jit(solution)/shard_map/ppermute | solution.py:530
  103.9 21.1 %collective-permute-start.25 = (bf16[4,5,48,384]{3,2,1,0:T(8,128)(2,1)}, bf16[4,5,48,384]{3,2,1,0:T(8,128)(2,1)}, u32[]{:S(2)}, u32[]{:S(2)}) collective-permute-start(bf16[4,5,48,384]{3,2,1,0:T(8,128)(2,1)} %pad_maximum_fusion.refs_1_.refs_0_), channel_id=1, source_target_pairs={{0,2},{1,3},{2,0},{3,1},{4,6},{5,7},{6,4},{7,5},{8,10},{9,11},{10,... | collective-permute-start | bytes 2211848 | tf_op jit(solution)/shard_map/ppermute | solution.py:583
  126.7 21.4 %collective-permute-start.34 = (bf16[4,1,240,384]{3,2,1,0:T(8,128)(2,1)S(1)}, bf16[4,1,240,384]{3,2,1,0:T(8,128)(2,1)S(1)}, u32[]{:S(2)}, u32[]{:S(2)}) collective-permute-start(bf16[4,1,240,384]{3,2,1,0:T(8,128)(2,1)S(1)} %pad_maximum_fusion.3.refs_9_.refs_2_), channel_id=1, source_target_pairs={{0,16},{16,0},{1,17},{17,1},{2,18},{18,2},{3,19},{19,3},{4,20},{20... | collective-permute-start | bytes 2211848 | tf_op jit(solution)/shard_map/ppermute | solution.py:530
  127.7 20.4 %collective-permute-start.33 = (bf16[4,1,240,384]{3,2,1,0:T(8,128)(2,1)S(1)}, bf16[4,1,240,384]{3,2,1,0:T(8,128)(2,1)S(1)}, u32[]{:S(2)}, u32[]{:S(2)}) collective-permute-start(bf16[4,1,240,384]{3,2,1,0:T(8,128)(2,1)S(1)} %pad_maximum_fusion.2.refs_8_.refs_0_), channel_id=1, source_target_pairs={{0,2},{1,3},{2,0},{3,1},{4,6},{5,7},{6,4},{7,5},{8,10},{9,11},{10,... | collective-permute-start | bytes 2211848 | tf_op jit(solution)/shard_map/ppermute | solution.py:583
  242.7 15.2 %collective-permute-start.47 = (bf16[8,240,768]{2,1,0:T(8,128)(2,1)}, bf16[8,240,768]{2,1,0:T(8,128)(2,1)}, u32[]{:S(2)}, u32[]{:S(2)}) collective-permute-start(bf16[8,240,768]{2,1,0:T(8,128)(2,1)} %get-tuple-element.167), channel_id=1, source_target_pairs={{0,1},{1,0},{2,3},{3,2},{4,5},{5,4},{6,7},{7,6},{8,9},{9,8},{10,11... | collective-permute-start | bytes 8847368 | tf_op jit(solution)/shard_map/ppermute | solution.py:579
  247.4 34.6 %collective-permute-start.46 = (bf16[4,2,240,384]{3,2,1,0:T(8,128)(2,1)}, bf16[4,2,240,384]{3,2,1,0:T(8,128)(2,1)}, u32[]{:S(2)}, u32[]{:S(2)}) collective-permute-start(bf16[4,2,240,384]{3,2,1,0:T(8,128)(2,1)} %fusion.refs_0_), channel_id=1, source_target_pairs={{0,16},{16,0},{1,17},{17,1},{2,18},{18,2},{3,19},{19,3},{4,20},{20... | collective-permute-start | bytes 4423688 | tf_op jit(solution)/shard_map/ppermute | solution.py:514
  270.0 37.6 %collective-permute-start.49 = (bf16[4,240,768]{2,1,0:T(8,128)(2,1)}, bf16[4,240,768]{2,1,0:T(8,128)(2,1)}, u32[]{:S(2)}, u32[]{:S(2)}) collective-permute-start(bf16[4,240,768]{2,1,0:T(8,128)(2,1)} %fusion.1.refs_1_), channel_id=1, source_target_pairs={{0,2},{1,3},{2,0},{3,1},{4,6},{5,7},{6,4},{7,5},{8,10},{9,11},{10,... | collective-permute-start | bytes 4423688 | tf_op jit(solution)/shard_map/ppermute | solution.py:514
  294.5 20.6 %collective-permute-start.50 = (bf16[2,8,144,384]{3,2,1,0:T(8,128)(2,1)}, bf16[2,8,144,384]{3,2,1,0:T(8,128)(2,1)S(1)}, u32[]{:S(2)}, u32[]{:S(2)}) collective-permute-start(bf16[2,8,144,384]{3,2,1,0:T(8,128)(2,1)} %get-tuple-element.172.refs_0_), channel_id=1, source_target_pairs={{0,1},{1,0},{2,3},{3,2},{4,5},{5,4},{6,7},{7,6},{8,9},{9,8},{10,11... | collective-permute-start | bytes 5308424 | tf_op jit(solution)/shard_map/ppermute | solution.py:579
  307.0 48.2 %collective-permute-start.48 = (bf16[4,240,384]{2,1,0:T(8,128)(2,1)}, bf16[4,240,384]{2,1,0:T(8,128)(2,1)}, u32[]{:S(2)}, u32[]{:S(2)}) collective-permute-start(bf16[4,240,384]{2,1,0:T(8,128)(2,1)} %fusion.2.refs_4_), channel_id=1, source_target_pairs={{0,2},{1,3},{2,0},{3,1},{4,6},{5,7},{6,4},{7,5},{8,10},{9,11},{10,... | collective-permute-start | bytes 2211848 | tf_op jit(solution)/shard_map/ppermute | solution.py:514
  310.8 38.6 %collective-permute-start.55 = (bf16[240,768]{1,0:T(8,128)(2,1)}, bf16[240,768]{1,0:T(8,128)(2,1)}, u32[]{:S(2)}, u32[]{:S(2)}) collective-permute-start(bf16[240,768]{1,0:T(8,128)(2,1)} %get-tuple-element.253.refs_0_), channel_id=1, source_target_pairs={{0,4},{1,5},{2,6},{3,7},{4,0},{5,1},{6,2},{7,3},{8,12},{9,13},{10,... | collective-permute-start | bytes 1105928 | tf_op jit(solution)/shard_map/ppermute | solution.py:514
  310.8 38.6 %collective-permute-start.56 = (bf16[240,768]{1,0:T(8,128)(2,1)}, bf16[240,768]{1,0:T(8,128)(2,1)}, u32[]{:S(2)}, u32[]{:S(2)}) collective-permute-start(bf16[240,768]{1,0:T(8,128)(2,1)} %get-tuple-element.252.refs_1_), channel_id=1, source_target_pairs={{0,8},{1,9},{2,10},{3,11},{4,12},{5,13},{6,14},{7,15},{8,0},{9,1},... | collective-permute-start | bytes 1105928 | tf_op jit(solution)/shard_map/ppermute | solution.py:514
  312.7 36.7 %collective-permute-start.57 = (bf16[240,768]{1,0:T(8,128)(2,1)}, bf16[240,768]{1,0:T(8,128)(2,1)}, u32[]{:S(2)}, u32[]{:S(2)}) collective-permute-start(bf16[240,768]{1,0:T(8,128)(2,1)} %get-tuple-element.251.refs_2_), channel_id=1, source_target_pairs={{0,12},{1,13},{2,14},{3,15},{4,8},{5,9},{6,10},{7,11},{8,4},{9,5},... | collective-permute-start | bytes 1105928 | tf_op jit(solution)/shard_map/ppermute | solution.py:514
  316.3 21.4 %collective-permute-start.51 = (bf16[4,2,144,384]{3,2,1,0:T(8,128)(2,1)}, bf16[4,2,144,384]{3,2,1,0:T(8,128)(2,1)}, u32[]{:S(2)}, u32[]{:S(2)}) collective-permute-start(bf16[4,2,144,384]{3,2,1,0:T(8,128)(2,1)} %fusion.12.refs_3_), channel_id=1, source_target_pairs={{0,16},{16,0},{1,17},{17,1},{2,18},{18,2},{3,19},{19,3},{4,20},{20... | collective-permute-start | bytes 2654216 | tf_op jit(solution)/shard_map/ppermute | solution.py:514
  368.4 24.7 %collective-permute-start.62 = (bf16[240,768]{1,0:T(8,128)(2,1)S(1)}, bf16[240,768]{1,0:T(8,128)(2,1)S(1)}, u32[]{:S(2)}, u32[]{:S(2)}) collective-permute-start(bf16[240,768]{1,0:T(8,128)(2,1)S(1)} %copy-done.7), channel_id=1, source_target_pairs={{0,16},{16,0},{1,17},{17,1},{2,18},{18,2},{3,19},{19,3},{4,20},{20... | collective-permute-start | bytes 1105928 | tf_op jit(solution)/shard_map/ppermute | solution.py:530
  369.4 16.5 %collective-permute-start.53 = (bf16[240,384]{1,0:T(8,128)(2,1)}, bf16[240,384]{1,0:T(8,128)(2,1)S(1)}, u32[]{:S(2)}, u32[]{:S(2)}) collective-permute-start(bf16[240,384]{1,0:T(8,128)(2,1)} %get-tuple-element.249.refs_10_), channel_id=1, source_target_pairs={{0,8},{1,9},{2,10},{3,11},{4,12},{5,13},{6,14},{7,15},{8,0},{9,1},... | collective-permute-start | bytes 552968 | tf_op jit(solution)/shard_map/ppermute | solution.py:514
  371.3 14.6 %collective-permute-start.54 = (bf16[240,384]{1,0:T(8,128)(2,1)S(1)}, bf16[240,384]{1,0:T(8,128)(2,1)S(1)}, u32[]{:S(2)}, u32[]{:S(2)}) collective-permute-start(bf16[240,384]{1,0:T(8,128)(2,1)S(1)} %copy-done.22), channel_id=1, source_target_pairs={{0,12},{1,13},{2,14},{3,15},{4,8},{5,9},{6,10},{7,11},{8,4},{9,5},... | collective-permute-start | bytes 552968 | tf_op jit(solution)/shard_map/ppermute | solution.py:514
  379.9 16.5 %collective-permute-start.60 = (bf16[4,48,1024]{2,1,0:T(8,128)(2,1)S(1)}, bf16[4,48,1024]{2,1,0:T(8,128)(2,1)S(1)}, u32[]{:S(2)}, u32[]{:S(2)}) collective-permute-start(bf16[4,48,1024]{2,1,0:T(8,128)(2,1)S(1)} %fusion.21), channel_id=1, source_target_pairs={{0,2},{1,3},{2,0},{3,1},{4,6},{5,7},{6,4},{7,5},{8,10},{9,11},{10,... | collective-permute-start | bytes 1179656 | tf_op jit(solution)/shard_map/ppermute | solution.py:514
  (93 other events, 975.3 us)
